TPU v7x, 512 devices: a whole 4x4x16 slice. The times are simulated.
512 devices in a mesh: tile: 128 (over x, z, core), chan: 4 (over y).
Axes of the slice: x: 4, y: 4, z: 16, core: 2. Of those that a mesh axis runs over, the one named last changes fastest.
Arguments:
- atm_state: bfloat16 [256, 131072], P('chan', 'tile'), may hold values from -6 to 6
- ocean_state: bfloat16 [128, 131072], P('chan', 'tile'), may hold values from -6 to 6
- conv_weight: bfloat16 [9, 384, 256], replicated, may hold values from -0.109375 to 0.109375
- conv_bias: float32 [256], P('chan'), may hold values from -3 to 3
- regrid_weight: bfloat16 [1536, 128, 128], P('tile'), may hold values from 0 to 0.25
- out_grad: bfloat16 [256, 131072], P('chan', 'tile'), may hold values from -6 to 6
- atm_neighbours: int32 [128, 8], P('tile'), may hold values from -1 to 127, as said below
- coupling_sources: int32 [128, 4], P('tile'), may hold values from 0 to 127, as said below
- coupling_blocks: int32 [128, 12], P('tile'), may hold values from -1 to 7, as said below
- coupling_sends: int32 [128, 128, 3], P('tile'), may hold values from -1 to 7, as said below
Outputs:
- atm_output: bfloat16 [256, 131072], P('chan', 'tile')
- atm_input_grad: bfloat16 [256, 131072], P('chan', 'tile')
- ocean_grad: float32 [128, 131072], P('chan', 'tile')
- weight_grad: float32 [9, 384, 256], P(None, None, 'chan')
- bias_grad: float32 [256], P('chan')
Inputs may be any that keep to these rules, and one draw needn't show every extreme that they name: `atm_neighbours`: devices 8 * r to 8 * r + 7 hold the patches of row r of a grid of patches with 8 columns, in an order drawn from the seed; an entry names the device of the adjacent patch in that direction, -1 beyond the grid's edge; if device d names p in a direction, p names d in the opposite one. `coupling_sources`: the 4 sources of device p are different and differ from p + 128 / 2 by at most 3 modulo 128; the first source is p + 128 / 2 modulo 128. `coupling_blocks`: -1 marks an entry over land; the entries of the first source are never -1; in every draw some device has all 12 entries live. coupling_sends[q, p, c] is not -1 exactly where some entry k * 3 + c of device p has source q and is live.
All inputs are finite; a program needn't handle non-finite values.
Results may differ from a plain program's by a relative error of at most 0.008.
Values may be sent and summed in bfloat16 or wider, within the bound.
No kernel may reach another device: no remote copies, remote signals or barrier semaphores. Data moves between devices by JAX's collectives and lax.ppermute only.
A program may use at most 64 MiB of HBM per device.

v0:
```python
import math

import jax
import jax.numpy as jnp
from jax import lax
from jax.sharding import PartitionSpec as P

SC = 128
PATCH_COLS = 8
SPAN = 3


SIDE_OF = (0, 1, 2, 3, 0, 0, 1, 1)
OFFSETS = ((-1, -1), (-1, 0), (-1, 1), (0, -1), (0, 0), (0, 1), (1, -1), (1, 0), (1, 1))
PRECISE = lax.Precision.HIGHEST


def shifted(array, axis, by):
    size = lax.axis_size(axis)
    pairs = [(i, i + by) for i in range(size) if 0 <= i + by < size]
    return lax.ppermute(array, axis, pairs)


def from_behind(array, axis, by):
    size = lax.axis_size(axis)
    return lax.ppermute(array, axis, [(i, (i + by) % size) for i in range(size)])


def make_strips(surface):
    height = surface.shape[1]
    columns = surface.shape[2]
    west_col = jnp.pad(surface[:, :, 0], ((0, 0), (0, columns - height)))
    east_col = jnp.pad(surface[:, :, columns - 1], ((0, 0), (0, columns - height)))
    side_rows = (surface[:, 0, :], surface[:, height - 1, :], west_col, east_col)
    return jnp.stack([side_rows[side] for side in SIDE_OF], axis=0)


def pad_patch(surface, arrived):
    height = surface.shape[1]
    columns = surface.shape[2]
    north_row = jnp.concatenate(
        [arrived[4][:, columns - 1 :], arrived[0], arrived[5][:, :1]], axis=1
    )
    south_row = jnp.concatenate(
        [arrived[6][:, columns - 1 :], arrived[1], arrived[7][:, :1]], axis=1
    )
    central = jnp.concatenate(
        [arrived[2][:, :height, None], surface, arrived[3][:, :height, None]], axis=2
    )
    return jnp.concatenate([north_row[:, None], central, south_row[:, None]], axis=1)


def neighbour_halo(surfaces, neighbours, tile_count):
    stacked = jnp.concatenate(surfaces, axis=0)
    strips_out = make_strips(stacked)
    own_index = lax.axis_index("tile")
    max_offset = min(2 * PATCH_COLS - 1, tile_count - 1)
    arrived = jnp.zeros_like(strips_out)
    for offset in range(-max_offset, max_offset + 1):
        if offset != 0:
            outward = (neighbours == own_index + offset).astype(jnp.bfloat16)
            parcel = jnp.einsum(
                "d,dcs->cs", outward, strips_out, preferred_element_type=jnp.float32
            ).astype(jnp.bfloat16)
            landed = shifted(parcel, "tile", offset)
            inward = neighbours == own_index - offset
            arrived = jnp.where(inward[:, None, None], landed[None], arrived)
    padded = pad_patch(stacked, arrived)
    results = []
    first_index = 0
    for surface in surfaces:
        results.append(padded[first_index : first_index + surface.shape[0]])
        first_index = first_index + surface.shape[0]
    return results


def fetch_ocean(ocean_blocks, send_list, sources, tile_count):
    block_count = ocean_blocks.shape[1]
    block_ids = jnp.arange(block_count, dtype=jnp.int32)
    own_index = lax.axis_index("tile")
    gathered = jnp.zeros(
        (sources.shape[0], send_list.shape[1], ocean_blocks.shape[0], ocean_blocks.shape[2]),
        jnp.bfloat16,
    )
    for offset in range(-SPAN, SPAN + 1):
        distance = tile_count // 2 + offset
        target = (own_index - distance) % tile_count
        list_row = lax.dynamic_index_in_dim(send_list, target, 0, keepdims=False)
        selector = (list_row[:, None] == block_ids[None, :]).astype(jnp.bfloat16)
        parcel = jnp.einsum(
            "cb,kbs->cks", selector, ocean_blocks, preferred_element_type=jnp.float32
        ).astype(jnp.bfloat16)
        landed = from_behind(parcel, "tile", -distance)
        matches = sources == (own_index + distance) % tile_count
        gathered = jnp.where(matches[:, None, None, None], landed[None], gathered)
    return gathered


def return_ocean(return_terms, send_list, sources, block_count, tile_count):
    block_ids = jnp.arange(block_count, dtype=jnp.int32)
    own_index = lax.axis_index("tile")
    accumulated = jnp.zeros(
        (return_terms.shape[2], block_count, return_terms.shape[3]), jnp.float32
    )
    for offset in range(-SPAN, SPAN + 1):
        distance = tile_count // 2 + offset
        matches = (sources == (own_index + distance) % tile_count).astype(jnp.bfloat16)
        parcel = jnp.einsum(
            "k,kcis->cis", matches, return_terms, preferred_element_type=jnp.float32
        ).astype(jnp.bfloat16)
        landed = from_behind(parcel, "tile", distance)
        list_row = lax.dynamic_index_in_dim(
            send_list, (own_index - distance) % tile_count, 0, keepdims=False
        )
        selector = (list_row[:, None] == block_ids[None, :]).astype(jnp.bfloat16)
        accumulated = accumulated + jnp.einsum(
            "cb,cks->kbs", selector, landed, preferred_element_type=jnp.float32
        )
    return accumulated


def to_flat(padded, flat_len):
    channels = padded.shape[0]
    spread_len = padded.shape[1] * padded.shape[2]
    joined = padded.reshape(channels, spread_len)
    return jnp.pad(joined, ((0, 0), (1, flat_len - 1 - spread_len)))


def window(flat_rows, offset, stride, out_len, flipped):
    shift_row, shift_col = OFFSETS[offset]
    if flipped:
        shift_row, shift_col = (-shift_row, -shift_col)
    first_index = 1 + (1 + shift_row) * stride + shift_col
    return flat_rows[:, first_index : first_index + out_len]


def unflat(total_sum, height, columns):
    trimmed = total_sum[:, : height * (columns + 2)].reshape(
        total_sum.shape[0], height, columns + 2
    )
    return trimmed[:, :, 1 : columns + 1]


def contract_lead(weights, operand):
    return lax.dot_general(
        weights, operand, (((0,), (0,)), ((), ())), preferred_element_type=jnp.float32
    )


def contract_last(left_op, right_op):
    return lax.dot_general(
        left_op, right_op, (((1,), (1,)), ((), ())), preferred_element_type=jnp.float32
    )


def on_device(
    atm_state,
    ocean_state,
    conv_weight,
    conv_bias,
    regrid_weight,
    out_grad,
    atm_neighbours,
    coupling_sources,
    coupling_blocks,
    coupling_sends,
):
    atm_chans = atm_state.shape[0]
    cell_count = atm_state.shape[1]
    patch_rows = cell_count // SC
    ocean_chans = ocean_state.shape[0]
    ocean_count = ocean_state.shape[1] // 128
    chan_index = lax.axis_index("chan")
    tile_count = lax.axis_size("tile")
    atm_width = conv_weight.shape[2]
    stride = SC + 2
    out_len = -(-(patch_rows * stride) // 128) * 128
    flat_len = -(-(2 * stride + 2 + out_len) // 128) * 128
    neighbours = atm_neighbours[0]
    sources = coupling_sources[0]
    entry_blocks = coupling_blocks[0]
    send_list = coupling_sends[0]
    ocean_blocks = ocean_state.reshape(ocean_chans, ocean_count, 128)
    fetched = fetch_ocean(ocean_blocks, send_list, sources, tile_count)
    entries = fetched.reshape(-1, ocean_chans, 128)
    block_terms = jnp.einsum(
        "eks,est->ekt", entries, regrid_weight, preferred_element_type=jnp.float32
    )
    placement = entry_blocks[:, None] == jnp.arange(cell_count // 128, dtype=jnp.int32)[None, :]
    regridded = jnp.einsum(
        "ea,ekt->kat", placement.astype(jnp.float32), block_terms, precision=PRECISE
    )
    regridded = regridded.astype(jnp.bfloat16)
    atm_patch = atm_state.reshape(atm_chans, patch_rows, SC)
    padded_atm, padded_ocean = neighbour_halo((atm_patch, regridded), neighbours, tile_count)
    every_atm, every_ocean = (
        lax.all_gather(to_flat(padded_atm, flat_len), "chan", axis=0, tiled=True),
        lax.all_gather(to_flat(padded_ocean, flat_len), "chan", axis=0, tiled=True),
    )
    own_weight = lax.dynamic_slice_in_dim(conv_weight, chan_index * atm_chans, atm_chans, 2)
    total_sum = jnp.zeros((atm_chans, out_len), jnp.float32)
    for offset in range(9):
        total_sum = total_sum + contract_lead(
            own_weight[offset, :atm_width], window(every_atm, offset, stride, out_len, False)
        )
        total_sum = total_sum + contract_lead(
            own_weight[offset, atm_width:], window(every_ocean, offset, stride, out_len, False)
        )
    pre_act = unflat(total_sum, patch_rows, SC) + conv_bias[:, None, None]
    sigmoid_z = jax.nn.sigmoid(pre_act)
    atm_output = (atm_patch.astype(jnp.float32) + pre_act * sigmoid_z).astype(jnp.bfloat16)
    grad_patch = out_grad.reshape(atm_chans, patch_rows, SC)
    z_grad = (
        grad_patch.astype(jnp.float32) * sigmoid_z * (1.0 + pre_act * (1.0 - sigmoid_z))
    ).astype(jnp.bfloat16)
    padded_grad = neighbour_halo((z_grad,), neighbours, tile_count)[0]
    flat_grad = to_flat(padded_grad, flat_len)
    every_grad = lax.all_gather(flat_grad, "chan", axis=0, tiled=True)
    rows_atm = lax.dynamic_slice_in_dim(conv_weight, chan_index * atm_chans, atm_chans, 1)
    rows_ocean = lax.dynamic_slice_in_dim(
        conv_weight, atm_width + chan_index * ocean_chans, ocean_chans, 1
    )
    sum_atm = jnp.zeros((atm_chans, out_len), jnp.float32)
    sum_ocean = jnp.zeros((ocean_chans, out_len), jnp.float32)
    for offset in range(9):
        grad_window = window(every_grad, offset, stride, out_len, True)
        sum_atm = sum_atm + jnp.dot(
            rows_atm[offset], grad_window, preferred_element_type=jnp.float32
        )
        sum_ocean = sum_ocean + jnp.dot(
            rows_ocean[offset], grad_window, preferred_element_type=jnp.float32
        )
    atm_back = unflat(sum_atm, patch_rows, SC).reshape(atm_chans, cell_count)
    ocean_back = unflat(sum_ocean, patch_rows, SC).reshape(ocean_chans, cell_count)
    atm_input_grad = (out_grad.astype(jnp.float32) + atm_back).astype(jnp.bfloat16)
    ocean_delta = ocean_back.astype(jnp.bfloat16).reshape(ocean_chans, cell_count // 128, 128)
    chosen = jnp.einsum(
        "ea,kas->eks",
        placement.astype(jnp.bfloat16),
        ocean_delta,
        preferred_element_type=jnp.float32,
    ).astype(jnp.bfloat16)
    return_terms = jnp.einsum(
        "ekt,est->eks", chosen, regrid_weight, preferred_element_type=jnp.float32
    ).astype(jnp.bfloat16)
    return_terms = return_terms.reshape(sources.shape[0], -1, ocean_chans, 128)
    ocean_grad = return_ocean(return_terms, send_list, sources, ocean_count, tile_count).reshape(
        ocean_chans, ocean_count * 128
    )
    grad_out = jnp.pad(z_grad, ((0, 0), (0, 0), (1, 1))).reshape(atm_chans, patch_rows * stride)
    grad_out = jnp.pad(grad_out, ((0, 0), (0, out_len - patch_rows * stride)))
    offset_parts = []
    for offset in range(9):
        offset_parts.append(
            jnp.concatenate(
                [
                    contract_last(window(every_atm, offset, stride, out_len, False), grad_out),
                    contract_last(window(every_ocean, offset, stride, out_len, False), grad_out),
                ],
                axis=0,
            )
        )
    weight_part = jnp.stack(offset_parts, axis=0)
    bias_part = jnp.sum(z_grad.astype(jnp.float32), axis=(1, 2))
    weight_sum, bias_sum = lax.psum((weight_part, bias_part), "tile")
    grad_scale = 1.0 / math.sqrt(cell_count * tile_count)
    return (
        atm_output.reshape(atm_chans, cell_count),
        atm_input_grad,
        ocean_grad,
        weight_sum * grad_scale,
        bias_sum * grad_scale,
    )


def solution(mesh):
    placed = (
        P("chan", "tile"),
        P("chan", "tile"),
        P(),
        P("chan"),
        P("tile", None, None),
        P("chan", "tile"),
        P("tile", None),
        P("tile", None),
        P("tile", None),
        P("tile", None, None),
    )
    return jax.shard_map(
        on_device,
        mesh=mesh,
        in_specs=placed,
        out_specs=(
            P("chan", "tile"),
            P("chan", "tile"),
            P("chan", "tile"),
            P(None, None, "chan"),
            P("chan"),
        ),
        check_vma=False,
    )
```

profile of v0, /device:TPU:1, one launch (start us, length us, event | category | flops | bytes accessed | tf_op | source)
XLA Modules:
  0.0 800.5 jit_solution(7908078152723695715)
XLA Ops:
  10.2 13.4 %collective-permute-start = (bf16[3,32,128]{2,0,1:T(4,128)(2,1)S(1)}, bf16[3,32,128]{2,0,1:T(4,128)(2,1)S(1)}, u32[]{:S(2)}, u32[]{:S(2)}) collective-permute-start(bf16[3,32,128]{2,0,1:T(4,128)(2,1)S(1)} %convolution_convert_fusion.9), channel_id=1, source_target_pairs={{0,244},{4,248},{8,252},{12,256},{16,260},{20,264},{24,268},{28,27... | collective-permute-start | bytes 73736 | tf_op jit(solution)/shard_map/ppermute | solution.py:26
  23.8 4.2 collective-permute-start.1
  35.9 4.7 collective-permute-start.4
  44.1 10.7 %collective-permute-start.5 = (bf16[3,32,128]{2,0,1:T(4,128)(2,1)S(1)}, bf16[3,32,128]{2,0,1:T(4,128)(2,1)S(1)}, u32[]{:S(2)}, u32[]{:S(2)}) collective-permute-start(bf16[3,32,128]{2,0,1:T(4,128)(2,1)S(1)} %convolution_convert_fusion.4), channel_id=1, source_target_pairs={{0,264},{4,268},{8,272},{12,276},{16,280},{20,284},{24,288},{28,29... | collective-permute-start | bytes 73736 | tf_op jit(solution)/shard_map/ppermute | solution.py:26
  54.9 19.0 %collective-permute-start.6 = (bf16[3,32,128]{2,0,1:T(4,128)(2,1)S(1)}, bf16[3,32,128]{2,0,1:T(4,128)(2,1)S(1)}, u32[]{:S(2)}, u32[]{:S(2)}) collective-permute-start(bf16[3,32,128]{2,0,1:T(4,128)(2,1)S(1)} %convolution_convert_fusion.3), channel_id=1, source_target_pairs={{0,268},{4,272},{8,276},{12,280},{16,284},{20,288},{24,292},{28,29... | collective-permute-start | bytes 73736 | tf_op jit(solution)/shard_map/ppermute | solution.py:26
  76.9 6.6 collective-permute-done.6
  86.5 5.1 collective-permute-start.10
  91.6 10.0 %collective-permute-start.11 = (bf16[96,128]{0,1:T(8,128)(2,1)S(1)}, bf16[96,128]{0,1:T(8,128)(2,1)S(1)}, u32[]{:S(2)}, u32[]{:S(2)}) collective-permute-start(bf16[96,128]{0,1:T(8,128)(2,1)S(1)} %get-tuple-element.54), channel_id=1, source_target_pairs={{0,44},{4,48},{8,52},{12,56},{16,60},{20,64},{24,68},{28,72},{32,7... | collective-permute-start | bytes 73736 | tf_op jit(solution)/shard_map/ppermute | solution.py:21
  107.3 8.1 %collective-permute-start.14 = (bf16[96,128]{0,1:T(8,128)(2,1)S(1)}, bf16[96,128]{0,1:T(8,128)(2,1)S(1)}, u32[]{:S(2)}, u32[]{:S(2)}) collective-permute-start(bf16[96,128]{0,1:T(8,128)(2,1)S(1)} %get-tuple-element.57), channel_id=1, source_target_pairs={{0,32},{4,36},{8,40},{12,44},{16,48},{20,52},{24,56},{28,60},{32,6... | collective-permute-start | bytes 73736 | tf_op jit(solution)/shard_map/ppermute | solution.py:21
  115.4 5.3 collective-permute-start.15
  128.5 4.4 collective-permute-start.19
  144.4 13.0 %collective-permute-start.7 = (bf16[96,128]{0,1:T(8,128)(2,1)S(1)}, bf16[96,128]{0,1:T(8,128)(2,1)S(1)}, u32[]{:S(2)}, u32[]{:S(2)}) collective-permute-start(bf16[96,128]{0,1:T(8,128)(2,1)S(1)} %get-tuple-element.50), channel_id=1, source_target_pairs={{0,60},{4,64},{8,68},{12,72},{16,76},{20,80},{24,84},{28,88},{32,9... | collective-permute-start | bytes 73736 | tf_op jit(solution)/shard_map/ppermute | solution.py:21
  160.0 11.5 %collective-permute-start.9 = (bf16[96,128]{0,1:T(8,128)(2,1)S(1)}, bf16[96,128]{0,1:T(8,128)(2,1)S(1)}, u32[]{:S(2)}, u32[]{:S(2)}) collective-permute-start(bf16[96,128]{0,1:T(8,128)(2,1)S(1)} %get-tuple-element.52), channel_id=1, source_target_pairs={{0,52},{4,56},{8,60},{12,64},{16,68},{20,72},{24,76},{28,80},{32,8... | collective-permute-start | bytes 73736 | tf_op jit(solution)/shard_map/ppermute | solution.py:21
  203.9 8.3 %collective-permute-done.34 = bf16[96,128]{0,1:T(8,128)(2,1)S(1)} collective-permute-done((bf16[96,128]{0,1:T(8,128)(2,1)S(1)}, bf16[96,128]{0,1:T(8,128)(2,1)S(1)}, u32[]{:S(2)}, u32[]{:S(2)}) %collective-permute-start.34) | collective-permute-done | bytes 24608 | tf_op jit(solution)/shard_map/ppermute | solution.py:21
  212.2 12.5 %collective-permute-done.35 = bf16[96,128]{0,1:T(8,128)(2,1)S(1)} collective-permute-done((bf16[96,128]{0,1:T(8,128)(2,1)S(1)}, bf16[96,128]{0,1:T(8,128)(2,1)S(1)}, u32[]{:S(2)}, u32[]{:S(2)}) %collective-permute-start.35) | collective-permute-done | bytes 24608 | tf_op jit(solution)/shard_map/ppermute | solution.py:21
  227.2 10.4 %all_gather.9 = bf16[256,1536]{1,0:T(8,128)(2,1)S(1)} all-gather(bf16[64,1536]{1,0:T(8,128)(2,1)S(1)} %pad.35.clone), channel_id=1, replica_groups=mesh['tile'=128,'chan'=4] {'chan'}, dimensions={0}, use_global_device_ids=true | all-gather | bytes 983040 | tf_op jit(solution)/shard_map/all_gather | solution.py:197
  238.5 10.3 %all_gather.10 = bf16[128,1536]{1,0:T(8,128)(2,1)S(1)} all-gather(bf16[32,1536]{1,0:T(8,128)(2,1)S(1)} %pad.36), channel_id=1, replica_groups=mesh['tile'=128,'chan'=4] {'chan'}, dimensions={0}, use_global_device_ids=true | all-gather | bytes 491520 | tf_op jit(solution)/shard_map/all_gather | solution.py:198
  277.1 10.8 %collective-permute-start.37 = (bf16[64,128]{0,1:T(8,128)(2,1)S(1)}, bf16[64,128]{0,1:T(8,128)(2,1)S(1)}, u32[]{:S(2)}, u32[]{:S(2)}) collective-permute-start(bf16[64,128]{0,1:T(8,128)(2,1)S(1)} %get-tuple-element.20), channel_id=1, source_target_pairs={{0,60},{4,64},{8,68},{12,72},{16,76},{20,80},{24,84},{28,88},{32,9... | collective-permute-start | bytes 49160 | tf_op jit(solution)/shard_map/ppermute | solution.py:21
  287.9 14.7 %collective-permute-start.38 = (bf16[64,128]{0,1:T(8,128)(2,1)S(1)}, bf16[64,128]{0,1:T(8,128)(2,1)S(1)}, u32[]{:S(2)}, u32[]{:S(2)}) collective-permute-start(bf16[64,128]{0,1:T(8,128)(2,1)S(1)} %get-tuple-element.21), channel_id=1, source_target_pairs={{0,56},{4,60},{8,64},{12,68},{16,72},{20,76},{24,80},{28,84},{32,8... | collective-permute-start | bytes 49160 | tf_op jit(solution)/shard_map/ppermute | solution.py:21
  302.6 5.3 collective-permute-start.39
  307.9 7.7 collective-permute-start.40
  315.6 8.1 %collective-permute-start.41 = (bf16[64,128]{0,1:T(8,128)(2,1)S(1)}, bf16[64,128]{0,1:T(8,128)(2,1)S(1)}, u32[]{:S(2)}, u32[]{:S(2)}) collective-permute-start(bf16[64,128]{0,1:T(8,128)(2,1)S(1)} %get-tuple-element.24), channel_id=1, source_target_pairs={{0,44},{4,48},{8,52},{12,56},{16,60},{20,64},{24,68},{28,72},{32,7... | collective-permute-start | bytes 49160 | tf_op jit(solution)/shard_map/ppermute | solution.py:21
  323.8 10.5 %collective-permute-start.42 = (bf16[64,128]{0,1:T(8,128)(2,1)S(1)}, bf16[64,128]{0,1:T(8,128)(2,1)S(1)}, u32[]{:S(2)}, u32[]{:S(2)}) collective-permute-start(bf16[64,128]{0,1:T(8,128)(2,1)S(1)} %get-tuple-element.25), channel_id=1, source_target_pairs={{0,40},{4,44},{8,48},{12,52},{16,56},{20,60},{24,64},{28,68},{32,7... | collective-permute-start | bytes 49160 | tf_op jit(solution)/shard_map/ppermute | solution.py:21
  336.4 7.2 collective-permute-start.44
  343.6 9.7 %collective-permute-start.45 = (bf16[64,128]{0,1:T(8,128)(2,1)S(1)}, bf16[64,128]{0,1:T(8,128)(2,1)S(1)}, u32[]{:S(2)}, u32[]{:S(2)}) collective-permute-start(bf16[64,128]{0,1:T(8,128)(2,1)S(1)} %get-tuple-element.28), channel_id=1, source_target_pairs={{0,28},{4,32},{8,36},{12,40},{16,44},{20,48},{24,52},{28,56},{32,6... | collective-permute-start | bytes 49160 | tf_op jit(solution)/shard_map/ppermute | solution.py:21
  353.3 5.6 collective-permute-start.46
  388.9 280.6 %psum.15 = f32[64]{0:T(128)S(1)} all-reduce(f32[64]{0:T(128)} %get-tuple-element.87), channel_id=1, replica_groups=mesh['tile'=128,'chan'=4] {'tile'}, use_global_device_ids=true, to_apply=%region_2.3 | all-reduce | flops 64 | bytes 512 | tf_op jit(solution)/shard_map/psum | solution.py:265
  691.2 13.1 %all_gather.11 = bf16[256,1536]{1,0:T(8,128)(2,1)S(1)} all-gather(bf16[64,1536]{1,0:T(8,128)(2,1)S(1)} %pad.39.clone), channel_id=1, replica_groups=mesh['tile'=128,'chan'=4] {'chan'}, dimensions={0}, use_global_device_ids=true | all-gather | bytes 983040 | tf_op jit(solution)/shard_map/all_gather | solution.py:218
  714.0 20.1 %collective-permute-start.71 = (bf16[3,32,128]{2,0,1:T(4,128)(2,1)S(1)}, bf16[3,32,128]{2,0,1:T(4,128)(2,1)S(1)}, u32[]{:S(2)}, u32[]{:S(2)}) collective-permute-start(bf16[3,32,128]{2,0,1:T(4,128)(2,1)S(1)} %bitcast.530), channel_id=1, source_target_pairs={{0,260},{4,264},{8,268},{12,272},{16,276},{20,280},{24,284},{28,28... | collective-permute-start | bytes 73736 | tf_op jit(solution)/shard_map/ppermute | solution.py:26
  738.1 19.4 %collective-permute-start.72 = (bf16[3,32,128]{2,0,1:T(4,128)(2,1)S(1)}, bf16[3,32,128]{2,0,1:T(4,128)(2,1)S(1)}, u32[]{:S(2)}, u32[]{:S(2)}) collective-permute-start(bf16[3,32,128]{2,0,1:T(4,128)(2,1)S(1)} %bitcast.527), channel_id=1, source_target_pairs={{0,264},{4,268},{8,272},{12,276},{16,280},{20,284},{24,288},{28,29... | collective-permute-start | bytes 73736 | tf_op jit(solution)/shard_map/ppermute | solution.py:26
  760.2 19.0 %collective-permute-start.73 = (bf16[3,32,128]{2,0,1:T(4,128)(2,1)S(1)}, bf16[3,32,128]{2,0,1:T(4,128)(2,1)S(1)}, u32[]{:S(2)}, u32[]{:S(2)}) collective-permute-start(bf16[3,32,128]{2,0,1:T(4,128)(2,1)S(1)} %bitcast.533), channel_id=1, source_target_pairs={{0,268},{4,272},{8,276},{12,280},{16,284},{20,288},{24,292},{28,29... | collective-permute-start | bytes 73736 | tf_op jit(solution)/shard_map/ppermute | solution.py:26
  779.5 9.6 %collective-permute-start.67 = (bf16[3,32,128]{2,0,1:T(4,128)(2,1)S(1)}, bf16[3,32,128]{2,0,1:T(4,128)(2,1)S(1)}, u32[]{:S(2)}, u32[]{:S(2)}) collective-permute-start(bf16[3,32,128]{2,0,1:T(4,128)(2,1)S(1)} %bitcast.532), channel_id=1, source_target_pairs={{0,244},{4,248},{8,252},{12,256},{16,260},{20,264},{24,268},{28,27... | collective-permute-start | bytes 73736 | tf_op jit(solution)/shard_map/ppermute | solution.py:26
  (522 shorter events, 183.9 us)
Async XLA Ops:
  7.2 784.3 %all-reduce.11.cloned.1.call-start = ((), (), s32[]{:S(2)}) async-start(), calls=%async_computation | async-start | bytes 1769472 | tf_op jit(solution)/shard_map/psum | solution.py:265
  10.2 34.0 %collective-permute-start = (bf16[3,32,128]{2,0,1:T(4,128)(2,1)S(1)}, bf16[3,32,128]{2,0,1:T(4,128)(2,1)S(1)}, u32[]{:S(2)}, u32[]{:S(2)}) collective-permute-start(bf16[3,32,128]{2,0,1:T(4,128)(2,1)S(1)} %convolution_convert_fusion.9), channel_id=1, source_target_pairs={{0,244},{4,248},{8,252},{12,256},{16,260},{20,264},{24,268},{28,27... | collective-permute-start | bytes 73736 | tf_op jit(solution)/shard_map/ppermute | solution.py:26
  23.8 31.1 %collective-permute-start.1 = (bf16[3,32,128]{2,0,1:T(4,128)(2,1)S(1)}, bf16[3,32,128]{2,0,1:T(4,128)(2,1)S(1)}, u32[]{:S(2)}, u32[]{:S(2)}) collective-permute-start(bf16[3,32,128]{2,0,1:T(4,128)(2,1)S(1)} %convolution_convert_fusion.8), channel_id=1, source_target_pairs={{0,248},{4,252},{8,256},{12,260},{16,264},{20,268},{24,272},{28,27... | collective-permute-start | bytes 73736 | tf_op jit(solution)/shard_map/ppermute | solution.py:26
  28.2 48.6 %collective-permute-start.2 = (bf16[3,32,128]{2,0,1:T(4,128)(2,1)S(1)}, bf16[3,32,128]{2,0,1:T(4,128)(2,1)S(1)}, u32[]{:S(2)}, u32[]{:S(2)}) collective-permute-start(bf16[3,32,128]{2,0,1:T(4,128)(2,1)S(1)} %convolution_convert_fusion.7), channel_id=1, source_target_pairs={{0,252},{4,256},{8,260},{12,264},{16,268},{20,272},{24,276},{28,28... | collective-permute-start | bytes 73736 | tf_op jit(solution)/shard_map/ppermute | solution.py:26
  32.5 44.3 %collective-permute-start.3 = (bf16[3,32,128]{2,0,1:T(4,128)(2,1)S(1)}, bf16[3,32,128]{2,0,1:T(4,128)(2,1)S(1)}, u32[]{:S(2)}, u32[]{:S(2)}) collective-permute-start(bf16[3,32,128]{2,0,1:T(4,128)(2,1)S(1)} %convolution_convert_fusion.6), channel_id=1, source_target_pairs={{0,256},{4,260},{8,264},{12,268},{16,272},{20,276},{24,280},{28,28... | collective-permute-start | bytes 73736 | tf_op jit(solution)/shard_map/ppermute | solution.py:26
  35.9 41.0 %collective-permute-start.4 = (bf16[3,32,128]{2,0,1:T(4,128)(2,1)S(1)}, bf16[3,32,128]{2,0,1:T(4,128)(2,1)S(1)}, u32[]{:S(2)}, u32[]{:S(2)}) collective-permute-start(bf16[3,32,128]{2,0,1:T(4,128)(2,1)S(1)} %convolution_convert_fusion.5), channel_id=1, source_target_pairs={{0,260},{4,264},{8,268},{12,272},{16,276},{20,280},{24,284},{28,28... | collective-permute-start | bytes 73736 | tf_op jit(solution)/shard_map/ppermute | solution.py:26
  44.1 32.8 %collective-permute-start.5 = (bf16[3,32,128]{2,0,1:T(4,128)(2,1)S(1)}, bf16[3,32,128]{2,0,1:T(4,128)(2,1)S(1)}, u32[]{:S(2)}, u32[]{:S(2)}) collective-permute-start(bf16[3,32,128]{2,0,1:T(4,128)(2,1)S(1)} %convolution_convert_fusion.4), channel_id=1, source_target_pairs={{0,264},{4,268},{8,272},{12,276},{16,280},{20,284},{24,288},{28,29... | collective-permute-start | bytes 73736 | tf_op jit(solution)/shard_map/ppermute | solution.py:26
  54.9 28.6 %collective-permute-start.6 = (bf16[3,32,128]{2,0,1:T(4,128)(2,1)S(1)}, bf16[3,32,128]{2,0,1:T(4,128)(2,1)S(1)}, u32[]{:S(2)}, u32[]{:S(2)}) collective-permute-start(bf16[3,32,128]{2,0,1:T(4,128)(2,1)S(1)} %convolution_convert_fusion.3), channel_id=1, source_target_pairs={{0,268},{4,272},{8,276},{12,280},{16,284},{20,288},{24,292},{28,29... | collective-permute-start | bytes 73736 | tf_op jit(solution)/shard_map/ppermute | solution.py:26
  86.5 28.9 %collective-permute-start.10 = (bf16[96,128]{0,1:T(8,128)(2,1)S(1)}, bf16[96,128]{0,1:T(8,128)(2,1)S(1)}, u32[]{:S(2)}, u32[]{:S(2)}) collective-permute-start(bf16[96,128]{0,1:T(8,128)(2,1)S(1)} %get-tuple-element.53), channel_id=1, source_target_pairs={{0,48},{4,52},{8,56},{12,60},{16,64},{20,68},{24,72},{28,76},{32,8... | collective-permute-start | bytes 73736 | tf_op jit(solution)/shard_map/ppermute | solution.py:21
  91.6 29.1 %collective-permute-start.11 = (bf16[96,128]{0,1:T(8,128)(2,1)S(1)}, bf16[96,128]{0,1:T(8,128)(2,1)S(1)}, u32[]{:S(2)}, u32[]{:S(2)}) collective-permute-start(bf16[96,128]{0,1:T(8,128)(2,1)S(1)} %get-tuple-element.54), channel_id=1, source_target_pairs={{0,44},{4,48},{8,52},{12,56},{16,60},{20,64},{24,68},{28,72},{32,7... | collective-permute-start | bytes 73736 | tf_op jit(solution)/shard_map/ppermute | solution.py:21
  140.7 30.8 %collective-permute-start.23 = (bf16[96,128]{0,1:T(8,128)(2,1)S(1)}, bf16[96,128]{0,1:T(8,128)(2,1)S(1)}, u32[]{:S(2)}, u32[]{:S(2)}) collective-permute-start(bf16[96,128]{0,1:T(8,128)(2,1)S(1)} %get-tuple-element.66), channel_id=1, source_target_pairs={{8,0},{12,4},{16,8},{20,12},{24,16},{28,20},{32,24},{36,28},{40,32... | collective-permute-start | bytes 73736 | tf_op jit(solution)/shard_map/ppermute | solution.py:21
  142.0 30.8 %collective-permute-start.24 = (bf16[96,128]{0,1:T(8,128)(2,1)S(1)}, bf16[96,128]{0,1:T(8,128)(2,1)S(1)}, u32[]{:S(2)}, u32[]{:S(2)}) collective-permute-start(bf16[96,128]{0,1:T(8,128)(2,1)S(1)} %get-tuple-element.67), channel_id=1, source_target_pairs={{12,0},{16,4},{20,8},{24,12},{28,16},{32,20},{36,24},{40,28},{44,3... | collective-permute-start | bytes 73736 | tf_op jit(solution)/shard_map/ppermute | solution.py:21
  144.4 29.7 %collective-permute-start.7 = (bf16[96,128]{0,1:T(8,128)(2,1)S(1)}, bf16[96,128]{0,1:T(8,128)(2,1)S(1)}, u32[]{:S(2)}, u32[]{:S(2)}) collective-permute-start(bf16[96,128]{0,1:T(8,128)(2,1)S(1)} %get-tuple-element.50), channel_id=1, source_target_pairs={{0,60},{4,64},{8,68},{12,72},{16,76},{20,80},{24,84},{28,88},{32,9... | collective-permute-start | bytes 73736 | tf_op jit(solution)/shard_map/ppermute | solution.py:21
  193.9 30.8 %collective-permute-start.35 = (bf16[96,128]{0,1:T(8,128)(2,1)S(1)}, bf16[96,128]{0,1:T(8,128)(2,1)S(1)}, u32[]{:S(2)}, u32[]{:S(2)}) collective-permute-start(bf16[96,128]{0,1:T(8,128)(2,1)S(1)} %get-tuple-element.78), channel_id=1, source_target_pairs={{56,0},{60,4},{64,8},{68,12},{72,16},{76,20},{80,24},{84,28},{88,3... | collective-permute-start | bytes 73736 | tf_op jit(solution)/shard_map/ppermute | solution.py:21
  196.0 28.7 %collective-permute-start.36 = (bf16[96,128]{0,1:T(8,128)(2,1)S(1)}, bf16[96,128]{0,1:T(8,128)(2,1)}, u32[]{:S(2)}, u32[]{:S(2)}) collective-permute-start(bf16[96,128]{0,1:T(8,128)(2,1)S(1)} %get-tuple-element.79), channel_id=1, source_target_pairs={{60,0},{64,4},{68,8},{72,12},{76,16},{80,20},{84,24},{88,28},{92,3... | collective-permute-start | bytes 73736 | tf_op jit(solution)/shard_map/ppermute | solution.py:21
  277.1 46.7 %collective-permute-start.37 = (bf16[64,128]{0,1:T(8,128)(2,1)S(1)}, bf16[64,128]{0,1:T(8,128)(2,1)S(1)}, u32[]{:S(2)}, u32[]{:S(2)}) collective-permute-start(bf16[64,128]{0,1:T(8,128)(2,1)S(1)} %get-tuple-element.20), channel_id=1, source_target_pairs={{0,60},{4,64},{8,68},{12,72},{16,76},{20,80},{24,84},{28,88},{32,9... | collective-permute-start | bytes 49160 | tf_op jit(solution)/shard_map/ppermute | solution.py:21
  287.9 46.4 %collective-permute-start.38 = (bf16[64,128]{0,1:T(8,128)(2,1)S(1)}, bf16[64,128]{0,1:T(8,128)(2,1)S(1)}, u32[]{:S(2)}, u32[]{:S(2)}) collective-permute-start(bf16[64,128]{0,1:T(8,128)(2,1)S(1)} %get-tuple-element.21), channel_id=1, source_target_pairs={{0,56},{4,60},{8,64},{12,68},{16,72},{20,76},{24,80},{28,84},{32,8... | collective-permute-start | bytes 49160 | tf_op jit(solution)/shard_map/ppermute | solution.py:21
  302.6 33.8 %collective-permute-start.39 = (bf16[64,128]{0,1:T(8,128)(2,1)S(1)}, bf16[64,128]{0,1:T(8,128)(2,1)S(1)}, u32[]{:S(2)}, u32[]{:S(2)}) collective-permute-start(bf16[64,128]{0,1:T(8,128)(2,1)S(1)} %get-tuple-element.22), channel_id=1, source_target_pairs={{0,52},{4,56},{8,60},{12,64},{16,68},{20,72},{24,76},{28,80},{32,8... | collective-permute-start | bytes 49160 | tf_op jit(solution)/shard_map/ppermute | solution.py:21
  307.9 35.7 %collective-permute-start.40 = (bf16[64,128]{0,1:T(8,128)(2,1)S(1)}, bf16[64,128]{0,1:T(8,128)(2,1)S(1)}, u32[]{:S(2)}, u32[]{:S(2)}) collective-permute-start(bf16[64,128]{0,1:T(8,128)(2,1)S(1)} %get-tuple-element.23), channel_id=1, source_target_pairs={{0,48},{4,52},{8,56},{12,60},{16,64},{20,68},{24,72},{28,76},{32,8... | collective-permute-start | bytes 49160 | tf_op jit(solution)/shard_map/ppermute | solution.py:21
  315.6 37.7 %collective-permute-start.41 = (bf16[64,128]{0,1:T(8,128)(2,1)S(1)}, bf16[64,128]{0,1:T(8,128)(2,1)S(1)}, u32[]{:S(2)}, u32[]{:S(2)}) collective-permute-start(bf16[64,128]{0,1:T(8,128)(2,1)S(1)} %get-tuple-element.24), channel_id=1, source_target_pairs={{0,44},{4,48},{8,52},{12,56},{16,60},{20,64},{24,68},{28,72},{32,7... | collective-permute-start | bytes 49160 | tf_op jit(solution)/shard_map/ppermute | solution.py:21
  323.8 35.2 %collective-permute-start.42 = (bf16[64,128]{0,1:T(8,128)(2,1)S(1)}, bf16[64,128]{0,1:T(8,128)(2,1)S(1)}, u32[]{:S(2)}, u32[]{:S(2)}) collective-permute-start(bf16[64,128]{0,1:T(8,128)(2,1)S(1)} %get-tuple-element.25), channel_id=1, source_target_pairs={{0,40},{4,44},{8,48},{12,52},{16,56},{20,60},{24,64},{28,68},{32,7... | collective-permute-start | bytes 49160 | tf_op jit(solution)/shard_map/ppermute | solution.py:21
  378.3 291.3 %collective-permute-start.57 = (bf16[64,128]{0,1:T(8,128)(2,1)}, bf16[64,128]{0,1:T(8,128)(2,1)}, u32[]{:S(2)}, u32[]{:S(2)}) collective-permute-start(bf16[64,128]{0,1:T(8,128)(2,1)} %get-tuple-element.40), channel_id=1, source_target_pairs={{24,0},{28,4},{32,8},{36,12},{40,16},{44,20},{48,24},{52,28},{56,3... | collective-permute-start | bytes 49160 | tf_op jit(solution)/shard_map/ppermute | solution.py:21
  379.6 291.2 %collective-permute-start.58 = (bf16[64,128]{0,1:T(8,128)(2,1)}, bf16[64,128]{0,1:T(8,128)(2,1)}, u32[]{:S(2)}, u32[]{:S(2)}) collective-permute-start(bf16[64,128]{0,1:T(8,128)(2,1)} %get-tuple-element.41), channel_id=1, source_target_pairs={{28,0},{32,4},{36,8},{40,12},{44,16},{48,20},{52,24},{56,28},{60,3... | collective-permute-start | bytes 49160 | tf_op jit(solution)/shard_map/ppermute | solution.py:21
  381.6 290.5 %collective-permute-start.59 = (bf16[64,128]{0,1:T(8,128)(2,1)}, bf16[64,128]{0,1:T(8,128)(2,1)}, u32[]{:S(2)}, u32[]{:S(2)}) collective-permute-start(bf16[64,128]{0,1:T(8,128)(2,1)} %get-tuple-element.42), channel_id=1, source_target_pairs={{32,0},{36,4},{40,8},{44,12},{48,16},{52,20},{56,24},{60,28},{64,3... | collective-permute-start | bytes 49160 | tf_op jit(solution)/shard_map/ppermute | solution.py:21
  383.0 290.5 %collective-permute-start.60 = (bf16[64,128]{0,1:T(8,128)(2,1)}, bf16[64,128]{0,1:T(8,128)(2,1)}, u32[]{:S(2)}, u32[]{:S(2)}) collective-permute-start(bf16[64,128]{0,1:T(8,128)(2,1)} %get-tuple-element.43), channel_id=1, source_target_pairs={{36,0},{40,4},{44,8},{48,12},{52,16},{56,20},{60,24},{64,28},{68,3... | collective-permute-start | bytes 49160 | tf_op jit(solution)/shard_map/ppermute | solution.py:21
  386.6 288.2 %collective-permute-start.61 = (bf16[64,128]{0,1:T(8,128)(2,1)}, bf16[64,128]{0,1:T(8,128)(2,1)}, u32[]{:S(2)}, u32[]{:S(2)}) collective-permute-start(bf16[64,128]{0,1:T(8,128)(2,1)} %get-tuple-element.44), channel_id=1, source_target_pairs={{40,0},{44,4},{48,8},{52,12},{56,16},{60,20},{64,24},{68,28},{72,3... | collective-permute-start | bytes 49160 | tf_op jit(solution)/shard_map/ppermute | solution.py:21
  712.0 48.2 %collective-permute-start.68 = (bf16[3,32,128]{2,0,1:T(4,128)(2,1)S(1)}, bf16[3,32,128]{2,0,1:T(4,128)(2,1)S(1)}, u32[]{:S(2)}, u32[]{:S(2)}) collective-permute-start(bf16[3,32,128]{2,0,1:T(4,128)(2,1)S(1)} %bitcast.531), channel_id=1, source_target_pairs={{0,248},{4,252},{8,256},{12,260},{16,264},{20,268},{24,272},{28,27... | collective-permute-start | bytes 73736 | tf_op jit(solution)/shard_map/ppermute | solution.py:26
  714.0 65.5 %collective-permute-start.71 = (bf16[3,32,128]{2,0,1:T(4,128)(2,1)S(1)}, bf16[3,32,128]{2,0,1:T(4,128)(2,1)S(1)}, u32[]{:S(2)}, u32[]{:S(2)}) collective-permute-start(bf16[3,32,128]{2,0,1:T(4,128)(2,1)S(1)} %bitcast.530), channel_id=1, source_target_pairs={{0,260},{4,264},{8,268},{12,272},{16,276},{20,280},{24,284},{28,28... | collective-permute-start | bytes 73736 | tf_op jit(solution)/shard_map/ppermute | solution.py:26
  734.2 55.2 %collective-permute-start.70 = (bf16[3,32,128]{2,0,1:T(4,128)(2,1)S(1)}, bf16[3,32,128]{2,0,1:T(4,128)(2,1)S(1)}, u32[]{:S(2)}, u32[]{:S(2)}) collective-permute-start(bf16[3,32,128]{2,0,1:T(4,128)(2,1)S(1)} %bitcast.529), channel_id=1, source_target_pairs={{0,256},{4,260},{8,264},{12,268},{16,272},{20,276},{24,280},{28,28... | collective-permute-start | bytes 73736 | tf_op jit(solution)/shard_map/ppermute | solution.py:26
  736.1 53.5 %collective-permute-start.69 = (bf16[3,32,128]{2,0,1:T(4,128)(2,1)S(1)}, bf16[3,32,128]{2,0,1:T(4,128)(2,1)S(1)}, u32[]{:S(2)}, u32[]{:S(2)}) collective-permute-start(bf16[3,32,128]{2,0,1:T(4,128)(2,1)S(1)} %bitcast.528), channel_id=1, source_target_pairs={{0,252},{4,256},{8,260},{12,264},{16,268},{20,272},{24,276},{28,28... | collective-permute-start | bytes 73736 | tf_op jit(solution)/shard_map/ppermute | solution.py:26
  738.1 51.8 %collective-permute-start.72 = (bf16[3,32,128]{2,0,1:T(4,128)(2,1)S(1)}, bf16[3,32,128]{2,0,1:T(4,128)(2,1)S(1)}, u32[]{:S(2)}, u32[]{:S(2)}) collective-permute-start(bf16[3,32,128]{2,0,1:T(4,128)(2,1)S(1)} %bitcast.527), channel_id=1, source_target_pairs={{0,264},{4,268},{8,272},{12,276},{16,280},{20,284},{24,288},{28,29... | collective-permute-start | bytes 73736 | tf_op jit(solution)/shard_map/ppermute | solution.py:26
  760.2 30.0 %collective-permute-start.73 = (bf16[3,32,128]{2,0,1:T(4,128)(2,1)S(1)}, bf16[3,32,128]{2,0,1:T(4,128)(2,1)S(1)}, u32[]{:S(2)}, u32[]{:S(2)}) collective-permute-start(bf16[3,32,128]{2,0,1:T(4,128)(2,1)S(1)} %bitcast.533), channel_id=1, source_target_pairs={{0,268},{4,272},{8,276},{12,280},{16,284},{20,288},{24,292},{28,29... | collective-permute-start | bytes 73736 | tf_op jit(solution)/shard_map/ppermute | solution.py:26
  (140 other events, 4125.9 us)
Sparse Core Ops, SparseCore 0:
  389.1 355.7 all-reduce.10
where the time goes:
time: 803 us; the launch traced here: 801 us
  starting transfers between devices  346 us (43%)
  blocking collectives  314 us (39%)
  waiting for transfers between devices  57.9 us (7%)
  matrix products  24.8 us (3%)
  other arithmetic  20.2 us (3%)
  local copies, waits for them, and re-layouts  19.9 us (2%)
  between operations  17.6 us (2%)
    psum x1, blocking collectives, on_device(): weight_sum, bias_sum = lax.psum((weight_part, bias_part), 'tile')  281 us
    ppermute x60, starting transfers between devices, shifted(): return lax.ppermute(array, axis, pairs)  212 us
    ppermute x14, starting transfers between devices, from_behind(): lax.ppermute(array, axis, [(i, (i + by) % size) for i in range(size)])  133 us
    ppermute x60, waiting for transfers between devices, shifted(): return lax.ppermute(array, axis, pairs)  51.3 us
  transfers between devices with their start and end apart: 75, of which 19 were waited for; matrix products, arithmetic and copies ran while one was open for 3% of the time, Pallas kernels for 0%

commit v1 on v0

v1 whole, which is shorter than its diff:
```python
import functools
import math

import jax
import jax.numpy as jnp
import numpy as np
from jax import lax
from jax.experimental import pallas as pl
from jax.experimental.pallas import tpu as pltpu
from jax.sharding import PartitionSpec as P

BF, F32 = jnp.bfloat16, jnp.float32
TILES = 128
HALF = TILES // 2
LANES = 128
OG0, OC0, BIAS0 = 48, 68, 92
VMEM = pl.BlockSpec(memory_space=pltpu.VMEM)
SMEM = pl.BlockSpec(memory_space=pltpu.SMEM)

CHIP_STEPS = (-1, 0, 1)
ROW_CHIPS = [[8 * r + 2 * i + c for i in range(4)] for r in range(16) for c in range(2)]
SAME_CORE = [[2 * i + c for i in range(64)] for c in range(2)]


def one_hot(shape, pairs):
    table = np.zeros(shape, np.float32)
    for at in pairs:
        table[at] = 1.0
    return table.astype(jnp.bfloat16)


def edge_tables():
    atm = [(128 * (l // 2) + l % 2, l) for l in range(16)]
    atm += [(128 * (l // 2) + 126 + l % 2, 16 + l) for l in range(16)]
    grad = [(128 * r, 32 + r) for r in range(8)] + [(128 * r + 127, 40 + r) for r in range(8)]
    ocean = [(cell, lane + 64) for cell, lane in atm]
    return np.stack([one_hot((1024, 128), pairs) for pairs in (atm, grad, ocean)])


def corner_tables():
    tables = []
    for south in (0, 1):
        for east in (0, 1):
            first = 10 if south else 0
            near = 9 if south else 0
            col = 0 if east else 126
            both = [(128 * q + col + j, 4 * (first + q) + 2 * east + j) for q in (0, 1) for j in (0, 1)]
            both.append((256 + (0 if east else 127), OG0 + 2 * near + east))
            parts = [both]
            for q in (0, 1):
                parts.append([(384 + col + j, OC0 + 2 * (first + q) + j) for j in (0, 1)])
            tables.append(np.stack([one_hot((512, 128), pairs) for pairs in parts]))
    return np.stack(tables)


def beside_tables():
    tables = []
    for east in (0, 1):
        given = 0 if east else 16
        both = [(given + 2 * i + j, 4 * (i + 2) + 2 * east + j) for i in range(8) for j in (0, 1)]
        both += [((32 if east else 40) + i, OG0 + 2 * (i + 1) + east) for i in range(8)]
        ocean = [(64 + given + 2 * i + j, OC0 + 2 * (i + 2) + j) for i in range(8) for j in (0, 1)]
        tables.append(np.stack([one_hot((128, 128), pairs) for pairs in (both, ocean)]))
    return np.stack(tables)


def shift_tables():
    back = one_hot((128, 128), [(j - 1, j) for j in range(1, 128)])
    ahead = one_hot((128, 128), [(j + 1, j) for j in range(127)])
    return np.stack([back, ahead])


def input_side_tables():
    west = one_hot((128, 128 * 12), [(4 * r + 1, 128 * r) for r in range(12)])
    east = one_hot((128, 128 * 12), [(4 * r + 2, 128 * r + 127) for r in range(12)])
    gather = [(1536 + l, l) for l in range(48)]
    gather += [(128 * r + 127 * w, 48 + 2 * r + w) for r in range(12) for w in (0, 1)]
    taps = []
    for s in (-1, 0, 1):
        for t in (-1, 0, 1):
            at = 128 * (3 * (s + 1) + t + 1)
            for i in range(-1, 9):
                for w in (0, 1):
                    r = i + s + 2
                    col = (128 if w else -1) + t
                    lane = {-2: 4 * r, -1: 4 * r + 1, 128: 4 * r + 2, 129: 4 * r + 3, 0: 48 + 2 * r, 127: 49 + 2 * r}[col]
                    taps.append((lane, at + OG0 + 2 * (i + 1) + w))
    ocean = [one_hot((128, 128), [(OC0 + 2 * r + j, 4 * r + 2 * e + j) for r in range(12) for j in (0, 1)]) for e in (0, 1)]
    return np.stack([west, east]), one_hot((1664, 128), gather), one_hot((128, 9 * 128), taps), np.stack(ocean)


def grad_side_tables():
    west = one_hot((128, 128 * 10), [(OG0 + 2 * r, 128 * r) for r in range(10)])
    east = one_hot((128, 128 * 10), [(OG0 + 2 * r + 1, 128 * r + 127) for r in range(10)])
    return np.stack([west, east])


def dot(a, b):
    return jnp.dot(a, b, preferred_element_type=F32)


def dot_last(a, b):
    return lax.dot_general(a, b, (((1,), (1,)), ((), ())), preferred_element_type=F32)


def call(kernel, outs, in_specs, scratch=(), limit=32):
    return pl.pallas_call(
        kernel,
        out_shape=[jax.ShapeDtypeStruct(shape, dtype) for shape, dtype in outs],
        in_specs=list(in_specs),
        out_specs=[VMEM] * len(outs),
        scratch_shapes=list(scratch),
        compiler_params=pltpu.CompilerParams(vmem_limit_bytes=limit << 20),
    )


def parcels_kernel(place, sends, ocean, atm, grad, *outs):
    tile = place[0]
    facing = 1 - 2 * (tile & 1)

    def parcel(out, at, shift):
        target = (tile + HALF + shift) & (TILES - 1)
        for slot in range(3):
            block = sends[slot, target]
            start = pl.multiple_of(jnp.maximum(block, 0) * LANES, LANES)
            data = ocean[:, pl.ds(start, LANES)]
            rows = pl.ds(at + 32 * slot, 32)
            out[rows, :] = jnp.where(block >= 0, data, jnp.zeros_like(data))

    for step, out in zip(CHIP_STEPS, outs[:3]):
        parcel(out, 0, 2 * step)
        parcel(out, 96, 2 * step + facing)
    parcel(outs[3], 0, -3 * facing)
    for chan in range(4):
        outs[4][chan, 0:64] = atm[...]
        outs[4][chan, 64:128] = grad[...]


def regrid_kernel(place, sources, blocks, a0, a1, a2, crossed, far, weights, atm, grad, picks, regridded, north, south, sides, held, acc):
    tile = place[0]
    facing = 1 - 2 * (tile & 1)
    for i, ref in enumerate((a0, a1, a2)):
        held[pl.ds(96 * i, 96), :] = ref[0:96, :]
    held[288:576, :] = crossed[0:288, :]
    held[576:672, :] = far[...]
    acc[...] = jnp.zeros_like(acc)
    for k in range(4):
        shift = ((sources[0, k] - tile - HALF + 3 + 2 * TILES) & (TILES - 1)) - 3
        odd = shift & 1
        even_at = 1 - (shift >> 1)
        odd_at = jnp.where(shift == -3 * facing, 6, 4 + ((facing - shift) >> 1))
        at = jnp.clip(jnp.where(odd == 1, odd_at, even_at), 0, 6)
        for slot in range(3):
            block = blocks[0, 3 * k + slot]

            @pl.when(block >= 0)
            def _():
                rows = pl.ds(pl.multiple_of(at * 96 + 32 * slot, 32), 32)
                into = pl.ds(pl.multiple_of(block * 32, 32), 32)
                acc[into, :] += dot(held[rows, :], weights[3 * k + slot])

    for a in range(8):
        regridded[:, LANES * a : LANES * (a + 1)] = acc[32 * a : 32 * (a + 1), :].astype(BF)
    north[:, 0:256] = atm[:, 0:256]
    north[:, 256:384] = grad[:, 0:128]
    north[0:32, 384:512] = regridded[:, 0:128]
    north[32:64, 384:512] = regridded[:, 128:256]
    south[:, 0:256] = atm[:, 768:1024]
    south[:, 256:384] = grad[:, 896:1024]
    south[0:32, 384:512] = regridded[:, 768:896]
    south[32:64, 384:512] = regridded[:, 896:1024]
    edges = dot(atm[...], picks[0]) + dot(grad[...], picks[1])
    sides[0:32, :] = (edges[0:32] + dot(regridded[...], picks[2])).astype(BF)
    sides[32:64, :] = edges[32:64].astype(BF)


def select_kernel(place, own_near, mate_near, gathered, corners, beside, own, mate):
    core = place[0] & 1
    for near, out in ((own_near, own), (mate_near, mate)):

        def pick(direction):
            device = near[0, direction]
            here = (device >= 0) & ((device & 1) == core)
            chip = (device & 7) >> 1
            return jnp.where(here, chip, 0), here

        def strip(direction, lanes):
            chip, here = pick(direction)
            data = gathered[chip, :, lanes[0] : lanes[1]]
            return jnp.where(here, data, jnp.zeros_like(data))

        out[:, 0:512] = strip(0, (0, 512))
        out[:, 512:1024] = strip(1, (512, 1024))
        total = jnp.zeros((64, 128), F32)
        halves = [jnp.zeros((32, 128), F32), jnp.zeros((32, 128), F32)]
        for east in (0, 1):
            data = strip(2 + east, (1024, 1152))
            total = total + dot(data, beside[east, 0])
            halves[east] = halves[east] + dot(data[0:32], beside[east, 1])
            for at_south in (0, 1):
                corner = 2 * at_south + east
                data = strip(4 + corner, (512, 1024) if at_south else (0, 512))
                total = total + dot(data, corners[corner, 0])
                halves[east] = halves[east] + dot(data[0:32], corners[corner, 1])
                halves[east] = halves[east] + dot(data[32:64], corners[corner, 2])
        out[0:32, 1024:1152] = (total[0:32] + halves[0]).astype(BF)
        out[32:64, 1024:1152] = (total[32:64] + halves[1]).astype(BF)


def pack_kernel(own, crossed, regridded, bias, shard):
    shard[:, 0:1024] = own[:, 0:1024] + crossed[:, 0:1024]
    side = own[:, 1024:1152].astype(F32) + crossed[:, 1024:1152].astype(F32)
    lane = lax.broadcasted_iota(jnp.int32, (64, 128), 1)
    rest = bias[...]
    for i in range(3):
        part = rest.astype(BF).astype(F32)
        side = jnp.where(lane == BIAS0 + i, part, side)
        rest = rest - part
    shard[:, 1024:1152] = side.astype(BF)
    shard[0:32, 1152:1664] = regridded[:, 0:512]
    shard[32:64, 1152:1664] = regridded[:, 512:1024]


def forward_kernel(
    place, inner, outer, weights, shifts, in_edges, in_gather, in_taps, ocean_sides,
    output, z_all, mine, theirs, plain, taps, side_taps, grads, outs,
):
    chan, core = place[1], place[0] & 1
    for c in range(4):
        atm = slice(64 * c, 64 * c + 64)
        sea = slice(256 + 32 * c, 288 + 32 * c)
        plain[atm, 0:256] = outer[c, :, 0:256]
        plain[atm, 256:1280] = inner[c, 0:64, :]
        plain[atm, 1280:1536] = outer[c, :, 512:768]
        plain[atm, 1536:1664] = outer[c, :, 1024:1152]
        plain[sea, 0:128] = outer[c, 0:32, 384:512]
        plain[sea, 128:256] = outer[c, 32:64, 384:512]
        plain[sea, 256:768] = outer[c, 0:32, 1152:1664]
        plain[sea, 768:1280] = outer[c, 32:64, 1152:1664]
        plain[sea, 1280:1408] = outer[c, 0:32, 896:1024]
        plain[sea, 1408:1536] = outer[c, 32:64, 896:1024]
        side = dot(outer[c, 0:32, 1024:1152], ocean_sides[0]) + dot(outer[c, 32:64, 1024:1152], ocean_sides[1])
        plain[sea, 1536:1664] = side.astype(BF)
        grads[atm, 0:128] = outer[c, :, 256:384]
        grads[atm, 128:1152] = inner[c, 64:128, :]
        grads[atm, 1152:1280] = outer[c, :, 768:896]
        lane = lax.broadcasted_iota(jnp.int32, (64, 128), 1)
        side = outer[c, :, 1024:1152]
        grads[atm, 1280:1408] = jnp.where((lane >= OG0) & (lane < OC0), side, jnp.zeros_like(side))
    side = plain[:, 1536:1664]
    for at, t in ((0, 0), (2, 1)):
        rows = slice(384 * at, 384 * at + 384)
        edges = dot(side, in_edges[t])
        for r in range(12):
            lanes = slice(128 * r, 128 * r + 128)
            moved = dot(plain[:, lanes], shifts[t])
            taps[rows, lanes] = (moved + edges[:, lanes]).astype(BF)
    taps[384:768, :] = plain[:, 0:1536]
    columns = dot(plain[...], in_gather[...]).astype(BF)
    for s in range(3):
        for t in range(3):
            lanes = slice(128 * (3 * s + t), 128 * (3 * s + t) + 128)
            side_taps[384 * t : 384 * t + 384, 128 * s : 128 * s + 128] = dot(columns, in_taps[:, lanes]).astype(BF)
    bias = jnp.concatenate(
        [jnp.sum(outer[c, :, 1024 + BIAS0 : 1024 + BIAS0 + 3].astype(F32), axis=1, keepdims=True) for c in range(4)], axis=0
    )

    def activate(total, lanes):
        pre = total + bias
        gate = 1.0 / (1.0 + jnp.exp(-pre))
        z_all[:, lanes] = (grads[:, lanes].astype(F32) * gate * (1.0 + pre * (1.0 - gate))).astype(BF)
        return pre * gate

    for r in range(0, 10, 2):
        total = jnp.zeros((256, 256), F32)
        for s in range(3):
            total = total + dot(weights[s], taps[:, 128 * (r + s) : 128 * (r + s) + 256])
        silu = activate(total, slice(128 * r, 128 * r + 256))
        for q in (0, 1):
            row = r + q - 1
            if 0 <= row < 8:
                state = plain[0:256, 128 * (row + 2) : 128 * (row + 3)].astype(F32)
                outs[:, 128 * row : 128 * row + 128] = (state + silu[:, 128 * q : 128 * q + 128]).astype(BF)
    total = jnp.zeros((256, 128), F32)
    for s in range(3):
        total = total + dot(weights[s], side_taps[:, 128 * s : 128 * s + 128])
    activate(total, slice(1280, 1408))
    rows = pl.ds(pl.multiple_of(chan * 64, 64), 64)
    output[...] = outs[rows, :]
    own = z_all[rows, 128:1152]
    sums = dot_last(jnp.ones((16, 1024), BF), own)
    for half, first in ((0, mine), (1, theirs)):
        first[54:64] = jnp.zeros((10, 16, 128), F32)
        first[54, :, 0:64] = sums
    for s in range(3):
        found = dot_last(own, taps[:, 128 * (s + 1) : 128 * (s + 1) + 1024])
        for t in range(3):
            for a in range(4):
                for l in range(3):
                    piece = found[16 * a : 16 * a + 16, 384 * t + 128 * l : 384 * t + 128 * l + 128]
                    row = 4 * (3 * s + t) + a
                    half, at = row // 18, (row % 18) * 3 + l

                    @pl.when(core == half)
                    def _():
                        mine[at] = piece

                    @pl.when(core != half)
                    def _():
                        theirs[at] = piece


def backward_kernel(
    place, sources, blocks, z_all, weights, shifts, z_edges, regrid_weights, grad,
    input_grad, r0, r1, r2, far, taps, delta, terms,
):
    tile, chan = place[0], place[1]
    facing = 1 - 2 * (tile & 1)
    side = z_all[:, 1280:1408]
    for at, t in ((0, 1), (2, 0)):
        rows = slice(256 * at, 256 * at + 256)
        edges = dot(side, z_edges[t])
        for r in range(10):
            lanes = slice(128 * r, 128 * r + 128)
            moved = dot(z_all[:, lanes], shifts[t])
            taps[rows, lanes] = (moved + edges[:, lanes]).astype(BF)
    taps[256:512, :] = z_all[:, 0:1280]
    atm_rows = pl.ds(pl.multiple_of(chan * 64, 64), 64)
    sea_rows = pl.ds(pl.multiple_of(256 + chan * 32, 32), 32)
    for q in range(4):
        atm_total = jnp.zeros((64, 256), F32)
        sea_total = jnp.zeros((32, 256), F32)
        for s in range(3):
            first = 128 * (2 * q + 2 - s)
            for t in range(3):
                window = taps[256 * t : 256 * t + 256, first : first + 256]
                atm_total = atm_total + dot(weights[3 * s + t, atm_rows, :], window)
                sea_total = sea_total + dot(weights[3 * s + t, sea_rows, :], window)
        lanes = slice(256 * q, 256 * q + 256)
        input_grad[:, lanes] = (grad[:, lanes].astype(F32) + atm_total).astype(BF)
        delta[:, lanes] = sea_total.astype(BF)
    for e in range(12):
        block = blocks[0, e]
        lanes = pl.ds(pl.multiple_of(jnp.maximum(block, 0) * LANES, LANES), LANES)
        term = dot_last(delta[:, lanes], regrid_weights[e])
        terms[32 * e : 32 * e + 32, :] = jnp.where(block >= 0, term, 0.0).astype(BF)
    terms[384:480, :] = jnp.zeros((96, 128), BF)

    def parcel(out, at, shift):
        target = (tile + HALF + shift) & (TILES - 1)
        found = jnp.int32(4)
        for k in range(4):
            found = jnp.where(sources[0, k] == target, k, found)
        out[at : at + 96, :] = terms[pl.ds(pl.multiple_of(found * 96, 96), 96), :]

    for step, out in zip(CHIP_STEPS, (r0, r1, r2)):
        parcel(out, 0, 2 * step)
        parcel(out, 96, 2 * step + facing)
    parcel(far, 0, -3 * facing)


def return_kernel(place, sends, a0, a1, a2, crossed, far, ocean_grad, acc):
    tile = place[0]
    facing = 1 - 2 * (tile & 1)
    acc[...] = jnp.zeros_like(acc)

    def add(ref, first, shift):
        sender = (tile + HALF + shift) & (TILES - 1)
        for slot in range(3):
            block = sends[slot, sender]

            @pl.when(block >= 0)
            def _():
                into = pl.ds(pl.multiple_of(block * 32, 32), 32)
                acc[into, :] += ref[first + 32 * slot : first + 32 * slot + 32, :].astype(F32)

    for i, (step, ref) in enumerate(zip(CHIP_STEPS, (a0, a1, a2))):
        add(ref, 0, -2 * step)
        add(crossed, 96 * i, -2 * step + facing)
    add(far, 0, -3 * facing)
    for b in range(8):
        ocean_grad[:, LANES * b : LANES * (b + 1)] = acc[32 * b : 32 * (b + 1), :]


def sum_kernel(scale, arrived, out):
    total = jnp.sum(arrived[...].astype(F32), axis=0) * scale
    for i in range(64):
        out[i] = total.astype(BF)


def finish_kernel(place, held, crossed, weight_grad, bias_grad):
    core = place[0] & 1
    for half in range(2):
        for a in range(18):
            row = 18 * half + a
            k, part = row // 4, row % 4
            for l in range(3):
                at = 3 * a + l
                piece = jnp.where(core == half, held[at].astype(F32), crossed[at].astype(F32))
                weight_grad[k, 16 * part : 16 * part + 16, 128 * l : 128 * l + 128] = piece
    bias_grad[...] = held[54].astype(F32)[0:8]


def send(array, target):
    return lax.ppermute(array, "tile", [(i, target(i)) for i in range(TILES)])


def spread(a0, a1, a2, far):
    moved = [send(a, lambda i, step=step: (i + HALF + 2 * step) % TILES) for step, a in zip(CHIP_STEPS, (a0, a1, a2))]
    beyond = send(far, lambda i: (i + HALF - 3 * (1 - 2 * (i % 2))) % TILES)
    return moved, beyond


def to_mate(array):
    return send(array, lambda i: i ^ 1)


def on_device(
    atm_state,
    ocean_state,
    conv_weight,
    conv_bias,
    regrid_weight,
    out_grad,
    atm_neighbours,
    coupling_sources,
    coupling_blocks,
    coupling_sends,
):
    place = jnp.stack([lax.axis_index("tile"), lax.axis_index("chan")]).astype(jnp.int32)
    sends = coupling_sends[0].T
    flipped = jnp.swapaxes(conv_weight.reshape(3, 1152, 256), 1, 2)
    b0, b1, b2, far, copies = call(
        parcels_kernel, [((192, 128), BF)] * 3 + [((96, 128), BF), ((4, 128, 1024), BF)], [SMEM, SMEM, VMEM, VMEM, VMEM]
    )(place, sends, ocean_state, atm_state, out_grad)
    inner = lax.all_to_all(copies, "chan", 0, 0)
    (a0, a1, a2), far = spread(b0, b1, b2, far)
    table = jnp.pad(atm_neighbours.astype(BF), ((0, 15), (0, 120)))
    crossed = to_mate(jnp.concatenate([a0[96:], a1[96:], a2[96:], table], axis=0))
    mate_near = crossed[288:289, 0:8].astype(jnp.int32)
    regridded, north, south, sides = call(
        regrid_kernel,
        [((32, 1024), BF), ((64, 512), BF), ((64, 512), BF), ((64, 128), BF)],
        [SMEM] * 3 + [VMEM] * 9,
        [pltpu.VMEM((672, 128), BF), pltpu.VMEM((256, 128), F32)],
    )(place, coupling_sources, coupling_blocks, a0, a1, a2, crossed, far, regrid_weight, atm_state, out_grad, jnp.asarray(edge_tables()))
    from_north = lax.ppermute(south, "tile", [(i, i + 8) for i in range(TILES - 8)])
    from_south = lax.ppermute(north, "tile", [(i + 8, i) for i in range(TILES - 8)])
    strips = lax.all_gather(jnp.concatenate([from_north, from_south, sides], axis=1), "tile", axis_index_groups=ROW_CHIPS)
    own, mate = call(select_kernel, [((64, 1152), BF)] * 2, [SMEM] * 3 + [VMEM] * 3)(
        place, atm_neighbours, mate_near, strips, jnp.asarray(corner_tables()), jnp.asarray(beside_tables())
    )
    crossed = to_mate(mate)
    (shard,) = call(pack_kernel, [((64, 1664), BF)], [VMEM] * 4)(own, crossed, regridded, conv_bias.reshape(64, 1))
    outer = lax.all_gather(shard, "chan")
    in_edges, in_gather, in_taps, ocean_sides = (jnp.asarray(table) for table in input_side_tables())
    shifts = jnp.asarray(shift_tables())
    atm_output, z_all, mine, theirs = call(
        forward_kernel,
        [((64, 1024), BF), ((256, 1408), BF), ((64, 16, 128), F32), ((64, 16, 128), F32)],
        [SMEM] + [VMEM] * 8,
        [
            pltpu.VMEM((384, 1664), BF),
            pltpu.VMEM((1152, 1536), BF),
            pltpu.VMEM((1152, 384), BF),
            pltpu.VMEM((256, 1408), BF),
            pltpu.VMEM((256, 1024), BF),
        ],
        limit=48,
    )(place, inner, outer, flipped, shifts, in_edges, in_gather, in_taps, ocean_sides)
    theirs = to_mate(theirs)
    input_grad, b0, b1, b2, far = call(
        backward_kernel,
        [((64, 1024), BF)] + [((192, 128), BF)] * 3 + [((96, 128), BF)],
        [SMEM] * 3 + [VMEM] * 6,
        [pltpu.VMEM((768, 1280), BF), pltpu.VMEM((32, 1024), BF), pltpu.VMEM((480, 128), BF)],
        limit=48,
    )(place, coupling_sources, coupling_blocks, z_all, conv_weight, shifts, jnp.asarray(grad_side_tables()), regrid_weight, out_grad)
    shares = lax.all_to_all((mine + theirs).astype(BF), "tile", 0, 0, axis_index_groups=SAME_CORE)
    (a0, a1, a2), far = spread(b0, b1, b2, far)
    crossed = to_mate(jnp.concatenate([a0[96:], a1[96:], a2[96:]], axis=0))
    (ocean_grad,) = call(return_kernel, [((32, 1024), F32)], [SMEM] * 2 + [VMEM] * 5, [pltpu.VMEM((256, 128), F32)])(
        place, sends, a0, a1, a2, crossed, far
    )
    scale = 1.0 / math.sqrt(atm_state.shape[1] * TILES)
    (summed,) = call(functools.partial(sum_kernel, scale), [((64, 16, 128), BF)], [VMEM])(shares)
    held = lax.all_to_all(summed, "tile", 0, 0, axis_index_groups=SAME_CORE)
    crossed = to_mate(held)
    weight_grad, bias_grad = call(finish_kernel, [((9, 64, 384), F32), ((8, 128), F32)], [SMEM, VMEM, VMEM])(place, held, crossed)
    return atm_output, input_grad, ocean_grad, jnp.swapaxes(weight_grad, 1, 2), bias_grad[0, 0:64]


def solution(mesh):
    placed = (
        P("chan", "tile"),
        P("chan", "tile"),
        P(),
        P("chan"),
        P("tile", None, None),
        P("chan", "tile"),
        P("tile", None),
        P("tile", None),
        P("tile", None),
        P("tile", None, None),
    )
    return jax.shard_map(
        on_device,
        mesh=mesh,
        in_specs=placed,
        out_specs=(
            P("chan", "tile"),
            P("chan", "tile"),
            P("chan", "tile"),
            P(None, None, "chan"),
            P("chan"),
        ),
        check_vma=False,
    )
```

time: 803 us -> 224 us (0.28)
  starting transfers between devices: 346 us -> 67.1 us
  blocking collectives: 314 us -> 91.4 us
  waiting for transfers between devices: 57.9 us -> 19.7 us
  matrix products: 24.8 us -> 0 us
  Pallas kernels: 0 us -> 24.7 us
  other arithmetic: 20.2 us -> 0.83 us
  between operations: 17.6 us -> 1 us
    ppermute x74 -> x15, starting transfers between devices: 346 us -> 62.9 us  [the longest x13 59.9 us: send(): return lax.ppermute(array, 'tile', [(i, target(i)) for i in range(TILES)])]
    psum x1 -> x0, blocking collectives: 281 us -> none  [on_device(): weight_sum, bias_sum = lax.psum((weight_part, bias_part), 'tile')]
    all_to_all x0 -> x2, blocking collectives: none -> 58.9 us  [the longest x1 33.9 us: on_device(): lax.all_to_all((mine + theirs).astype(BF), 'tile', 0, 0, axis_index_group...]
    ppermute x74 -> x15, waiting for transfers between devices: 57.9 us -> 19.7 us  [the longest x13 11.8 us: send(): return lax.ppermute(array, 'tile', [(i, target(i)) for i in range(TILES)])]
    dot_general x79 -> x0, matrix products: 24.8 us -> none  [the longest x18 6.6 us: contract_lead(): lax.dot_general(weights, operand, (((0,), (0,)), ((), ())), preferred_ele...]
    pallas_call x0 -> x9, Pallas kernels: none -> 24.7 us  [the longest x1 11.2 us: on_device(): call(forward_kernel, [((64, 1024), BF), ((256, 1408), BF), ((64, 16, 128)...]
    all_gather x3 -> x2, blocking collectives: 33.8 us -> 32.6 us  [the longest x1 19.4 us: on_device(): lax.all_gather(jnp.concatenate([from_north, from_south, sides], axis=1),...]
  transfers between devices with their start and end apart: 75 -> 16, of which waited for: 19 -> 6; matrix products, arithmetic and copies ran while one was open for 3% -> 2% of each run, Pallas kernels for 0% -> 5%
where the time goes in v1:
time: 224 us; the launch traced here: 222 us
  blocking collectives  91.4 us (41%)
  starting transfers between devices  67.1 us (30%)
  Pallas kernels  24.7 us (11%)
  waiting for transfers between devices  19.7 us (9%)
  local copies, waits for them, and re-layouts  16.8 us (8%)
    ppermute x13, starting transfers between devices, send(): return lax.ppermute(array, 'tile', [(i, target(i)) for i in range(TILES)])  59.9 us
    all_to_all x1, blocking collectives, on_device(): lax.all_to_all((mine + theirs).astype(BF), 'tile', 0, 0, axis_index_group...  33.9 us
    all_to_all x1, blocking collectives, on_device(): held = lax.all_to_all(summed, 'tile', 0, 0, axis_index_groups=SAME_CORE)  25 us
    all_gather x1, blocking collectives, on_device(): lax.all_gather(jnp.concatenate([from_north, from_south, sides], axis=1),...  19.4 us
    all_gather x1, blocking collectives, on_device(): outer = lax.all_gather(shard, 'chan')  13.1 us
    unnamed x61, local copies, waits for them, and re-layouts  12.7 us
    ppermute x13, waiting for transfers between devices, send(): return lax.ppermute(array, 'tile', [(i, target(i)) for i in range(TILES)])  11.8 us
    pallas_call x1, Pallas kernels, on_device(): call(forward_kernel, [((64, 1024), BF), ((256, 1408), BF), ((64, 16, 128)...  11.2 us
  transfers between devices with their start and end apart: 16, of which 6 were waited for; matrix products, arithmetic and copies ran while one was open for 2% of the time, Pallas kernels for 5%

profile of v1, /device:TPU:1, one launch (start us, length us, event | category | flops | bytes accessed | tf_op | source)
XLA Modules:
  0.0 221.6 jit_solution(9404912571110557954)
XLA Ops:
  4.1 1.7 shard_map.218
  5.8 12.9 %collective-permute-start = (bf16[192,128]{1,0:T(8,128)(2,1)S(1)}, bf16[192,128]{1,0:T(8,128)(2,1)S(1)}, u32[]{:S(2)}, u32[]{:S(2)}) collective-permute-start(bf16[192,128]{1,0:T(8,128)(2,1)S(1)} %get-tuple-element.28), channel_id=1, source_target_pairs={{0,248},{4,252},{8,256},{12,260},{16,264},{20,268},{24,272},{28,27... | collective-permute-start | bytes 147464 | tf_op jit(solution)/shard_map/ppermute | solution.py:405
  18.7 4.4 %collective-permute-start.1 = (bf16[192,128]{1,0:T(8,128)(2,1)S(1)}, bf16[192,128]{1,0:T(8,128)(2,1)S(1)}, u32[]{:S(2)}, u32[]{:S(2)}) collective-permute-start(bf16[192,128]{1,0:T(8,128)(2,1)S(1)} %get-tuple-element.29), channel_id=1, source_target_pairs={{0,256},{4,260},{8,264},{12,268},{16,272},{20,276},{24,280},{28,28... | collective-permute-start | bytes 147464 | tf_op jit(solution)/shard_map/ppermute | solution.py:405
  23.1 1.9 collective-permute-start.2
  25.7 4.3 %collective-permute-done.2.a2 = bf16[192,128]{1,0:T(8,128)(2,1)S(1)} collective-permute-done((bf16[192,128]{1,0:T(8,128)(2,1)S(1)}, bf16[192,128]{1,0:T(8,128)(2,1)S(1)}, u32[]{:S(2)}, u32[]{:S(2)}) %collective-permute-start.2) | collective-permute-done | bytes 49184 | tf_op jit(solution)/shard_map/ppermute | solution.py:405
  30.0 4.3 %collective-permute-start.3 = (bf16[304,128]{1,0:T(8,128)(2,1)S(1)}, bf16[304,128]{1,0:T(8,128)(2,1)S(1)}, u32[]{:S(2)}, u32[]{:S(2)}) collective-permute-start(bf16[304,128]{1,0:T(8,128)(2,1)S(1)} %fusion.1), channel_id=1, source_target_pairs={{0,4},{4,0},{8,12},{12,8},{16,20},{20,16},{24,28},{28,24},{32,36},... | collective-permute-start | bytes 233480 | tf_op jit(solution)/shard_map/ppermute | solution.py:405
  34.3 1.9 collective-permute-start.4
  36.3 4.2 %all-to-all-start = ((bf16[4,128,1024]{2,1,0:T(8,128)(2,1)}), bf16[4,128,1024]{2,1,0:T(8,128)(2,1)S(1)}, u32[]{:S(2)}, u32[]{:S(2)}) async-start(bf16[4,128,1024]{2,1,0:T(8,128)(2,1)} %get-tuple-element.27), calls=%async_computation | async-start | bytes 2097152 | tf_op jit(solution)/shard_map/all_to_all | solution.py:436
  40.5 2.4 %collective-permute-done.4.far = bf16[96,128]{1,0:T(8,128)(2,1)S(1)} collective-permute-done((bf16[96,128]{1,0:T(8,128)(2,1)S(1)}, bf16[96,128]{1,0:T(8,128)(2,1)S(1)}, u32[]{:S(2)}, u32[]{:S(2)}) %collective-permute-start.4) | collective-permute-done | bytes 24608 | tf_op jit(solution)/shard_map/ppermute | solution.py:405
  42.9 2.2 shard_map.219
  45.8 1.7 collective-permute-start.5
  48.8 8.0 %collective-permute-done.6 = bf16[64,512]{1,0:T(8,128)(2,1)S(1)} collective-permute-done((bf16[64,512]{1,0:T(8,128)(2,1)S(1)}, bf16[64,512]{1,0:T(8,128)(2,1)S(1)}, u32[]{:S(2)}, u32[]{:S(2)}) %collective-permute-start.6) | collective-permute-done | bytes 65568 | tf_op jit(solution)/shard_map/ppermute | solution.py:448
  56.8 19.4 %all-gather = bf16[256,1152]{1,0:T(8,128)(2,1)S(1)} all-gather(bf16[64,1152]{1,0:T(8,128)(2,1)S(1)} %pad_maximum_fusion), channel_id=2, replica_groups={{0,8,16,24},{4,12,20,28},{32,40,48,56},{36,44,52,60},{64,72,80,88},{68,..., dimensions={0}, use_global_device_ids=true | all-gather | bytes 737280 | tf_op jit(solution)/shard_map/all_gather | solution.py:449
  77.5 1.9 shard_map.220
  79.4 1.9 collective-permute-start.7
  82.7 2.2 %copy.26 = bf16[3,1152,256]{1,2,0:T(8,128)(2,1)} copy(bf16[3,1152,256]{2,1,0:T(8,128)(2,1)S(1)} %bitcast.15) | data formatting | bytes 3538944 | tf_op jit(solution)/shard_map/reshape | solution.py:432
  87.5 13.1 %all-gather.1 = bf16[256,1664]{1,0:T(8,128)(2,1)} all-gather(bf16[64,1664]{1,0:T(8,128)(2,1)S(1)} %shard_map.221), channel_id=3, replica_groups=mesh['tile'=128,'chan'=4] {'chan'}, dimensions={0}, use_global_device_ids=true | all-gather | bytes 1064960 | tf_op jit(solution)/shard_map/all_gather | solution.py:455
  106.4 11.2 %shard_map.222 = (bf16[64,1024]{1,0:T(8,128)(2,1)}, bf16[256,1408]{1,0:T(8,128)(2,1)S(1)}, f32[64,16,128]{2,1,0:T(8,128)S(1)}, f32[64,16,128]{2,1,0:T(8,128)S(1)}) custom-call(s32[2]{0:T(128)S(1)} %copy-done.22, bf16[4,128,1024]{2,1,0:T(8,128)(2,1)S(1)} %all-to-all-done.inner, bf16[4,64,1664]{2,1,0:T(8,128)(2,1)S(1)} %bitcast.16, ...), custom_call_target="tpu_custom_call" | custom-call | tf_op jit(solution)/shard_map/pallas_call | solution.py:458
  117.6 4.6 %collective-permute-start.13 = (f32[64,16,128]{2,1,0:T(8,128)S(1)}, f32[64,16,128]{2,1,0:T(8,128)S(1)}, u32[]{:S(2)}, u32[]{:S(2)}) collective-permute-start(f32[64,16,128]{2,1,0:T(8,128)S(1)} %get-tuple-element.46), channel_id=1, source_target_pairs={{0,4},{4,0},{8,12},{12,8},{16,20},{20,16},{24,28},{28,24},{32,36},... | collective-permute-start | bytes 1572872 | tf_op jit(solution)/shard_map/ppermute | solution.py:405
  122.2 1.5 collective-permute-done.13
  123.8 33.9 %all_to_all.15.arrived = bf16[64,16,128]{2,1,0:T(8,128)(2,1)S(1)} all-to-all(bf16[64,16,128]{2,1,0:T(8,128)(2,1)S(1)} %add_convert_fusion), channel_id=1, replica_groups={{0,8,16,24,32,40,48,56,64,72,80,88,96,104,112,120,128,136,144,152,160,1..., dimensions={0} | all-to-all | bytes 524288 | tf_op jit(solution)/shard_map/all_to_all | solution.py:479
  157.8 25.0 %all_to_all.16.held = bf16[64,16,128]{2,1,0:T(8,128)(2,1)S(1)} all-to-all(bf16[64,16,128]{2,1,0:T(8,128)(2,1)S(1)} %shard_map.225), channel_id=1, replica_groups={{0,8,16,24,32,40,48,56,64,72,80,88,96,104,112,120,128,136,144,152,160,1..., dimensions={0} | all-to-all | bytes 524288 | tf_op jit(solution)/shard_map/all_to_all | solution.py:487
  182.7 5.9 %collective-permute-start.14 = (bf16[64,16,128]{2,1,0:T(8,128)(2,1)S(1)}, bf16[64,16,128]{2,1,0:T(8,128)(2,1)S(1)}, u32[]{:S(2)}, u32[]{:S(2)}) collective-permute-start(bf16[64,16,128]{2,1,0:T(8,128)(2,1)S(1)} %all_to_all.16.held), channel_id=1, source_target_pairs={{0,4},{4,0},{8,12},{12,8},{16,20},{20,16},{24,28},{28,24},{32,36},... | collective-permute-start | bytes 786440 | tf_op jit(solution)/shard_map/ppermute | solution.py:405
  188.6 3.7 %shard_map.223 = (bf16[64,1024]{1,0:T(8,128)(2,1)}, bf16[192,128]{1,0:T(8,128)(2,1)S(1)}, bf16[192,128]{1,0:T(8,128)(2,1)S(1)}, bf16[192,128]{1,0:T(8,128)(2,1)S(1)}, bf16[96,128]{1,0:T(8,128)(2,1)S(1)}) custom-call(s32[2]{0:T(128)S(1)} %copy-done.22, s32[1,4]{1,0:T(1,128)S(1)} %copy-done.26, s32[1,12]{1,0:T(1,128)S(1)} %copy-done.28, ...), custom_call_target="tpu_custom_call" | custom-call | tf_op jit(solution)/shard_map/pallas_call | solution.py:472
  192.4 3.4 %collective-permute-start.8 = (bf16[192,128]{1,0:T(8,128)(2,1)S(1)}, bf16[192,128]{1,0:T(8,128)(2,1)S(1)}, u32[]{:S(2)}, u32[]{:S(2)}) collective-permute-start(bf16[192,128]{1,0:T(8,128)(2,1)S(1)} %get-tuple-element.41), channel_id=1, source_target_pairs={{0,248},{4,252},{8,256},{12,260},{16,264},{20,268},{24,272},{28,27... | collective-permute-start | bytes 147464 | tf_op jit(solution)/shard_map/ppermute | solution.py:405
  195.8 3.3 %collective-permute-start.9 = (bf16[192,128]{1,0:T(8,128)(2,1)S(1)}, bf16[192,128]{1,0:T(8,128)(2,1)S(1)}, u32[]{:S(2)}, u32[]{:S(2)}) collective-permute-start(bf16[192,128]{1,0:T(8,128)(2,1)S(1)} %get-tuple-element.42), channel_id=1, source_target_pairs={{0,256},{4,260},{8,264},{12,268},{16,272},{20,276},{24,280},{28,28... | collective-permute-start | bytes 147464 | tf_op jit(solution)/shard_map/ppermute | solution.py:405
  199.1 5.7 %collective-permute-start.10 = (bf16[192,128]{1,0:T(8,128)(2,1)S(1)}, bf16[192,128]{1,0:T(8,128)(2,1)S(1)}, u32[]{:S(2)}, u32[]{:S(2)}) collective-permute-start(bf16[192,128]{1,0:T(8,128)(2,1)S(1)} %get-tuple-element.43), channel_id=1, source_target_pairs={{0,264},{4,268},{8,272},{12,276},{16,280},{20,284},{24,288},{28,29... | collective-permute-start | bytes 147464 | tf_op jit(solution)/shard_map/ppermute | solution.py:405
  206.0 3.6 %collective-permute-start.11 = (bf16[288,128]{1,0:T(8,128)(2,1)S(1)}, bf16[288,128]{1,0:T(8,128)(2,1)S(1)}, u32[]{:S(2)}, u32[]{:S(2)}) collective-permute-start(bf16[288,128]{1,0:T(8,128)(2,1)S(1)} %pad_maximum_fusion.1), channel_id=1, source_target_pairs={{0,4},{4,0},{8,12},{12,8},{16,20},{20,16},{24,28},{28,24},{32,36},... | collective-permute-start | bytes 221192 | tf_op jit(solution)/shard_map/ppermute | solution.py:405
  209.7 6.2 %collective-permute-start.12 = (bf16[96,128]{1,0:T(8,128)(2,1)S(1)}, bf16[96,128]{1,0:T(8,128)(2,1)S(1)}, u32[]{:S(2)}, u32[]{:S(2)}) collective-permute-start(bf16[96,128]{1,0:T(8,128)(2,1)S(1)} %get-tuple-element.44), channel_id=1, source_target_pairs={{0,244},{4,272},{8,252},{12,280},{16,260},{20,288},{24,268},{28,29... | collective-permute-start | bytes 73736 | tf_op jit(solution)/shard_map/ppermute | solution.py:405
  215.9 2.2 %collective-permute-done.12.far = bf16[96,128]{1,0:T(8,128)(2,1)S(1)} collective-permute-done((bf16[96,128]{1,0:T(8,128)(2,1)S(1)}, bf16[96,128]{1,0:T(8,128)(2,1)S(1)}, u32[]{:S(2)}, u32[]{:S(2)}) %collective-permute-start.12) | collective-permute-done | bytes 24608 | tf_op jit(solution)/shard_map/ppermute | solution.py:405
  218.1 1.4 shard_map.224
  219.6 1.5 shard_map.226
  (90 shorter events, 19.1 us)
Async XLA Ops:
  0.6 42.3 %copy-start.3 = (bf16[12,128,128]{2,1,0:T(8,128)(2,1)S(1)}, bf16[12,128,128]{2,1,0:T(8,128)(2,1)}, u32[]{:S(2)}) copy-start(bf16[12,128,128]{2,1,0:T(8,128)(2,1)} %regrid_weights.1) | copy-start | bytes 1179652
  1.4 32.9 %copy-start.23 = (s32[1,128,3]{1,2,0:T(4,128)}, s32[1,128,3]{1,2,0:T(4,128)S(1)}, u32[]{:S(2)}) copy-start(s32[1,128,3]{1,2,0:T(4,128)S(1)} %copy.29) | copy-start | bytes 4612
  1.5 41.4 %copy-start.20 = (s32[2]{0:T(128)}, s32[2]{0:T(128)S(1)}, u32[]{:S(2)}) copy-start(s32[2]{0:T(128)S(1)} %pad_add_fusion.place) | copy-start | bytes 28
  4.1 38.8 %copy-start.5 = (bf16[64,1024]{1,0:T(8,128)(2,1)S(1)}, bf16[64,1024]{1,0:T(8,128)(2,1)}, u32[]{:S(2)}) copy-start(bf16[64,1024]{1,0:T(8,128)(2,1)} %grad.5) | copy-start | bytes 393220
  4.1 38.8 %copy-start.6 = (bf16[3,1024,128]{2,1,0:T(8,128)(2,1)S(1)}, bf16[3,1024,128]{2,1,0:T(8,128)(2,1)}, u32[]{:S(2)}) copy-start(bf16[3,1024,128]{2,1,0:T(8,128)(2,1)} %constant.30.clone.picks) | copy-start | bytes 2359300
  4.1 38.8 %copy-start.10 = (bf16[64,1024]{1,0:T(8,128)(2,1)S(1)}, bf16[64,1024]{1,0:T(8,128)(2,1)}, u32[]{:S(2)}) copy-start(bf16[64,1024]{1,0:T(8,128)(2,1)} %atm.3) | copy-start | bytes 393220
  4.1 38.8 %copy-start.25 = (s32[1,4]{1,0:T(1,128)S(1)}, s32[1,4]{1,0:T(1,128)}, u32[]{:S(2)}) copy-start(s32[1,4]{1,0:T(1,128)} %sources.3) | copy-start | bytes 52
  4.1 38.8 %copy-start.27 = (s32[1,12]{1,0:T(1,128)S(1)}, s32[1,12]{1,0:T(1,128)}, u32[]{:S(2)}) copy-start(s32[1,12]{1,0:T(1,128)} %blocks.3) | copy-start | bytes 148
  5.8 19.8 %collective-permute-start = (bf16[192,128]{1,0:T(8,128)(2,1)S(1)}, bf16[192,128]{1,0:T(8,128)(2,1)S(1)}, u32[]{:S(2)}, u32[]{:S(2)}) collective-permute-start(bf16[192,128]{1,0:T(8,128)(2,1)S(1)} %get-tuple-element.28), channel_id=1, source_target_pairs={{0,248},{4,252},{8,256},{12,260},{16,264},{20,268},{24,272},{28,27... | collective-permute-start | bytes 147464 | tf_op jit(solution)/shard_map/ppermute | solution.py:405
  18.7 7.0 %collective-permute-start.1 = (bf16[192,128]{1,0:T(8,128)(2,1)S(1)}, bf16[192,128]{1,0:T(8,128)(2,1)S(1)}, u32[]{:S(2)}, u32[]{:S(2)}) collective-permute-start(bf16[192,128]{1,0:T(8,128)(2,1)S(1)} %get-tuple-element.29), channel_id=1, source_target_pairs={{0,256},{4,260},{8,264},{12,268},{16,272},{20,276},{24,280},{28,28... | collective-permute-start | bytes 147464 | tf_op jit(solution)/shard_map/ppermute | solution.py:405
  23.1 6.9 %collective-permute-start.2 = (bf16[192,128]{1,0:T(8,128)(2,1)S(1)}, bf16[192,128]{1,0:T(8,128)(2,1)S(1)}, u32[]{:S(2)}, u32[]{:S(2)}) collective-permute-start(bf16[192,128]{1,0:T(8,128)(2,1)S(1)} %get-tuple-element.30), channel_id=1, source_target_pairs={{0,264},{4,268},{8,272},{12,276},{16,280},{20,284},{24,288},{28,29... | collective-permute-start | bytes 147464 | tf_op jit(solution)/shard_map/ppermute | solution.py:405
  30.0 12.9 %collective-permute-start.3 = (bf16[304,128]{1,0:T(8,128)(2,1)S(1)}, bf16[304,128]{1,0:T(8,128)(2,1)S(1)}, u32[]{:S(2)}, u32[]{:S(2)}) collective-permute-start(bf16[304,128]{1,0:T(8,128)(2,1)S(1)} %fusion.1), channel_id=1, source_target_pairs={{0,4},{4,0},{8,12},{12,8},{16,20},{20,16},{24,28},{28,24},{32,36},... | collective-permute-start | bytes 233480 | tf_op jit(solution)/shard_map/ppermute | solution.py:405
  34.3 8.5 %collective-permute-start.4 = (bf16[96,128]{1,0:T(8,128)(2,1)S(1)}, bf16[96,128]{1,0:T(8,128)(2,1)S(1)}, u32[]{:S(2)}, u32[]{:S(2)}) collective-permute-start(bf16[96,128]{1,0:T(8,128)(2,1)S(1)} %get-tuple-element.31), channel_id=1, source_target_pairs={{0,244},{4,272},{8,252},{12,280},{16,260},{20,288},{24,268},{28,29... | collective-permute-start | bytes 73736 | tf_op jit(solution)/shard_map/ppermute | solution.py:405
  36.3 64.4 %all-to-all-start = ((bf16[4,128,1024]{2,1,0:T(8,128)(2,1)}), bf16[4,128,1024]{2,1,0:T(8,128)(2,1)S(1)}, u32[]{:S(2)}, u32[]{:S(2)}) async-start(bf16[4,128,1024]{2,1,0:T(8,128)(2,1)} %get-tuple-element.27), calls=%async_computation | async-start | bytes 2097152 | tf_op jit(solution)/shard_map/all_to_all | solution.py:436
  40.5 35.7 %copy-start.2 = (bf16[4,3,512,128]{3,2,1,0:T(8,128)(2,1)S(1)}, bf16[4,3,512,128]{3,2,1,0:T(8,128)(2,1)}, u32[]{:S(2)}) copy-start(bf16[4,3,512,128]{3,2,1,0:T(8,128)(2,1)} %constant.31.clone.corners) | copy-start | bytes 4718596
  40.5 35.7 %copy-start.14 = (bf16[2,2,128,128]{3,2,1,0:T(8,128)(2,1)S(1)}, bf16[2,2,128,128]{3,2,1,0:T(8,128)(2,1)}, u32[]{:S(2)}) copy-start(bf16[2,2,128,128]{3,2,1,0:T(8,128)(2,1)} %constant.32.clone.beside) | copy-start | bytes 393220
  45.8 36.9 %copy-start = (bf16[9,384,256]{2,1,0:T(8,128)(2,1)S(1)}, bf16[9,384,256]{2,1,0:T(8,128)(2,1)}, u32[]{:S(2)}) copy-start(bf16[9,384,256]{2,1,0:T(8,128)(2,1)} %weights.3) | copy-start | bytes 5308420
  45.8 3.0 %collective-permute-start.5 = (bf16[64,512]{1,0:T(8,128)(2,1)S(1)}, bf16[64,512]{1,0:T(8,128)(2,1)S(1)}, u32[]{:S(2)}, u32[]{:S(2)}) collective-permute-start(bf16[64,512]{1,0:T(8,128)(2,1)S(1)} %get-tuple-element.32), channel_id=1, source_target_pairs={{0,32},{4,36},{8,40},{12,44},{16,48},{20,52},{24,56},{28,60},{32,6... | collective-permute-start | bytes 196616 | tf_op jit(solution)/shard_map/ppermute | solution.py:447
  47.5 9.3 %collective-permute-start.6 = (bf16[64,512]{1,0:T(8,128)(2,1)S(1)}, bf16[64,512]{1,0:T(8,128)(2,1)S(1)}, u32[]{:S(2)}, u32[]{:S(2)}) collective-permute-start(bf16[64,512]{1,0:T(8,128)(2,1)S(1)} %get-tuple-element.33), channel_id=1, source_target_pairs={{32,0},{36,4},{40,8},{44,12},{48,16},{52,20},{56,24},{60,28},{64,3... | collective-permute-start | bytes 196616 | tf_op jit(solution)/shard_map/ppermute | solution.py:448
  79.4 5.5 %collective-permute-start.7 = (bf16[64,1152]{1,0:T(8,128)(2,1)}, bf16[64,1152]{1,0:T(8,128)(2,1)}, u32[]{:S(2)}, u32[]{:S(2)}) collective-permute-start(bf16[64,1152]{1,0:T(8,128)(2,1)} %get-tuple-element.36), channel_id=1, source_target_pairs={{0,4},{4,0},{8,12},{12,8},{16,20},{20,16},{24,28},{28,24},{32,36},... | collective-permute-start | bytes 442376 | tf_op jit(solution)/shard_map/ppermute | solution.py:405
  82.7 18.0 %copy-start.13 = (bf16[2,128,128]{2,1,0:T(8,128)(2,1)S(1)}, bf16[2,128,128]{2,1,0:T(8,128)(2,1)}, u32[]{:S(2)}) copy-start(bf16[2,128,128]{2,1,0:T(8,128)(2,1)} %constant.37.clone.shifts) | copy-start | bytes 196612
  117.6 71.0 %copy-start.8 = (bf16[2,128,1280]{2,1,0:T(8,128)(2,1)S(1)}, bf16[2,128,1280]{2,1,0:T(8,128)(2,1)}, u32[]{:S(2)}) copy-start(bf16[2,128,1280]{2,1,0:T(8,128)(2,1)} %constant.38.clone.z_edges) | copy-start | bytes 1966084
  117.6 71.0 %copy-start.26 = (s32[1,4]{1,0:T(1,128)S(1)}, s32[1,4]{1,0:T(1,128)}, u32[]{:S(2)}) copy-start(s32[1,4]{1,0:T(1,128)} %sources.3) | copy-start | bytes 52
  117.6 71.0 %copy-start.28 = (s32[1,12]{1,0:T(1,128)S(1)}, s32[1,12]{1,0:T(1,128)}, u32[]{:S(2)}) copy-start(s32[1,12]{1,0:T(1,128)} %blocks.3) | copy-start | bytes 148
  117.6 6.1 %collective-permute-start.13 = (f32[64,16,128]{2,1,0:T(8,128)S(1)}, f32[64,16,128]{2,1,0:T(8,128)S(1)}, u32[]{:S(2)}, u32[]{:S(2)}) collective-permute-start(f32[64,16,128]{2,1,0:T(8,128)S(1)} %get-tuple-element.46), channel_id=1, source_target_pairs={{0,4},{4,0},{8,12},{12,8},{16,20},{20,16},{24,28},{28,24},{32,36},... | collective-permute-start | bytes 1572872 | tf_op jit(solution)/shard_map/ppermute | solution.py:405
  182.7 36.8 %collective-permute-start.14 = (bf16[64,16,128]{2,1,0:T(8,128)(2,1)S(1)}, bf16[64,16,128]{2,1,0:T(8,128)(2,1)S(1)}, u32[]{:S(2)}, u32[]{:S(2)}) collective-permute-start(bf16[64,16,128]{2,1,0:T(8,128)(2,1)S(1)} %all_to_all.16.held), channel_id=1, source_target_pairs={{0,4},{4,0},{8,12},{12,8},{16,20},{20,16},{24,28},{28,24},{32,36},... | collective-permute-start | bytes 786440 | tf_op jit(solution)/shard_map/ppermute | solution.py:405
  188.6 29.5 %copy-start.24 = (s32[1,128,3]{1,2,0:T(4,128)S(1)}, s32[1,128,3]{1,2,0:T(4,128)}, u32[]{:S(2)}) copy-start(s32[1,128,3]{1,2,0:T(4,128)} %copy-done.23) | copy-start | bytes 4612
  192.4 12.4 %collective-permute-start.8 = (bf16[192,128]{1,0:T(8,128)(2,1)S(1)}, bf16[192,128]{1,0:T(8,128)(2,1)S(1)}, u32[]{:S(2)}, u32[]{:S(2)}) collective-permute-start(bf16[192,128]{1,0:T(8,128)(2,1)S(1)} %get-tuple-element.41), channel_id=1, source_target_pairs={{0,248},{4,252},{8,256},{12,260},{16,264},{20,268},{24,272},{28,27... | collective-permute-start | bytes 147464 | tf_op jit(solution)/shard_map/ppermute | solution.py:405
  195.8 9.0 %collective-permute-start.9 = (bf16[192,128]{1,0:T(8,128)(2,1)S(1)}, bf16[192,128]{1,0:T(8,128)(2,1)S(1)}, u32[]{:S(2)}, u32[]{:S(2)}) collective-permute-start(bf16[192,128]{1,0:T(8,128)(2,1)S(1)} %get-tuple-element.42), channel_id=1, source_target_pairs={{0,256},{4,260},{8,264},{12,268},{16,272},{20,276},{24,280},{28,28... | collective-permute-start | bytes 147464 | tf_op jit(solution)/shard_map/ppermute | solution.py:405
  199.1 6.9 %collective-permute-start.10 = (bf16[192,128]{1,0:T(8,128)(2,1)S(1)}, bf16[192,128]{1,0:T(8,128)(2,1)S(1)}, u32[]{:S(2)}, u32[]{:S(2)}) collective-permute-start(bf16[192,128]{1,0:T(8,128)(2,1)S(1)} %get-tuple-element.43), channel_id=1, source_target_pairs={{0,264},{4,268},{8,272},{12,276},{16,280},{20,284},{24,288},{28,29... | collective-permute-start | bytes 147464 | tf_op jit(solution)/shard_map/ppermute | solution.py:405
  206.0 12.1 %collective-permute-start.11 = (bf16[288,128]{1,0:T(8,128)(2,1)S(1)}, bf16[288,128]{1,0:T(8,128)(2,1)S(1)}, u32[]{:S(2)}, u32[]{:S(2)}) collective-permute-start(bf16[288,128]{1,0:T(8,128)(2,1)S(1)} %pad_maximum_fusion.1), channel_id=1, source_target_pairs={{0,4},{4,0},{8,12},{12,8},{16,20},{20,16},{24,28},{28,24},{32,36},... | collective-permute-start | bytes 221192 | tf_op jit(solution)/shard_map/ppermute | solution.py:405
  209.7 8.4 %collective-permute-start.12 = (bf16[96,128]{1,0:T(8,128)(2,1)S(1)}, bf16[96,128]{1,0:T(8,128)(2,1)S(1)}, u32[]{:S(2)}, u32[]{:S(2)}) collective-permute-start(bf16[96,128]{1,0:T(8,128)(2,1)S(1)} %get-tuple-element.44), channel_id=1, source_target_pairs={{0,244},{4,272},{8,252},{12,280},{16,260},{20,288},{24,268},{28,29... | collective-permute-start | bytes 73736 | tf_op jit(solution)/shard_map/ppermute | solution.py:405
  (14 other events, 11.9 us)

commit v2 on v1

v2 whole, which is shorter than its diff:
```python
import functools
import math

import jax
import jax.numpy as jnp
from jax import lax
from jax.experimental import pallas as pl
from jax.experimental.pallas import tpu as pltpu
from jax.sharding import PartitionSpec as P

BF, F32 = jnp.bfloat16, jnp.float32
TILES = 128
HALF = TILES // 2
LANES = 128
OG0, OC0, BIAS0 = 48, 68, 92
VMEM = pl.BlockSpec(memory_space=pltpu.VMEM)
SMEM = pl.BlockSpec(memory_space=pltpu.SMEM)
HELD = pl.BlockSpec(memory_space=pl.ANY)

CHIP_STEPS = (-1, 0, 1)
ROW_CHIPS = [[8 * r + 2 * i + c for i in range(4)] for r in range(16) for c in range(2)]
SAME_CORE = [[2 * i + c for i in range(64)] for c in range(2)]


def grid(rows, columns):
    shape = (rows, columns)
    return lax.broadcasted_iota(jnp.int32, shape, 0), lax.broadcasted_iota(jnp.int32, shape, 1)


def marks(where):
    return jnp.where(where, 1.0, 0.0).astype(BF)


def edge_table(first):
    cell, lane = grid(1024, 128)
    col, at = cell & 127, first + 2 * (cell >> 7)
    return marks(((col < 2) & (lane == at + col)) | ((col >= 126) & (lane == at + col - 110)))


def grad_edge_table():
    cell, lane = grid(1024, 128)
    col, row = cell & 127, cell >> 7
    return marks(((col == 0) & (lane == 32 + row)) | ((col == 127) & (lane == 40 + row)))


def pair_table(given, to):
    lane, into = grid(128, 128)
    return marks((lane >= given) & (lane < given + 2) & (into - to == lane - given))


def single_table(given, to):
    lane, into = grid(128, 128)
    return marks((lane == given) & (into == to))


def beside_table(given, to, step):
    lane, into = grid(128, 128)
    at = lane - given
    return marks((at >= 0) & (at < 16) & (into == to + step * (at >> 1) + (at & 1)))


def beside_grad_table(given, to):
    lane, into = grid(128, 128)
    at = lane - given
    return marks((at >= 0) & (at < 8) & (into == to + 2 * at))


def shift_table(step):
    lane, into = grid(128, 128)
    return marks(lane == into + step)


def shift_tables():
    return jnp.concatenate([shift_table(-1), shift_table(1)], axis=1)


def edge_rows():
    lane, into = grid(128, 256)
    return jnp.where(into == 0, lane, jnp.where(into == 255, lane - 1, -8))


def edge_marks(rows, first):
    return marks(rows == first)


def gather_table():
    lane, into = grid(1536, 128)
    col, row = lane & 127, lane >> 7
    return marks(((col == 0) & (into == 48 + 2 * row)) | ((col == 127) & (into == 49 + 2 * row)))


def tap_table(s, t):
    lane, into = grid(128, 128)
    at = into - OG0
    east, row = at & 1, (at >> 1) + s + 1
    col = jnp.where(east == 1, 128, -1) + t
    near = jnp.where(col == 0, 48 + 2 * row, 49 + 2 * row)
    far = jnp.where(col < 0, 4 * row + col + 2, 4 * row + col - 126)
    given = jnp.where((col == 0) | (col == 127), near, far)
    return marks((at >= 0) & (at < 20) & (lane == given))


def ocean_side_table(east):
    lane, into = grid(128, 128)
    at = lane - OC0
    return marks((at >= 0) & (at < 24) & (into == 4 * (at >> 1) + (at & 1) + 2 * east))


def dot(a, b):
    return jnp.dot(a, b, preferred_element_type=F32)


def dot_last(a, b):
    return lax.dot_general(a, b, (((1,), (1,)), ((), ())), preferred_element_type=F32)


def call(kernel, outs, in_specs, scratch=(), limit=32, cost=1):
    return pl.pallas_call(
        kernel,
        out_shape=[jax.ShapeDtypeStruct(shape, dtype) for shape, dtype in outs],
        in_specs=list(in_specs),
        out_specs=[VMEM] * len(outs),
        scratch_shapes=list(scratch),
        compiler_params=pltpu.CompilerParams(vmem_limit_bytes=limit << 20),
        cost_estimate=pl.CostEstimate(flops=cost * 10**9, bytes_accessed=cost * 3 * 10**6, transcendentals=0),
    )


def parcels_kernel(sends, ocean, *outs):
    tile = lax.axis_index("tile")
    facing = 1 - 2 * (tile & 1)

    def parcel(out, at, shift):
        target = (tile + HALF + shift) & (TILES - 1)
        for slot in range(3):
            block = sends[slot, target]
            start = pl.multiple_of(jnp.maximum(block, 0) * LANES, LANES)
            data = ocean[:, pl.ds(start, LANES)]
            rows = pl.ds(at + 32 * slot, 32)
            out[rows, :] = jnp.where(block >= 0, data, jnp.zeros_like(data))

    for step, out in zip(CHIP_STEPS, outs[:3]):
        parcel(out, 0, 2 * step)
        parcel(out, 96, 2 * step + facing)
    parcel(outs[3], 0, -3 * facing)


def copies_kernel(atm, grad, copies):
    for chan in range(4):
        copies[chan, 0:64] = atm[...]
        copies[chan, 64:128] = grad[...]


def regrid_kernel(sources, blocks, a0, a1, a2, crossed, far, weights, atm, grad, regridded, north, south, sides, held, acc):
    tile = lax.axis_index("tile")
    facing = 1 - 2 * (tile & 1)
    for i, ref in enumerate((a0, a1, a2)):
        held[pl.ds(96 * i, 96), :] = ref[0:96, :]
    held[288:576, :] = crossed[0:288, :]
    held[576:672, :] = far[...]
    acc[...] = jnp.zeros_like(acc)
    for k in range(4):
        shift = ((sources[0, k] - tile - HALF + 3 + 2 * TILES) & (TILES - 1)) - 3
        odd = shift & 1
        even_at = 1 - (shift >> 1)
        odd_at = jnp.where(shift == -3 * facing, 6, 4 + ((facing - shift) >> 1))
        at = jnp.clip(jnp.where(odd == 1, odd_at, even_at), 0, 6)
        for slot in range(3):
            block = blocks[0, 3 * k + slot]

            @pl.when(block >= 0)
            def _():
                rows = pl.ds(pl.multiple_of(at * 96 + 32 * slot, 32), 32)
                into = pl.ds(pl.multiple_of(block * 32, 32), 32)
                acc[into, :] += dot(held[rows, :], weights[3 * k + slot])

    for a in range(8):
        regridded[:, LANES * a : LANES * (a + 1)] = acc[32 * a : 32 * (a + 1), :].astype(BF)
    north[:, 0:256] = atm[:, 0:256]
    north[:, 256:384] = grad[:, 0:128]
    north[0:32, 384:512] = regridded[:, 0:128]
    north[32:64, 384:512] = regridded[:, 128:256]
    south[:, 0:256] = atm[:, 768:1024]
    south[:, 256:384] = grad[:, 896:1024]
    south[0:32, 384:512] = regridded[:, 768:896]
    south[32:64, 384:512] = regridded[:, 896:1024]
    edges = dot(atm[...], edge_table(0)) + dot(grad[...], grad_edge_table())
    sides[0:32, :] = (edges[0:32] + dot(regridded[...], edge_table(64))).astype(BF)
    sides[32:64, :] = edges[32:64].astype(BF)


def select_kernel(own_near, mate_near, gathered, regridded, bias, own, mate):
    core = lax.axis_index("tile") & 1
    for near, out in ((own_near, own), (mate_near, mate)):

        def pick(direction):
            device = near[0, direction]
            here = (device >= 0) & ((device & 1) == core)
            chip = (device & 7) >> 1
            return jnp.where(here, chip, 0), here

        def strip(direction, lanes):
            chip, here = pick(direction)
            data = gathered[chip, :, lanes[0] : lanes[1]]
            return jnp.where(here, data, jnp.zeros_like(data))

        out[:, 0:512] = strip(0, (0, 512))
        out[:, 512:1024] = strip(1, (512, 1024))
        total = jnp.zeros((64, 128), F32)
        halves = [jnp.zeros((32, 128), F32), jnp.zeros((32, 128), F32)]
        for east in (0, 1):
            data = strip(2 + east, (1024, 1152))
            given = 0 if east else 16
            picks = beside_table(given, 8 + 2 * east, 4) + beside_grad_table(32 if east else 40, OG0 + 2 + east)
            total = total + dot(data, picks)
            halves[east] = halves[east] + dot(data[0:32], beside_table(64 + given, OC0 + 4, 2))
            col = 0 if east else 126
            for at_south in (0, 1):
                first, beyond = (10, 9) if at_south else (0, 0)
                data = strip(4 + 2 * at_south + east, (512, 1024) if at_south else (0, 512))
                for q in (0, 1):
                    total = total + dot(data[:, 128 * q : 128 * q + 128], pair_table(col, 4 * (first + q) + 2 * east))
                    halves[east] = halves[east] + dot(data[32 * q : 32 * q + 32, 384:512], pair_table(col, OC0 + 2 * (first + q)))
                total = total + dot(data[:, 256:384], single_table(0 if east else 127, OG0 + 2 * beyond + east))
        out[0:32, 1024:1152] = (total[0:32] + halves[0]).astype(BF)
        out[32:64, 1024:1152] = (total[32:64] + halves[1]).astype(BF)
    side = own[:, 1024:1152].astype(F32)
    row, _ = grid(64, 64)
    _, lane = grid(64, 128)
    rest = jnp.sum(jnp.where(row == lane[:, 0:64], bias[...], 0.0), axis=1, keepdims=True)
    for i in range(3):
        part = rest.astype(BF).astype(F32)
        side = jnp.where(lane == BIAS0 + i, part, side)
        rest = rest - part
    own[:, 1024:1152] = side.astype(BF)
    own[0:32, 1152:1664] = regridded[:, 0:512]
    own[32:64, 1152:1664] = regridded[:, 512:1024]


def forward_kernel(
    inner, outer_held, flipped, output, z_all, mine, theirs, side_atm, taps, side_taps, grads, outs, weights, outer, lifted, sems
):
    chan, core = lax.axis_index("chan"), lax.axis_index("tile") & 1
    fetches = [pltpu.make_async_copy(outer_held, outer, sems.at[0])]
    for c in range(4):
        own = slice(64 * c, 64 * c + 64)
        state = taps.at[pl.ds(384 + 64 * c, 64), pl.ds(256, 1024)]
        fetches.append(pltpu.make_async_copy(inner.at[c, pl.ds(0, 64)], state, sems.at[1 + c]))
        fetches.append(pltpu.make_async_copy(inner.at[c, pl.ds(64, 64)], grads.at[own, pl.ds(128, 1024)], sems.at[5 + c]))
    fetches.append(pltpu.make_async_copy(flipped, weights, sems.at[9]))
    for fetch in fetches:
        fetch.start()
    fetches[0].wait()
    _, lane = grid(64, 128)
    for c in range(4):
        atm = slice(64 * c, 64 * c + 64)
        mid = slice(384 + 64 * c, 448 + 64 * c)
        sea = slice(640 + 32 * c, 672 + 32 * c)
        taps[mid, 0:256] = outer[c, :, 0:256]
        taps[mid, 1280:1536] = outer[c, :, 512:768]
        side_atm[atm, :] = outer[c, :, 1024:1152]
        taps[sea, 0:128] = outer[c, 0:32, 384:512]
        taps[sea, 128:256] = outer[c, 32:64, 384:512]
        taps[sea, 256:768] = outer[c, 0:32, 1152:1664]
        taps[sea, 768:1280] = outer[c, 32:64, 1152:1664]
        taps[sea, 1280:1408] = outer[c, 0:32, 896:1024]
        taps[sea, 1408:1536] = outer[c, 32:64, 896:1024]
        side = dot(outer[c, 0:32, 1024:1152], ocean_side_table(0)) + dot(outer[c, 32:64, 1024:1152], ocean_side_table(1))
        side_atm[256 + 32 * c : 288 + 32 * c, :] = side.astype(BF)
        grads[atm, 0:128] = outer[c, :, 256:384]
        grads[atm, 1152:1280] = outer[c, :, 768:896]
        side = outer[c, :, 1024:1152]
        grads[atm, 1280:1408] = jnp.where((lane >= OG0) & (lane < OC0), side, jnp.zeros_like(side))
    for fetch in fetches[1:9]:
        fetch.wait()
    side = side_atm[...]
    shifts, edges = shift_tables(), edge_rows()
    for r in range(12):
        lanes = slice(128 * r, 128 * r + 128)
        table = jnp.concatenate([shifts, edge_marks(edges, 4 * r + 1)], axis=0)
        moved = dot(jnp.concatenate([taps[384:768, lanes], side], axis=1), table).astype(BF)
        taps[0:384, lanes] = moved[:, 0:128]
        taps[768:1152, lanes] = moved[:, 128:256]
    _, lane = grid(384, 128)
    columns = dot(taps[384:768, :], gather_table()).astype(BF)
    columns = jnp.where(lane < 48, side, columns)
    moved = dot(columns, jnp.concatenate([tap_table(s, t) for s in (-1, 0, 1) for t in (-1, 0, 1)], axis=1)).astype(BF)
    for s in range(3):
        for t in range(3):
            at = 128 * (3 * s + t)
            side_taps[384 * t : 384 * t + 384, 128 * s : 128 * s + 128] = moved[:, at : at + 128]
    bias = jnp.concatenate(
        [jnp.sum(outer[c, :, 1024 + BIAS0 : 1024 + BIAS0 + 3].astype(F32), axis=1, keepdims=True) for c in range(4)], axis=0
    )

    fetches[9].wait()

    def activate(total, lanes):
        pre = total + bias
        gate = 1.0 / (1.0 + jnp.exp(-pre))
        z_all[:, lanes] = (grads[:, lanes].astype(F32) * gate * (1.0 + pre * (1.0 - gate))).astype(BF)
        return pre * gate

    for r in range(0, 10, 2):
        total = jnp.zeros((256, 256), F32)
        for s in range(3):
            total = total + dot(weights[s], taps[:, 128 * (r + s) : 128 * (r + s) + 256])
        silu = activate(total, slice(128 * r, 128 * r + 256))
        for q in (0, 1):
            row = r + q - 1
            if 0 <= row < 8:
                state = taps[384:640, 128 * (row + 2) : 128 * (row + 3)].astype(F32)
                outs[:, 128 * row : 128 * row + 128] = (state + silu[:, 128 * q : 128 * q + 128]).astype(BF)
    total = jnp.zeros((256, 128), F32)
    for s in range(3):
        total = total + dot(weights[s], side_taps[:, 128 * s : 128 * s + 128])
    activate(total, slice(1280, 1408))
    rows = pl.ds(pl.multiple_of(chan * 64, 64), 64)
    output[...] = outs[rows, :]
    own = z_all[rows, 128:1152]
    sums = dot_last(jnp.ones((16, 1024), BF), own)
    for half, first in ((0, mine), (1, theirs)):
        first[54:64] = jnp.zeros((10, 16, 128), F32)
        first[54, :, 0:64] = sums
    lifted[...] = jnp.zeros_like(lifted)
    for s in range(3):
        lifted[64 * s : 64 * s + 64, 128 * (s + 1) : 128 * (s + 1) + 1024] = own
    found = dot_last(lifted[...], taps[...])
    for s in range(3):
        for t in range(3):
            for a in range(4):
                for l in range(3):
                    piece = found[64 * s + 16 * a : 64 * s + 16 * a + 16, 384 * t + 128 * l : 384 * t + 128 * l + 128]
                    row = 4 * (3 * s + t) + a
                    half, at = row // 18, (row % 18) * 3 + l

                    @pl.when(core == half)
                    def _():
                        mine[at] = piece

                    @pl.when(core != half)
                    def _():
                        theirs[at] = piece


def backward_kernel(
    sources, blocks, z_all, weights_held, regrid_weights, grad,
    input_grad, r0, r1, r2, far, taps, delta, terms, weights, sem,
):
    fetch = pltpu.make_async_copy(weights_held, weights, sem)
    fetch.start()
    tile, chan = lax.axis_index("tile"), lax.axis_index("chan")
    facing = 1 - 2 * (tile & 1)
    side = z_all[:, 1280:1408]
    shifts, edges = shift_tables(), edge_rows()
    for r in range(10):
        lanes = slice(128 * r, 128 * r + 128)
        table = jnp.concatenate([shifts, edge_marks(edges, OG0 + 2 * r)], axis=0)
        moved = dot(jnp.concatenate([z_all[:, lanes], side], axis=1), table).astype(BF)
        taps[512:768, lanes] = moved[:, 0:128]
        taps[0:256, lanes] = moved[:, 128:256]
    taps[256:512, :] = z_all[:, 0:1280]
    atm_rows = pl.ds(pl.multiple_of(chan * 64, 64), 64)
    sea_rows = pl.ds(pl.multiple_of(256 + chan * 32, 32), 32)
    fetch.wait()
    for q in range(4):
        atm_total = jnp.zeros((64, 256), F32)
        sea_total = jnp.zeros((32, 256), F32)
        for s in range(3):
            first = 128 * (2 * q + 2 - s)
            for t in range(3):
                window = taps[256 * t : 256 * t + 256, first : first + 256]
                atm_total = atm_total + dot(weights[3 * s + t, atm_rows, :], window)
                sea_total = sea_total + dot(weights[3 * s + t, sea_rows, :], window)
        lanes = slice(256 * q, 256 * q + 256)
        input_grad[:, lanes] = (grad[:, lanes].astype(F32) + atm_total).astype(BF)
        delta[:, lanes] = sea_total.astype(BF)
    for e in range(12):
        block = blocks[0, e]
        lanes = pl.ds(pl.multiple_of(jnp.maximum(block, 0) * LANES, LANES), LANES)
        term = dot_last(delta[:, lanes], regrid_weights[e])
        terms[32 * e : 32 * e + 32, :] = jnp.where(block >= 0, term, 0.0).astype(BF)
    terms[384:480, :] = jnp.zeros((96, 128), BF)

    def parcel(out, at, shift):
        target = (tile + HALF + shift) & (TILES - 1)
        found = jnp.int32(4)
        for k in range(4):
            found = jnp.where(sources[0, k] == target, k, found)
        out[at : at + 96, :] = terms[pl.ds(pl.multiple_of(found * 96, 96), 96), :]

    for step, out in zip(CHIP_STEPS, (r0, r1, r2)):
        parcel(out, 0, 2 * step)
        parcel(out, 96, 2 * step + facing)
    parcel(far, 0, -3 * facing)


def return_kernel(sends, a0, a1, a2, crossed, far, ocean_grad, acc):
    tile = lax.axis_index("tile")
    facing = 1 - 2 * (tile & 1)
    acc[...] = jnp.zeros_like(acc)

    def add(ref, first, shift):
        sender = (tile + HALF + shift) & (TILES - 1)
        for slot in range(3):
            block = sends[slot, sender]

            @pl.when(block >= 0)
            def _():
                into = pl.ds(pl.multiple_of(block * 32, 32), 32)
                acc[into, :] += ref[first + 32 * slot : first + 32 * slot + 32, :].astype(F32)

    for i, (step, ref) in enumerate(zip(CHIP_STEPS, (a0, a1, a2))):
        add(ref, 0, -2 * step)
        add(crossed, 96 * i, -2 * step + facing)
    add(far, 0, -3 * facing)
    for b in range(8):
        ocean_grad[:, LANES * b : LANES * (b + 1)] = acc[32 * b : 32 * (b + 1), :]


def sum_kernel(scale, arrived, out):
    total = (jnp.sum(arrived[...].astype(F32), axis=0) * scale).astype(BF)
    for i in range(64):
        out[i] = total


def finish_kernel(held, crossed, weight_grad, bias_grad):
    core = lax.axis_index("tile") & 1
    for half in range(2):
        for a in range(18):
            row = 18 * half + a
            k, part = row // 4, row % 4
            for l in range(3):
                at = 3 * a + l
                piece = jnp.where(core == half, held[at].astype(F32), crossed[at].astype(F32))
                weight_grad[k, 16 * part : 16 * part + 16, 128 * l : 128 * l + 128] = piece
    bias_grad[...] = held[54].astype(F32)[0:8]


def send(array, target):
    return lax.ppermute(array, "tile", [(i, target(i)) for i in range(TILES)])


def chip_send(array, at):
    return send(array, lambda i: (i + HALF + 2 * CHIP_STEPS[at]) % TILES)


def far_send(array):
    return send(array, lambda i: (i + HALF - 3 * (1 - 2 * (i % 2))) % TILES)


def to_mate(array):
    return send(array, lambda i: i ^ 1)


def on_device(
    atm_state,
    ocean_state,
    conv_weight,
    conv_bias,
    regrid_weight,
    out_grad,
    atm_neighbours,
    coupling_sources,
    coupling_blocks,
    coupling_sends,
):
    sends = coupling_sends[0].T
    flipped = jnp.swapaxes(conv_weight.reshape(3, 1152, 256), 1, 2)
    b0, b1, b2, far = call(parcels_kernel, [((192, 128), BF)] * 3 + [((96, 128), BF)], [SMEM, VMEM])(sends, ocean_state)
    (copies,) = call(copies_kernel, [((4, 128, 1024), BF)], [VMEM, VMEM])(atm_state, out_grad)
    inner = lax.all_to_all(copies, "chan", 0, 0)
    a0, a1, a2, far = chip_send(b0, 0), chip_send(b1, 1), chip_send(b2, 2), far_send(far)
    far, flipped = lax.optimization_barrier((far, flipped))
    table = jnp.pad(atm_neighbours.astype(BF), ((0, 15), (0, 120)))
    crossed = to_mate(jnp.concatenate([a0[96:], a1[96:], a2[96:], table], axis=0))
    mate_near = crossed[288:289, 0:8].astype(jnp.int32)
    regridded, north, south, sides = call(
        regrid_kernel,
        [((32, 1024), BF), ((64, 512), BF), ((64, 512), BF), ((64, 128), BF)],
        [SMEM] * 2 + [VMEM] * 8,
        [pltpu.VMEM((672, 128), BF), pltpu.VMEM((256, 128), F32)],
    )(coupling_sources, coupling_blocks, a0, a1, a2, crossed, far, regrid_weight, atm_state, out_grad)
    from_north = lax.ppermute(south, "tile", [(i, i + 8) for i in range(TILES - 8)])
    from_south = lax.ppermute(north, "tile", [(i + 8, i) for i in range(TILES - 8)])
    strips = jnp.concatenate([from_north, from_south, sides], axis=1)
    strips, inner = lax.optimization_barrier((strips, inner))
    strips = lax.all_gather(strips, "tile", axis_index_groups=ROW_CHIPS)
    own, mate = call(select_kernel, [((64, 1664), BF), ((64, 1152), BF)], [SMEM] * 2 + [VMEM] * 3)(
        atm_neighbours, mate_near, strips, regridded, conv_bias.reshape(1, 64)
    )
    shard = own + jnp.pad(to_mate(mate), ((0, 0), (0, 512)))
    outer = lax.all_gather(shard, "chan")
    atm_output, z_all, mine, theirs = call(
        forward_kernel,
        [((64, 1024), BF), ((256, 1408), BF), ((64, 16, 128), F32), ((64, 16, 128), F32)],
        [HELD] * 3,
        [
            pltpu.VMEM((384, 128), BF),
            pltpu.VMEM((1152, 1536), BF),
            pltpu.VMEM((1152, 384), BF),
            pltpu.VMEM((256, 1408), BF),
            pltpu.VMEM((256, 1024), BF),
            pltpu.VMEM((3, 256, 1152), BF),
            pltpu.VMEM((4, 64, 1664), BF),
            pltpu.VMEM((192, 1536), BF),
            pltpu.SemaphoreType.DMA((10,)),
        ],
        limit=60,
        cost=10,
    )(inner, outer, flipped)
    total = (mine + to_mate(theirs)).astype(BF)
    total, z_all = lax.optimization_barrier((total, z_all))
    shares = lax.all_to_all(total, "tile", 0, 0, axis_index_groups=SAME_CORE)
    input_grad, b0, b1, b2, far = call(
        backward_kernel,
        [((64, 1024), BF)] + [((192, 128), BF)] * 3 + [((96, 128), BF)],
        [SMEM] * 2 + [VMEM, HELD, VMEM, VMEM],
        [
            pltpu.VMEM((768, 1280), BF),
            pltpu.VMEM((32, 1024), BF),
            pltpu.VMEM((480, 128), BF),
            pltpu.VMEM((9, 384, 256), BF),
            pltpu.SemaphoreType.DMA,
        ],
        limit=48,
        cost=4,
    )(coupling_sources, coupling_blocks, z_all, conv_weight, regrid_weight, out_grad)
    a0, a1, a2 = chip_send(b0, 0), chip_send(b1, 1), chip_send(b2, 2)
    shares, a0, a1, a2, far = lax.optimization_barrier((shares, a0, a1, a2, far))
    scale = 1.0 / math.sqrt(atm_state.shape[1] * TILES)
    (summed,) = call(functools.partial(sum_kernel, scale), [((64, 16, 128), BF)], [VMEM])(shares)
    summed, far = lax.optimization_barrier((summed, far))
    held = lax.all_to_all(summed, "tile", 0, 0, axis_index_groups=SAME_CORE)
    far = far_send(far)
    crossed = to_mate(jnp.concatenate([a0[96:], a1[96:], a2[96:]], axis=0))
    (ocean_grad,) = call(return_kernel, [((32, 1024), F32)], [SMEM] + [VMEM] * 5, [pltpu.VMEM((256, 128), F32)])(
        sends, a0, a1, a2, crossed, far
    )
    held, ocean_grad = lax.optimization_barrier((held, ocean_grad))
    crossed = to_mate(held)
    weight_grad, bias_grad = call(finish_kernel, [((9, 64, 384), F32), ((8, 128), F32)], [VMEM, VMEM])(held, crossed)
    return atm_output, input_grad, ocean_grad, jnp.swapaxes(weight_grad, 1, 2), bias_grad[0, 0:64]


def solution(mesh):
    placed = (
        P("chan", "tile"),
        P("chan", "tile"),
        P(),
        P("chan"),
        P("tile", None, None),
        P("chan", "tile"),
        P("tile", None),
        P("tile", None),
        P("tile", None),
        P("tile", None, None),
    )
    return jax.shard_map(
        on_device,
        mesh=mesh,
        in_specs=placed,
        out_specs=(
            P("chan", "tile"),
            P("chan", "tile"),
            P("chan", "tile"),
            P(None, None, "chan"),
            P("chan"),
        ),
        check_vma=False,
    )
```

time: 224 us -> 185 us (0.83)
  blocking collectives: 91.4 us -> 25.7 us
  starting transfers between devices: 67.1 us -> 97.8 us
  local copies, waits for them, and re-layouts: 16.8 us -> 4.34 us
  waiting for transfers between devices: 19.7 us -> 31.1 us
  Pallas kernels: 24.7 us -> 22 us
    all_to_all x2 -> x0, blocking collectives: 58.9 us -> none  [the longest x1 33.9 us: on_device(): lax.all_to_all((mine + theirs).astype(BF), 'tile', 0, 0, axis_index_group...]
    all_to_all x0 -> x2, starting transfers between devices: none -> 22.7 us  [the longest x1 12.9 us: on_device(): held = lax.all_to_all(summed, 'tile', 0, 0, axis_index_groups=SAME_CORE)]
    unnamed x61 -> x21, local copies, waits for them, and re-layouts: 12.7 us -> 1.57 us
    ppermute x13, starting transfers between devices: 59.9 us -> 66.9 us  [send(): return lax.ppermute(array, 'tile', [(i, target(i)) for i in range(TILES)])]
    all_gather x1, blocking collectives: 19.4 us -> 12.6 us  [on_device(): strips = lax.all_gather(strips, 'tile', axis_index_groups=ROW_CHIPS)]
    ppermute x1, waiting for transfers between devices: 7.98 us -> 14 us  [on_device(): lax.ppermute(north, 'tile', [(i + 8, i) for i in range(TILES - 8)])]
    ppermute x13, waiting for transfers between devices: 11.8 us -> 17.1 us  [send(): return lax.ppermute(array, 'tile', [(i, target(i)) for i in range(TILES)])]
    pallas_call x5, Pallas kernels: 7.58 us -> 5.24 us  [the longest x1 1.45 us: on_device(): call(return_kernel, [((32, 1024), F32)], [SMEM] + [VMEM] * 5, [pltpu.VMEM...]
  transfers between devices with their start and end apart: 16 -> 18, of which waited for: 6 -> 8; matrix products, arithmetic and copies ran while one was open for 2% -> 1% of each run, Pallas kernels for 5% -> 5%
where the time goes in v2:
time: 185 us; the launch traced here: 184 us
  starting transfers between devices  97.8 us (53%)
  waiting for transfers between devices  31.1 us (17%)
  blocking collectives  25.7 us (14%)
  Pallas kernels  22 us (12%)
  local copies, waits for them, and re-layouts  4.34 us (2%)
  other arithmetic  1.87 us (1%)
    ppermute x13, starting transfers between devices, send(): return lax.ppermute(array, 'tile', [(i, target(i)) for i in range(TILES)])  66.9 us
    ppermute x13, waiting for transfers between devices, send(): return lax.ppermute(array, 'tile', [(i, target(i)) for i in range(TILES)])  17.1 us
    ppermute x1, waiting for transfers between devices, on_device(): lax.ppermute(north, 'tile', [(i + 8, i) for i in range(TILES - 8)])  14 us
    all_gather x1, blocking collectives, on_device(): outer = lax.all_gather(shard, 'chan')  13.2 us
    all_to_all x1, starting transfers between devices, on_device(): held = lax.all_to_all(summed, 'tile', 0, 0, axis_index_groups=SAME_CORE)  12.9 us
    all_gather x1, blocking collectives, on_device(): strips = lax.all_gather(strips, 'tile', axis_index_groups=ROW_CHIPS)  12.6 us
    all_to_all x1, starting transfers between devices, on_device(): shares = lax.all_to_all(total, 'tile', 0, 0, axis_index_groups=SAME_CORE)  9.84 us
    pallas_call x1, Pallas kernels, on_device(): call(forward_kernel, [((64, 1024), BF), ((256, 1408), BF), ((64, 16, 128)...  9.71 us
  transfers between devices with their start and end apart: 18, of which 8 were waited for; matrix products, arithmetic and copies ran while one was open for 1% of the time, Pallas kernels for 5%

profile of v2, /device:TPU:1, one launch (start us, length us, event | category | flops | bytes accessed | tf_op | source)
XLA Modules:
  0.0 183.9 jit_solution(17225416633323278947)
XLA Ops:
  2.8 12.9 %collective-permute-start = (bf16[192,128]{1,0:T(8,128)(2,1)S(1)}, bf16[192,128]{1,0:T(8,128)(2,1)S(1)}, u32[]{:S(2)}, u32[]{:S(2)}) collective-permute-start(bf16[192,128]{1,0:T(8,128)(2,1)S(1)} %get-tuple-element.41), channel_id=1, source_target_pairs={{0,248},{4,252},{8,256},{12,260},{16,264},{20,268},{24,272},{28,27... | collective-permute-start | bytes 147464 | tf_op jit(solution)/shard_map/ppermute | solution.py:441
  15.7 4.4 %collective-permute-start.1 = (bf16[192,128]{1,0:T(8,128)(2,1)S(1)}, bf16[192,128]{1,0:T(8,128)(2,1)S(1)}, u32[]{:S(2)}, u32[]{:S(2)}) collective-permute-start(bf16[192,128]{1,0:T(8,128)(2,1)S(1)} %get-tuple-element.42), channel_id=1, source_target_pairs={{0,256},{4,260},{8,264},{12,268},{16,272},{20,276},{24,280},{28,28... | collective-permute-start | bytes 147464 | tf_op jit(solution)/shard_map/ppermute | solution.py:441
  20.1 1.9 %collective-permute-start.2 = (bf16[192,128]{1,0:T(8,128)(2,1)S(1)}, bf16[192,128]{1,0:T(8,128)(2,1)S(1)}, u32[]{:S(2)}, u32[]{:S(2)}) collective-permute-start(bf16[192,128]{1,0:T(8,128)(2,1)S(1)} %get-tuple-element.43), channel_id=1, source_target_pairs={{0,264},{4,268},{8,272},{12,276},{16,280},{20,284},{24,288},{28,29... | collective-permute-start | bytes 147464 | tf_op jit(solution)/shard_map/ppermute | solution.py:441
  23.1 4.4 %all-to-all-start = ((bf16[4,128,1024]{2,1,0:T(8,128)(2,1)}), bf16[4,128,1024]{2,1,0:T(8,128)(2,1)}, u32[]{:S(2)}, u32[]{:S(2)}) async-start(bf16[4,128,1024]{2,1,0:T(8,128)(2,1)} %shard_map.139), calls=%async_computation | async-start | bytes 2097152 | tf_op jit(solution)/shard_map/all_to_all | solution.py:472
  27.6 3.7 %collective-permute-start.3 = (bf16[304,128]{1,0:T(8,128)(2,1)S(1)}, bf16[304,128]{1,0:T(8,128)(2,1)S(1)}, u32[]{:S(2)}, u32[]{:S(2)}) collective-permute-start(bf16[304,128]{1,0:T(8,128)(2,1)S(1)} %fusion.1), channel_id=1, source_target_pairs={{0,4},{4,0},{8,12},{12,8},{16,20},{20,16},{24,28},{28,24},{32,36},... | collective-permute-start | bytes 233480 | tf_op jit(solution)/shard_map/ppermute | solution.py:441
  31.3 1.9 %collective-permute-start.4 = (bf16[96,128]{1,0:T(8,128)(2,1)S(1)}, bf16[96,128]{1,0:T(8,128)(2,1)S(1)}, u32[]{:S(2)}, u32[]{:S(2)}) collective-permute-start(bf16[96,128]{1,0:T(8,128)(2,1)S(1)} %get-tuple-element.44), channel_id=1, source_target_pairs={{0,244},{4,272},{8,252},{12,280},{16,260},{20,288},{24,268},{28,29... | collective-permute-start | bytes 73736 | tf_op jit(solution)/shard_map/ppermute | solution.py:441
  33.3 2.2 %copy.15 = bf16[3,1152,256]{1,2,0:T(8,128)(2,1)} copy(bf16[3,1152,256]{2,1,0:T(8,128)(2,1)S(1)} %bitcast.13) | data formatting | bytes 3538944 | tf_op jit(solution)/shard_map/reshape | solution.py:469
  35.6 4.2 %collective-permute-done.4.far = bf16[96,128]{1,0:T(8,128)(2,1)S(1)} collective-permute-done((bf16[96,128]{1,0:T(8,128)(2,1)S(1)}, bf16[96,128]{1,0:T(8,128)(2,1)S(1)}, u32[]{:S(2)}, u32[]{:S(2)}) %collective-permute-start.4) | collective-permute-done | bytes 24608 | tf_op jit(solution)/shard_map/ppermute | solution.py:441
  39.8 2.4 %shard_map.138 = (bf16[32,1024]{1,0:T(8,128)(2,1)S(1)}, bf16[64,512]{1,0:T(8,128)(2,1)S(1)}, bf16[64,512]{1,0:T(8,128)(2,1)S(1)}, bf16[64,128]{1,0:T(8,128)(2,1)S(1)}) custom-call(s32[1,4]{1,0:T(1,128)S(1)} %copy-done.7, s32[1,12]{1,0:T(1,128)S(1)} %copy-done.8, bf16[192,128]{1,0:T(8,128)(2,1)S(1)} %collective-permute-done.a0, ...), custom_call_target="tpu_custom_call" | custom-call | flops 1000000000 | bytes 3000000 | tf_op jit(solution)/shard_map/pallas_call | solution.py:478
  42.3 2.5 %collective-permute-start.5 = (bf16[64,512]{1,0:T(8,128)(2,1)S(1)}, bf16[64,512]{1,0:T(8,128)(2,1)S(1)}, u32[]{:S(2)}, u32[]{:S(2)}) collective-permute-start(bf16[64,512]{1,0:T(8,128)(2,1)S(1)} %get-tuple-element.46), channel_id=1, source_target_pairs={{0,32},{4,36},{8,40},{12,44},{16,48},{20,52},{24,56},{28,60},{32,6... | collective-permute-start | bytes 196616 | tf_op jit(solution)/shard_map/ppermute | solution.py:484
  44.7 1.3 collective-permute-start.6
  46.1 14.0 %collective-permute-done.6 = bf16[64,512]{1,0:T(8,128)(2,1)S(1)} collective-permute-done((bf16[64,512]{1,0:T(8,128)(2,1)S(1)}, bf16[64,512]{1,0:T(8,128)(2,1)S(1)}, u32[]{:S(2)}, u32[]{:S(2)}) %collective-permute-start.6) | collective-permute-done | bytes 65568 | tf_op jit(solution)/shard_map/ppermute | solution.py:485
  60.0 12.6 %all-gather = bf16[256,1152]{1,0:T(8,128)(2,1)S(1)} all-gather(bf16[64,1152]{1,0:T(8,128)(2,1)S(1)} %pad_maximum_fusion), channel_id=2, replica_groups={{0,8,16,24},{4,12,20,28},{32,40,48,56},{36,44,52,60},{64,72,80,88},{68,..., dimensions={0}, use_global_device_ids=true | all-gather | bytes 737280 | tf_op jit(solution)/shard_map/all_gather | solution.py:488
  73.6 6.8 %collective-permute-start.7 = (bf16[64,1152]{1,0:T(8,128)(2,1)S(1)}, bf16[64,1152]{1,0:T(8,128)(2,1)S(1)}, u32[]{:S(2)}, u32[]{:S(2)}) collective-permute-start(bf16[64,1152]{1,0:T(8,128)(2,1)S(1)} %get-tuple-element.53), channel_id=1, source_target_pairs={{0,4},{4,0},{8,12},{12,8},{16,20},{20,16},{24,28},{28,24},{32,36},... | collective-permute-start | bytes 442376 | tf_op jit(solution)/shard_map/ppermute | solution.py:441
  81.5 13.2 %all-gather.1 = bf16[256,1664]{1,0:T(8,128)(2,1)} all-gather(bf16[64,1664]{1,0:T(8,128)(2,1)S(1)} %pad_add_fusion), channel_id=3, replica_groups=mesh['tile'=128,'chan'=4] {'chan'}, dimensions={0}, use_global_device_ids=true | all-gather | bytes 1064960 | tf_op jit(solution)/shard_map/all_gather | solution.py:493
  94.7 9.7 %shard_map.141 = (bf16[64,1024]{1,0:T(8,128)(2,1)}, bf16[256,1408]{1,0:T(8,128)(2,1)}, f32[64,16,128]{2,1,0:T(8,128)}, f32[64,16,128]{2,1,0:T(8,128)}) custom-call(bf16[4,128,1024]{2,1,0:T(8,128)(2,1)} %all-to-all-done.inner, bf16[4,64,1664]{2,1,0:T(8,128)(2,1)} %bitcast.19, bf16[3,256,1152]{2,1,0:T(8,128)(2,1)} %bitcast.18), custom_call_target="tpu_custom_call" | custom-call | flops 10000000000 | bytes 30000000 | tf_op jit(solution)/shard_map/pallas_call | solution.py:494
  104.4 4.6 %collective-permute-start.8 = (f32[64,16,128]{2,1,0:T(8,128)}, f32[64,16,128]{2,1,0:T(8,128)S(1)}, u32[]{:S(2)}, u32[]{:S(2)}) collective-permute-start(f32[64,16,128]{2,1,0:T(8,128)} %get-tuple-element.57), channel_id=1, source_target_pairs={{0,4},{4,0},{8,12},{12,8},{16,20},{20,16},{24,28},{28,24},{32,36},... | collective-permute-start | bytes 1572872 | tf_op jit(solution)/shard_map/ppermute | solution.py:441
  109.0 1.7 collective-permute-done.8
  110.7 1.8 add_convert_fusion
  112.5 9.8 %all-to-all-start.1 = ((bf16[64,16,128]{2,1,0:T(8,128)(2,1)}), bf16[64,16,128]{2,1,0:T(8,128)(2,1)S(1)}, u32[]{:S(2)}, u32[]{:S(2)}) async-start(bf16[64,16,128]{2,1,0:T(8,128)(2,1)} %add_convert_fusion), calls=%async_computation.1 | async-start | bytes 524288 | tf_op jit(solution)/shard_map/all_to_all | solution.py:514
  122.3 3.9 %shard_map.142 = (bf16[64,1024]{1,0:T(8,128)(2,1)}, bf16[192,128]{1,0:T(8,128)(2,1)S(1)}, bf16[192,128]{1,0:T(8,128)(2,1)S(1)}, bf16[192,128]{1,0:T(8,128)(2,1)S(1)}, bf16[96,128]{1,0:T(8,128)(2,1)S(1)}) custom-call(s32[1,4]{1,0:T(1,128)S(1)} %copy-done.7, s32[1,12]{1,0:T(1,128)S(1)} %copy-done.8, bf16[256,1408]{1,0:T(8,128)(2,1)S(1)} %copy-done.9, ...), custom_call_target="tpu_custom_call" | custom-call | flops 4000000000 | bytes 12000000 | tf_op jit(solution)/shard_map/pallas_call | solution.py:515
  126.2 5.1 %collective-permute-start.9 = (bf16[192,128]{1,0:T(8,128)(2,1)S(1)}, bf16[192,128]{1,0:T(8,128)(2,1)S(1)}, u32[]{:S(2)}, u32[]{:S(2)}) collective-permute-start(bf16[192,128]{1,0:T(8,128)(2,1)S(1)} %get-tuple-element.62), channel_id=1, source_target_pairs={{0,248},{4,252},{8,256},{12,260},{16,264},{20,268},{24,272},{28,27... | collective-permute-start | bytes 147464 | tf_op jit(solution)/shard_map/ppermute | solution.py:441
  131.3 4.5 %collective-permute-start.10 = (bf16[192,128]{1,0:T(8,128)(2,1)S(1)}, bf16[192,128]{1,0:T(8,128)(2,1)S(1)}, u32[]{:S(2)}, u32[]{:S(2)}) collective-permute-start(bf16[192,128]{1,0:T(8,128)(2,1)S(1)} %get-tuple-element.63), channel_id=1, source_target_pairs={{0,256},{4,260},{8,264},{12,268},{16,272},{20,276},{24,280},{28,28... | collective-permute-start | bytes 147464 | tf_op jit(solution)/shard_map/ppermute | solution.py:441
  135.9 2.6 %collective-permute-start.11 = (bf16[192,128]{1,0:T(8,128)(2,1)S(1)}, bf16[192,128]{1,0:T(8,128)(2,1)S(1)}, u32[]{:S(2)}, u32[]{:S(2)}) collective-permute-start(bf16[192,128]{1,0:T(8,128)(2,1)S(1)} %get-tuple-element.64), channel_id=1, source_target_pairs={{0,264},{4,268},{8,272},{12,276},{16,280},{20,284},{24,288},{28,29... | collective-permute-start | bytes 147464 | tf_op jit(solution)/shard_map/ppermute | solution.py:441
  138.9 4.3 %collective-permute-done.11.a2 = bf16[192,128]{1,0:T(8,128)(2,1)S(1)} collective-permute-done((bf16[192,128]{1,0:T(8,128)(2,1)S(1)}, bf16[192,128]{1,0:T(8,128)(2,1)S(1)}, u32[]{:S(2)}, u32[]{:S(2)}) %collective-permute-start.11) | collective-permute-done | bytes 49184 | tf_op jit(solution)/shard_map/ppermute | solution.py:441
  143.9 12.9 %all-to-all-start.2 = ((bf16[64,16,128]{2,1,0:T(8,128)(2,1)}), bf16[64,16,128]{2,1,0:T(8,128)(2,1)S(1)}, u32[]{:S(2)}, u32[]{:S(2)}) async-start(bf16[64,16,128]{2,1,0:T(8,128)(2,1)} %shard_map.143), calls=%async_computation.2 | async-start | bytes 524288 | tf_op jit(solution)/shard_map/all_to_all | solution.py:534
  156.9 4.8 %collective-permute-start.12 = (bf16[288,128]{1,0:T(8,128)(2,1)S(1)}, bf16[288,128]{1,0:T(8,128)(2,1)S(1)}, u32[]{:S(2)}, u32[]{:S(2)}) collective-permute-start(bf16[288,128]{1,0:T(8,128)(2,1)S(1)} %pad_maximum_fusion.1), channel_id=1, source_target_pairs={{0,4},{4,0},{8,12},{12,8},{16,20},{20,16},{24,28},{28,24},{32,36},... | collective-permute-start | bytes 221192 | tf_op jit(solution)/shard_map/ppermute | solution.py:441
  161.7 6.5 %collective-permute-start.13 = (bf16[96,128]{1,0:T(8,128)(2,1)S(1)}, bf16[96,128]{1,0:T(8,128)(2,1)S(1)}, u32[]{:S(2)}, u32[]{:S(2)}) collective-permute-start(bf16[96,128]{1,0:T(8,128)(2,1)S(1)} %get-tuple-element.72), channel_id=1, source_target_pairs={{0,244},{4,272},{8,252},{12,280},{16,260},{20,288},{24,268},{28,29... | collective-permute-start | bytes 73736 | tf_op jit(solution)/shard_map/ppermute | solution.py:441
  168.2 4.3 %collective-permute-done.13.far = bf16[96,128]{1,0:T(8,128)(2,1)S(1)} collective-permute-done((bf16[96,128]{1,0:T(8,128)(2,1)S(1)}, bf16[96,128]{1,0:T(8,128)(2,1)S(1)}, u32[]{:S(2)}, u32[]{:S(2)}) %collective-permute-start.13) | collective-permute-done | bytes 24608 | tf_op jit(solution)/shard_map/ppermute | solution.py:441
  172.5 1.4 shard_map.144
  174.0 7.2 %collective-permute-start.14 = (bf16[64,16,128]{2,1,0:T(8,128)(2,1)S(1)}, bf16[64,16,128]{2,1,0:T(8,128)(2,1)S(1)}, u32[]{:S(2)}, u32[]{:S(2)}) collective-permute-start(bf16[64,16,128]{2,1,0:T(8,128)(2,1)S(1)} %all-to-all-done.2.held), channel_id=1, source_target_pairs={{0,4},{4,0},{8,12},{12,8},{16,20},{20,16},{24,28},{28,24},{32,36},... | collective-permute-start | bytes 786440 | tf_op jit(solution)/shard_map/ppermute | solution.py:441
  181.2 1.1 collective-permute-done.14.crossed
  (51 shorter events, 8.2 us)
Async XLA Ops:
  1.3 0.8 copy-start.4
  2.2 19.9 %copy-start.2 = (bf16[64,1024]{1,0:T(8,128)(2,1)S(1)}, bf16[64,1024]{1,0:T(8,128)(2,1)}, u32[]{:S(2)}) copy-start(bf16[64,1024]{1,0:T(8,128)(2,1)} %atm.3) | copy-start | bytes 393220
  2.2 19.9 %copy-start.3 = (bf16[64,1024]{1,0:T(8,128)(2,1)S(1)}, bf16[64,1024]{1,0:T(8,128)(2,1)}, u32[]{:S(2)}) copy-start(bf16[64,1024]{1,0:T(8,128)(2,1)} %grad.5) | copy-start | bytes 393220
  2.8 24.7 %collective-permute-start = (bf16[192,128]{1,0:T(8,128)(2,1)S(1)}, bf16[192,128]{1,0:T(8,128)(2,1)S(1)}, u32[]{:S(2)}, u32[]{:S(2)}) collective-permute-start(bf16[192,128]{1,0:T(8,128)(2,1)S(1)} %get-tuple-element.41), channel_id=1, source_target_pairs={{0,248},{4,252},{8,256},{12,260},{16,264},{20,268},{24,272},{28,27... | collective-permute-start | bytes 147464 | tf_op jit(solution)/shard_map/ppermute | solution.py:441
  15.7 11.8 %collective-permute-start.1 = (bf16[192,128]{1,0:T(8,128)(2,1)S(1)}, bf16[192,128]{1,0:T(8,128)(2,1)S(1)}, u32[]{:S(2)}, u32[]{:S(2)}) collective-permute-start(bf16[192,128]{1,0:T(8,128)(2,1)S(1)} %get-tuple-element.42), channel_id=1, source_target_pairs={{0,256},{4,260},{8,264},{12,268},{16,272},{20,276},{24,280},{28,28... | collective-permute-start | bytes 147464 | tf_op jit(solution)/shard_map/ppermute | solution.py:441
  20.1 7.5 %collective-permute-start.2 = (bf16[192,128]{1,0:T(8,128)(2,1)S(1)}, bf16[192,128]{1,0:T(8,128)(2,1)S(1)}, u32[]{:S(2)}, u32[]{:S(2)}) collective-permute-start(bf16[192,128]{1,0:T(8,128)(2,1)S(1)} %get-tuple-element.43), channel_id=1, source_target_pairs={{0,264},{4,268},{8,272},{12,276},{16,280},{20,284},{24,288},{28,29... | collective-permute-start | bytes 147464 | tf_op jit(solution)/shard_map/ppermute | solution.py:441
  23.1 4.4 %copy-start.5 = (s32[1,8]{1,0:T(1,128)S(1)}, s32[1,8]{1,0:T(1,128)}, u32[]{:S(2)}) copy-start(s32[1,8]{1,0:T(1,128)} %own_near.1) | copy-start | bytes 100
  23.1 10.2 %copy-start = (bf16[9,384,256]{2,1,0:T(8,128)(2,1)S(1)}, bf16[9,384,256]{2,1,0:T(8,128)(2,1)}, u32[]{:S(2)}) copy-start(bf16[9,384,256]{2,1,0:T(8,128)(2,1)} %weights_held.1) | copy-start | bytes 5308420
  23.1 36.9 %all-to-all-start = ((bf16[4,128,1024]{2,1,0:T(8,128)(2,1)}), bf16[4,128,1024]{2,1,0:T(8,128)(2,1)}, u32[]{:S(2)}, u32[]{:S(2)}) async-start(bf16[4,128,1024]{2,1,0:T(8,128)(2,1)} %shard_map.139), calls=%async_computation | async-start | bytes 2097152 | tf_op jit(solution)/shard_map/all_to_all | solution.py:472
  27.6 12.2 %collective-permute-start.3 = (bf16[304,128]{1,0:T(8,128)(2,1)S(1)}, bf16[304,128]{1,0:T(8,128)(2,1)S(1)}, u32[]{:S(2)}, u32[]{:S(2)}) collective-permute-start(bf16[304,128]{1,0:T(8,128)(2,1)S(1)} %fusion.1), channel_id=1, source_target_pairs={{0,4},{4,0},{8,12},{12,8},{16,20},{20,16},{24,28},{28,24},{32,36},... | collective-permute-start | bytes 233480 | tf_op jit(solution)/shard_map/ppermute | solution.py:441
  31.3 8.5 %collective-permute-start.4 = (bf16[96,128]{1,0:T(8,128)(2,1)S(1)}, bf16[96,128]{1,0:T(8,128)(2,1)S(1)}, u32[]{:S(2)}, u32[]{:S(2)}) collective-permute-start(bf16[96,128]{1,0:T(8,128)(2,1)S(1)} %get-tuple-element.44), channel_id=1, source_target_pairs={{0,244},{4,272},{8,252},{12,280},{16,260},{20,288},{24,268},{28,29... | collective-permute-start | bytes 73736 | tf_op jit(solution)/shard_map/ppermute | solution.py:441
  33.3 6.5 %copy-start.1 = (bf16[12,128,128]{2,1,0:T(8,128)(2,1)S(1)}, bf16[12,128,128]{2,1,0:T(8,128)(2,1)}, u32[]{:S(2)}) copy-start(bf16[12,128,128]{2,1,0:T(8,128)(2,1)} %regrid_weights.1) | copy-start | bytes 1179652
  33.3 6.5 %copy-start.7 = (s32[1,4]{1,0:T(1,128)S(1)}, s32[1,4]{1,0:T(1,128)}, u32[]{:S(2)}) copy-start(s32[1,4]{1,0:T(1,128)} %sources.3) | copy-start | bytes 52
  33.3 6.5 %copy-start.8 = (s32[1,12]{1,0:T(1,128)S(1)}, s32[1,12]{1,0:T(1,128)}, u32[]{:S(2)}) copy-start(s32[1,12]{1,0:T(1,128)} %blocks.3) | copy-start | bytes 148
  39.8 32.8 %copy-start.6 = (f32[64]{0:T(128)S(1)}, f32[64]{0:T(128)}, u32[]{:S(2)}) copy-start(f32[64]{0:T(128)} %param.13) | copy-start | bytes 772
  42.3 3.8 %collective-permute-start.5 = (bf16[64,512]{1,0:T(8,128)(2,1)S(1)}, bf16[64,512]{1,0:T(8,128)(2,1)S(1)}, u32[]{:S(2)}, u32[]{:S(2)}) collective-permute-start(bf16[64,512]{1,0:T(8,128)(2,1)S(1)} %get-tuple-element.46), channel_id=1, source_target_pairs={{0,32},{4,36},{8,40},{12,44},{16,48},{20,52},{24,56},{28,60},{32,6... | collective-permute-start | bytes 196616 | tf_op jit(solution)/shard_map/ppermute | solution.py:484
  44.7 15.3 %collective-permute-start.6 = (bf16[64,512]{1,0:T(8,128)(2,1)S(1)}, bf16[64,512]{1,0:T(8,128)(2,1)S(1)}, u32[]{:S(2)}, u32[]{:S(2)}) collective-permute-start(bf16[64,512]{1,0:T(8,128)(2,1)S(1)} %get-tuple-element.47), channel_id=1, source_target_pairs={{32,0},{36,4},{40,8},{44,12},{48,16},{52,20},{56,24},{60,28},{64,3... | collective-permute-start | bytes 196616 | tf_op jit(solution)/shard_map/ppermute | solution.py:485
  73.6 7.8 %collective-permute-start.7 = (bf16[64,1152]{1,0:T(8,128)(2,1)S(1)}, bf16[64,1152]{1,0:T(8,128)(2,1)S(1)}, u32[]{:S(2)}, u32[]{:S(2)}) collective-permute-start(bf16[64,1152]{1,0:T(8,128)(2,1)S(1)} %get-tuple-element.53), channel_id=1, source_target_pairs={{0,4},{4,0},{8,12},{12,8},{16,20},{20,16},{24,28},{28,24},{32,36},... | collective-permute-start | bytes 442376 | tf_op jit(solution)/shard_map/ppermute | solution.py:441
  104.4 17.9 %copy-start.9 = (bf16[256,1408]{1,0:T(8,128)(2,1)S(1)}, bf16[256,1408]{1,0:T(8,128)(2,1)}, u32[]{:S(2)}) copy-start(bf16[256,1408]{1,0:T(8,128)(2,1)} %get-tuple-element.59.z_all) | copy-start | bytes 2162692
  104.4 6.3 %collective-permute-start.8 = (f32[64,16,128]{2,1,0:T(8,128)}, f32[64,16,128]{2,1,0:T(8,128)S(1)}, u32[]{:S(2)}, u32[]{:S(2)}) collective-permute-start(f32[64,16,128]{2,1,0:T(8,128)} %get-tuple-element.57), channel_id=1, source_target_pairs={{0,4},{4,0},{8,12},{12,8},{16,20},{20,16},{24,28},{28,24},{32,36},... | collective-permute-start | bytes 1572872 | tf_op jit(solution)/shard_map/ppermute | solution.py:441
  112.5 30.7 %all-to-all-start.1 = ((bf16[64,16,128]{2,1,0:T(8,128)(2,1)}), bf16[64,16,128]{2,1,0:T(8,128)(2,1)S(1)}, u32[]{:S(2)}, u32[]{:S(2)}) async-start(bf16[64,16,128]{2,1,0:T(8,128)(2,1)} %add_convert_fusion), calls=%async_computation.1 | async-start | bytes 524288 | tf_op jit(solution)/shard_map/all_to_all | solution.py:514
  126.2 12.2 %collective-permute-start.9 = (bf16[192,128]{1,0:T(8,128)(2,1)S(1)}, bf16[192,128]{1,0:T(8,128)(2,1)S(1)}, u32[]{:S(2)}, u32[]{:S(2)}) collective-permute-start(bf16[192,128]{1,0:T(8,128)(2,1)S(1)} %get-tuple-element.62), channel_id=1, source_target_pairs={{0,248},{4,252},{8,256},{12,260},{16,264},{20,268},{24,272},{28,27... | collective-permute-start | bytes 147464 | tf_op jit(solution)/shard_map/ppermute | solution.py:441
  131.3 7.6 %collective-permute-start.10 = (bf16[192,128]{1,0:T(8,128)(2,1)S(1)}, bf16[192,128]{1,0:T(8,128)(2,1)S(1)}, u32[]{:S(2)}, u32[]{:S(2)}) collective-permute-start(bf16[192,128]{1,0:T(8,128)(2,1)S(1)} %get-tuple-element.63), channel_id=1, source_target_pairs={{0,256},{4,260},{8,264},{12,268},{16,272},{20,276},{24,280},{28,28... | collective-permute-start | bytes 147464 | tf_op jit(solution)/shard_map/ppermute | solution.py:441
  135.9 7.3 %collective-permute-start.11 = (bf16[192,128]{1,0:T(8,128)(2,1)S(1)}, bf16[192,128]{1,0:T(8,128)(2,1)S(1)}, u32[]{:S(2)}, u32[]{:S(2)}) collective-permute-start(bf16[192,128]{1,0:T(8,128)(2,1)S(1)} %get-tuple-element.64), channel_id=1, source_target_pairs={{0,264},{4,268},{8,272},{12,276},{16,280},{20,284},{24,288},{28,29... | collective-permute-start | bytes 147464 | tf_op jit(solution)/shard_map/ppermute | solution.py:441
  143.9 30.0 %all-to-all-start.2 = ((bf16[64,16,128]{2,1,0:T(8,128)(2,1)}), bf16[64,16,128]{2,1,0:T(8,128)(2,1)S(1)}, u32[]{:S(2)}, u32[]{:S(2)}) async-start(bf16[64,16,128]{2,1,0:T(8,128)(2,1)} %shard_map.143), calls=%async_computation.2 | async-start | bytes 524288 | tf_op jit(solution)/shard_map/all_to_all | solution.py:534
  156.9 15.7 %collective-permute-start.12 = (bf16[288,128]{1,0:T(8,128)(2,1)S(1)}, bf16[288,128]{1,0:T(8,128)(2,1)S(1)}, u32[]{:S(2)}, u32[]{:S(2)}) collective-permute-start(bf16[288,128]{1,0:T(8,128)(2,1)S(1)} %pad_maximum_fusion.1), channel_id=1, source_target_pairs={{0,4},{4,0},{8,12},{12,8},{16,20},{20,16},{24,28},{28,24},{32,36},... | collective-permute-start | bytes 221192 | tf_op jit(solution)/shard_map/ppermute | solution.py:441
  161.7 10.8 %collective-permute-start.13 = (bf16[96,128]{1,0:T(8,128)(2,1)S(1)}, bf16[96,128]{1,0:T(8,128)(2,1)S(1)}, u32[]{:S(2)}, u32[]{:S(2)}) collective-permute-start(bf16[96,128]{1,0:T(8,128)(2,1)S(1)} %get-tuple-element.72), channel_id=1, source_target_pairs={{0,244},{4,272},{8,252},{12,280},{16,260},{20,288},{24,268},{28,29... | collective-permute-start | bytes 73736 | tf_op jit(solution)/shard_map/ppermute | solution.py:441
  174.0 8.3 %collective-permute-start.14 = (bf16[64,16,128]{2,1,0:T(8,128)(2,1)S(1)}, bf16[64,16,128]{2,1,0:T(8,128)(2,1)S(1)}, u32[]{:S(2)}, u32[]{:S(2)}) collective-permute-start(bf16[64,16,128]{2,1,0:T(8,128)(2,1)S(1)} %all-to-all-done.2.held), channel_id=1, source_target_pairs={{0,4},{4,0},{8,12},{12,8},{16,20},{20,16},{24,28},{28,24},{32,36},... | collective-permute-start | bytes 786440 | tf_op jit(solution)/shard_map/ppermute | solution.py:441

commit v3 on v2

--- a/solution.py
+++ b/solution.py
@@ -133,13 +133,12 @@
     def parcel(out, at, shift):
         target = (tile + HALF + shift) & (TILES - 1)
         for slot in range(3):
-            block = sends[slot, target]
+            block = sends[slot, 0, target]
             start = pl.multiple_of(jnp.maximum(block, 0) * LANES, LANES)
             data = ocean[:, pl.ds(start, LANES)]
-            rows = pl.ds(at + 32 * slot, 32)
-            out[rows, :] = jnp.where(block >= 0, data, jnp.zeros_like(data))
-
-    for step, out in zip(CHIP_STEPS, outs[:3]):
+            out[at + 32 * slot : at + 32 * slot + 32, :] = jnp.where(block >= 0, data, jnp.zeros_like(data))
+
+    for step, out in zip(CHIP_STEPS, outs):
         parcel(out, 0, 2 * step)
         parcel(out, 96, 2 * step + facing)
     parcel(outs[3], 0, -3 * facing)
@@ -155,7 +154,7 @@
     tile = lax.axis_index("tile")
     facing = 1 - 2 * (tile & 1)
     for i, ref in enumerate((a0, a1, a2)):
-        held[pl.ds(96 * i, 96), :] = ref[0:96, :]
+        held[96 * i : 96 * i + 96, :] = ref[0:96, :]
     held[288:576, :] = crossed[0:288, :]
     held[576:672, :] = far[...]
     acc[...] = jnp.zeros_like(acc)
@@ -320,8 +319,8 @@
     own = z_all[rows, 128:1152]
     sums = dot_last(jnp.ones((16, 1024), BF), own)
     for half, first in ((0, mine), (1, theirs)):
-        first[54:64] = jnp.zeros((10, 16, 128), F32)
-        first[54, :, 0:64] = sums
+        first[54:64] = jnp.zeros((10, 16, 128), first.dtype)
+        first[54, :, 0:64] = sums.astype(first.dtype)
     lifted[...] = jnp.zeros_like(lifted)
     for s in range(3):
         lifted[64 * s : 64 * s + 64, 128 * (s + 1) : 128 * (s + 1) + 1024] = own
@@ -340,7 +339,7 @@
 
                     @pl.when(core != half)
                     def _():
-                        theirs[at] = piece
+                        theirs[at] = piece.astype(BF)
 
 
 def backward_kernel(
@@ -403,7 +402,7 @@
     def add(ref, first, shift):
         sender = (tile + HALF + shift) & (TILES - 1)
         for slot in range(3):
-            block = sends[slot, sender]
+            block = sends[slot, 0, sender]
 
             @pl.when(block >= 0)
             def _():
@@ -418,13 +417,17 @@
         ocean_grad[:, LANES * b : LANES * (b + 1)] = acc[32 * b : 32 * (b + 1), :]
 
 
+def add_kernel(mine, crossed, total):
+    total[...] = (mine[...] + crossed[...].astype(F32)).astype(BF)
+
+
 def sum_kernel(scale, arrived, out):
     total = (jnp.sum(arrived[...].astype(F32), axis=0) * scale).astype(BF)
     for i in range(64):
         out[i] = total
 
 
-def finish_kernel(held, crossed, weight_grad, bias_grad):
+def finish_kernel(held, crossed, weight_grad):
     core = lax.axis_index("tile") & 1
     for half in range(2):
         for a in range(18):
@@ -434,7 +437,6 @@
                 at = 3 * a + l
                 piece = jnp.where(core == half, held[at].astype(F32), crossed[at].astype(F32))
                 weight_grad[k, 16 * part : 16 * part + 16, 128 * l : 128 * l + 128] = piece
-    bias_grad[...] = held[54].astype(F32)[0:8]
 
 
 def send(array, target):
@@ -465,7 +467,7 @@
     coupling_blocks,
     coupling_sends,
 ):
-    sends = coupling_sends[0].T
+    sends = jnp.transpose(coupling_sends, (2, 0, 1))
     flipped = jnp.swapaxes(conv_weight.reshape(3, 1152, 256), 1, 2)
     b0, b1, b2, far = call(parcels_kernel, [((192, 128), BF)] * 3 + [((96, 128), BF)], [SMEM, VMEM])(sends, ocean_state)
     (copies,) = call(copies_kernel, [((4, 128, 1024), BF)], [VMEM, VMEM])(atm_state, out_grad)
@@ -493,7 +495,7 @@
     outer = lax.all_gather(shard, "chan")
     atm_output, z_all, mine, theirs = call(
         forward_kernel,
-        [((64, 1024), BF), ((256, 1408), BF), ((64, 16, 128), F32), ((64, 16, 128), F32)],
+        [((64, 1024), BF), ((256, 1408), BF), ((64, 16, 128), F32), ((64, 16, 128), BF)],
         [HELD] * 3,
         [
             pltpu.VMEM((384, 128), BF),
@@ -506,10 +508,10 @@
             pltpu.VMEM((192, 1536), BF),
             pltpu.SemaphoreType.DMA((10,)),
         ],
-        limit=60,
+        limit=56,
         cost=10,
     )(inner, outer, flipped)
-    total = (mine + to_mate(theirs)).astype(BF)
+    (total,) = call(add_kernel, [((64, 16, 128), BF)], [VMEM, VMEM])(mine, to_mate(theirs))
     total, z_all = lax.optimization_barrier((total, z_all))
     shares = lax.all_to_all(total, "tile", 0, 0, axis_index_groups=SAME_CORE)
     input_grad, b0, b1, b2, far = call(
@@ -527,20 +529,22 @@
         cost=4,
     )(coupling_sources, coupling_blocks, z_all, conv_weight, regrid_weight, out_grad)
     a0, a1, a2 = chip_send(b0, 0), chip_send(b1, 1), chip_send(b2, 2)
-    shares, a0, a1, a2, far = lax.optimization_barrier((shares, a0, a1, a2, far))
+    shares, a0, a1, far = lax.optimization_barrier((shares, a0, a1, far))
     scale = 1.0 / math.sqrt(atm_state.shape[1] * TILES)
     (summed,) = call(functools.partial(sum_kernel, scale), [((64, 16, 128), BF)], [VMEM])(shares)
     summed, far = lax.optimization_barrier((summed, far))
     held = lax.all_to_all(summed, "tile", 0, 0, axis_index_groups=SAME_CORE)
     far = far_send(far)
+    a2, far = lax.optimization_barrier((a2, far))
     crossed = to_mate(jnp.concatenate([a0[96:], a1[96:], a2[96:]], axis=0))
     (ocean_grad,) = call(return_kernel, [((32, 1024), F32)], [SMEM] + [VMEM] * 5, [pltpu.VMEM((256, 128), F32)])(
         sends, a0, a1, a2, crossed, far
     )
     held, ocean_grad = lax.optimization_barrier((held, ocean_grad))
     crossed = to_mate(held)
-    weight_grad, bias_grad = call(finish_kernel, [((9, 64, 384), F32), ((8, 128), F32)], [VMEM, VMEM])(held, crossed)
-    return atm_output, input_grad, ocean_grad, jnp.swapaxes(weight_grad, 1, 2), bias_grad[0, 0:64]
+    bias_grad = held[54, 0, 0:64].astype(F32)
+    (weight_grad,) = call(finish_kernel, [((9, 64, 384), F32)], [VMEM, VMEM])(held, crossed)
+    return atm_output, input_grad, ocean_grad, jnp.swapaxes(weight_grad, 1, 2), bias_grad
 
 
 def solution(mesh):

time: 185 us -> 179 us (0.968)
  starting transfers between devices: 97.8 us -> 88.9 us
  blocking collectives: 25.7 us -> 33.9 us
  waiting for transfers between devices: 31.1 us -> 27 us
    all_gather x1, blocking collectives: 12.6 us -> 20.7 us  [on_device(): strips = lax.all_gather(strips, 'tile', axis_index_groups=ROW_CHIPS)]
    ppermute x13, starting transfers between devices: 66.9 us -> 60.5 us  [send(): return lax.ppermute(array, 'tile', [(i, target(i)) for i in range(TILES)])]
    ppermute x1, waiting for transfers between devices: 14 us -> 8.88 us  [on_device(): lax.ppermute(north, 'tile', [(i + 8, i) for i in range(TILES - 8)])]
    all_to_all x1, starting transfers between devices: 12.9 us -> 8.75 us  [on_device(): held = lax.all_to_all(summed, 'tile', 0, 0, axis_index_groups=SAME_CORE)]
    all_to_all x1, waiting for transfers between devices: 0.01 us -> 3.23 us  [on_device(): shares = lax.all_to_all(total, 'tile', 0, 0, axis_index_groups=SAME_CORE)]
    ppermute x13, waiting for transfers between devices: 17.1 us -> 14.9 us  [send(): return lax.ppermute(array, 'tile', [(i, target(i)) for i in range(TILES)])]
  transfers between devices with their start and end apart: 18 -> 18, of which waited for: 8 -> 11; matrix products, arithmetic and copies ran while one was open for 1% -> 2% of each run, Pallas kernels for 5% -> 4%
where the time goes in v3:
time: 179 us; the launch traced here: 178 us
  starting transfers between devices  88.9 us (50%)
  blocking collectives  33.9 us (19%)
  waiting for transfers between devices  27 us (15%)
  Pallas kernels  21.8 us (12%)
  local copies, waits for them, and re-layouts  4.84 us (3%)
    ppermute x13, starting transfers between devices, send(): return lax.ppermute(array, 'tile', [(i, target(i)) for i in range(TILES)])  60.5 us
    all_gather x1, blocking collectives, on_device(): strips = lax.all_gather(strips, 'tile', axis_index_groups=ROW_CHIPS)  20.7 us
    ppermute x13, waiting for transfers between devices, send(): return lax.ppermute(array, 'tile', [(i, target(i)) for i in range(TILES)])  14.9 us
    all_gather x1, blocking collectives, on_device(): outer = lax.all_gather(shard, 'chan')  13.2 us
    all_to_all x1, starting transfers between devices, on_device(): shares = lax.all_to_all(total, 'tile', 0, 0, axis_index_groups=SAME_CORE)  10.3 us
    pallas_call x1, Pallas kernels, on_device(): call(forward_kernel, [((64, 1024), BF), ((256, 1408), BF), ((64, 16, 128)...  9.67 us
    ppermute x1, waiting for transfers between devices, on_device(): lax.ppermute(north, 'tile', [(i + 8, i) for i in range(TILES - 8)])  8.88 us
    all_to_all x1, starting transfers between devices, on_device(): held = lax.all_to_all(summed, 'tile', 0, 0, axis_index_groups=SAME_CORE)  8.75 us
  transfers between devices with their start and end apart: 18, of which 11 were waited for; matrix products, arithmetic and copies ran while one was open for 2% of the time, Pallas kernels for 4%

profile of v3, /device:TPU:1, one launch (start us, length us, event | category | flops | bytes accessed | tf_op | source)
XLA Modules:
  0.0 178.0 jit_solution(1061256911370377159)
XLA Ops:
  2.8 12.9 %collective-permute-start = (bf16[192,128]{1,0:T(8,128)(2,1)S(1)}, bf16[192,128]{1,0:T(8,128)(2,1)S(1)}, u32[]{:S(2)}, u32[]{:S(2)}) collective-permute-start(bf16[192,128]{1,0:T(8,128)(2,1)S(1)} %get-tuple-element.40), channel_id=1, source_target_pairs={{0,248},{4,252},{8,256},{12,260},{16,264},{20,268},{24,272},{28,27... | collective-permute-start | bytes 147464 | tf_op jit(solution)/shard_map/ppermute | solution.py:443
  15.7 4.4 %collective-permute-start.1 = (bf16[192,128]{1,0:T(8,128)(2,1)S(1)}, bf16[192,128]{1,0:T(8,128)(2,1)S(1)}, u32[]{:S(2)}, u32[]{:S(2)}) collective-permute-start(bf16[192,128]{1,0:T(8,128)(2,1)S(1)} %get-tuple-element.41), channel_id=1, source_target_pairs={{0,256},{4,260},{8,264},{12,268},{16,272},{20,276},{24,280},{28,28... | collective-permute-start | bytes 147464 | tf_op jit(solution)/shard_map/ppermute | solution.py:443
  20.1 1.9 %collective-permute-start.2 = (bf16[192,128]{1,0:T(8,128)(2,1)S(1)}, bf16[192,128]{1,0:T(8,128)(2,1)S(1)}, u32[]{:S(2)}, u32[]{:S(2)}) collective-permute-start(bf16[192,128]{1,0:T(8,128)(2,1)S(1)} %get-tuple-element.42), channel_id=1, source_target_pairs={{0,264},{4,268},{8,272},{12,276},{16,280},{20,284},{24,288},{28,29... | collective-permute-start | bytes 147464 | tf_op jit(solution)/shard_map/ppermute | solution.py:443
  22.0 1.1 shard_map.139
  23.1 4.4 %all-to-all-start = ((bf16[4,128,1024]{2,1,0:T(8,128)(2,1)}), bf16[4,128,1024]{2,1,0:T(8,128)(2,1)}, u32[]{:S(2)}, u32[]{:S(2)}) async-start(bf16[4,128,1024]{2,1,0:T(8,128)(2,1)} %shard_map.139), calls=%async_computation | async-start | bytes 2097152 | tf_op jit(solution)/shard_map/all_to_all | solution.py:474
  27.6 3.7 %collective-permute-start.3 = (bf16[304,128]{1,0:T(8,128)(2,1)S(1)}, bf16[304,128]{1,0:T(8,128)(2,1)S(1)}, u32[]{:S(2)}, u32[]{:S(2)}) collective-permute-start(bf16[304,128]{1,0:T(8,128)(2,1)S(1)} %fusion.1), channel_id=1, source_target_pairs={{0,4},{4,0},{8,12},{12,8},{16,20},{20,16},{24,28},{28,24},{32,36},... | collective-permute-start | bytes 233480 | tf_op jit(solution)/shard_map/ppermute | solution.py:443
  31.3 1.9 %collective-permute-start.4 = (bf16[96,128]{1,0:T(8,128)(2,1)S(1)}, bf16[96,128]{1,0:T(8,128)(2,1)S(1)}, u32[]{:S(2)}, u32[]{:S(2)}) collective-permute-start(bf16[96,128]{1,0:T(8,128)(2,1)S(1)} %get-tuple-element.43), channel_id=1, source_target_pairs={{0,244},{4,272},{8,252},{12,280},{16,260},{20,288},{24,268},{28,29... | collective-permute-start | bytes 73736 | tf_op jit(solution)/shard_map/ppermute | solution.py:443
  33.3 2.2 %copy.15 = bf16[3,1152,256]{1,2,0:T(8,128)(2,1)} copy(bf16[3,1152,256]{2,1,0:T(8,128)(2,1)S(1)} %bitcast.10) | data formatting | bytes 3538944 | tf_op jit(solution)/shard_map/reshape | solution.py:471
  35.5 4.3 %collective-permute-done.4.far = bf16[96,128]{1,0:T(8,128)(2,1)S(1)} collective-permute-done((bf16[96,128]{1,0:T(8,128)(2,1)S(1)}, bf16[96,128]{1,0:T(8,128)(2,1)S(1)}, u32[]{:S(2)}, u32[]{:S(2)}) %collective-permute-start.4) | collective-permute-done | bytes 24608 | tf_op jit(solution)/shard_map/ppermute | solution.py:443
  39.8 1.5 shard_map.138
  41.3 3.7 %collective-permute-start.5 = (bf16[64,512]{1,0:T(8,128)(2,1)S(1)}, bf16[64,512]{1,0:T(8,128)(2,1)S(1)}, u32[]{:S(2)}, u32[]{:S(2)}) collective-permute-start(bf16[64,512]{1,0:T(8,128)(2,1)S(1)} %get-tuple-element.45), channel_id=1, source_target_pairs={{0,32},{4,36},{8,40},{12,44},{16,48},{20,52},{24,56},{28,60},{32,6... | collective-permute-start | bytes 196616 | tf_op jit(solution)/shard_map/ppermute | solution.py:486
  45.0 1.3 collective-permute-start.6
  46.3 8.9 %collective-permute-done.6 = bf16[64,512]{1,0:T(8,128)(2,1)S(1)} collective-permute-done((bf16[64,512]{1,0:T(8,128)(2,1)S(1)}, bf16[64,512]{1,0:T(8,128)(2,1)S(1)}, u32[]{:S(2)}, u32[]{:S(2)}) %collective-permute-start.6) | collective-permute-done | bytes 65568 | tf_op jit(solution)/shard_map/ppermute | solution.py:487
  55.2 20.7 %all-gather = bf16[256,1152]{1,0:T(8,128)(2,1)S(1)} all-gather(bf16[64,1152]{1,0:T(8,128)(2,1)S(1)} %pad_maximum_fusion), channel_id=2, replica_groups={{0,8,16,24},{4,12,20,28},{32,40,48,56},{36,44,52,60},{64,72,80,88},{68,..., dimensions={0}, use_global_device_ids=true | all-gather | bytes 737280 | tf_op jit(solution)/shard_map/all_gather | solution.py:490
  77.0 3.0 %collective-permute-start.7 = (bf16[64,1152]{1,0:T(8,128)(2,1)S(1)}, bf16[64,1152]{1,0:T(8,128)(2,1)S(1)}, u32[]{:S(2)}, u32[]{:S(2)}) collective-permute-start(bf16[64,1152]{1,0:T(8,128)(2,1)S(1)} %get-tuple-element.52), channel_id=1, source_target_pairs={{0,4},{4,0},{8,12},{12,8},{16,20},{20,16},{24,28},{28,24},{32,36},... | collective-permute-start | bytes 442376 | tf_op jit(solution)/shard_map/ppermute | solution.py:443
  81.1 13.2 %all-gather.1 = bf16[256,1664]{1,0:T(8,128)(2,1)} all-gather(bf16[64,1664]{1,0:T(8,128)(2,1)S(1)} %pad_add_fusion), channel_id=3, replica_groups=mesh['tile'=128,'chan'=4] {'chan'}, dimensions={0}, use_global_device_ids=true | all-gather | bytes 1064960 | tf_op jit(solution)/shard_map/all_gather | solution.py:495
  94.2 9.7 %shard_map.141 = (bf16[64,1024]{1,0:T(8,128)(2,1)}, bf16[256,1408]{1,0:T(8,128)(2,1)}, f32[64,16,128]{2,1,0:T(8,128)}, bf16[64,16,128]{2,1,0:T(8,128)(2,1)}) custom-call(bf16[4,128,1024]{2,1,0:T(8,128)(2,1)} %all-to-all-done.inner, bf16[4,64,1664]{2,1,0:T(8,128)(2,1)} %bitcast.16, bf16[3,256,1152]{2,1,0:T(8,128)(2,1)} %bitcast.15), custom_call_target="tpu_custom_call" | custom-call | flops 10000000000 | bytes 30000000 | tf_op jit(solution)/shard_map/pallas_call | solution.py:496
  103.9 4.5 %collective-permute-start.8 = (bf16[64,16,128]{2,1,0:T(8,128)(2,1)}, bf16[64,16,128]{2,1,0:T(8,128)(2,1)S(1)}, u32[]{:S(2)}, u32[]{:S(2)}) collective-permute-start(bf16[64,16,128]{2,1,0:T(8,128)(2,1)} %get-tuple-element.56), channel_id=1, source_target_pairs={{0,4},{4,0},{8,12},{12,8},{16,20},{20,16},{24,28},{28,24},{32,36},... | collective-permute-start | bytes 786440 | tf_op jit(solution)/shard_map/ppermute | solution.py:443
  108.4 1.4 collective-permute-done.8.crossed
  111.5 10.3 %all-to-all-start.1 = ((bf16[64,16,128]{2,1,0:T(8,128)(2,1)}), bf16[64,16,128]{2,1,0:T(8,128)(2,1)S(1)}, u32[]{:S(2)}, u32[]{:S(2)}) async-start(bf16[64,16,128]{2,1,0:T(8,128)(2,1)} %shard_map.142), calls=%async_computation.1 | async-start | bytes 524288 | tf_op jit(solution)/shard_map/all_to_all | solution.py:516
  121.8 3.9 %shard_map.143 = (bf16[64,1024]{1,0:T(8,128)(2,1)}, bf16[192,128]{1,0:T(8,128)(2,1)S(1)}, bf16[192,128]{1,0:T(8,128)(2,1)S(1)}, bf16[192,128]{1,0:T(8,128)(2,1)S(1)}, bf16[96,128]{1,0:T(8,128)(2,1)S(1)}) custom-call(s32[1,4]{1,0:T(1,128)S(1)} %copy-done.9, s32[1,12]{1,0:T(1,128)S(1)} %copy-done.10, bf16[256,1408]{1,0:T(8,128)(2,1)S(1)} %copy-done.12, ...), custom_call_target="tpu_custom_call" | custom-call | flops 4000000000 | bytes 12000000 | tf_op jit(solution)/shard_map/pallas_call | solution.py:517
  125.7 5.1 %collective-permute-start.9 = (bf16[192,128]{1,0:T(8,128)(2,1)S(1)}, bf16[192,128]{1,0:T(8,128)(2,1)S(1)}, u32[]{:S(2)}, u32[]{:S(2)}) collective-permute-start(bf16[192,128]{1,0:T(8,128)(2,1)S(1)} %get-tuple-element.61), channel_id=1, source_target_pairs={{0,248},{4,252},{8,256},{12,260},{16,264},{20,268},{24,272},{28,27... | collective-permute-start | bytes 147464 | tf_op jit(solution)/shard_map/ppermute | solution.py:443
  130.8 4.5 %collective-permute-start.10 = (bf16[192,128]{1,0:T(8,128)(2,1)S(1)}, bf16[192,128]{1,0:T(8,128)(2,1)S(1)}, u32[]{:S(2)}, u32[]{:S(2)}) collective-permute-start(bf16[192,128]{1,0:T(8,128)(2,1)S(1)} %get-tuple-element.62), channel_id=1, source_target_pairs={{0,256},{4,260},{8,264},{12,268},{16,272},{20,276},{24,280},{28,28... | collective-permute-start | bytes 147464 | tf_op jit(solution)/shard_map/ppermute | solution.py:443
  136.2 2.2 %collective-permute-done.10.a1 = bf16[192,128]{1,0:T(8,128)(2,1)S(1)} collective-permute-done((bf16[192,128]{1,0:T(8,128)(2,1)S(1)}, bf16[192,128]{1,0:T(8,128)(2,1)S(1)}, u32[]{:S(2)}, u32[]{:S(2)}) %collective-permute-start.10) | collective-permute-done | bytes 49184 | tf_op jit(solution)/shard_map/ppermute | solution.py:443
  138.4 3.2 %all-to-all-done.1.arrived = bf16[64,16,128]{2,1,0:T(8,128)(2,1)S(1)} async-done(((bf16[64,16,128]{2,1,0:T(8,128)(2,1)}), bf16[64,16,128]{2,1,0:T(8,128)(2,1)S(1)}, u32[]{:S(2)}, u32[]{:S(2)}) %all-to-all-start.1) | async-done | bytes 262176 | tf_op jit(solution)/shard_map/all_to_all | solution.py:516
  142.4 8.8 %all-to-all-start.2 = ((bf16[64,16,128]{2,1,0:T(8,128)(2,1)}), bf16[64,16,128]{2,1,0:T(8,128)(2,1)S(1)}, u32[]{:S(2)}, u32[]{:S(2)}) async-start(bf16[64,16,128]{2,1,0:T(8,128)(2,1)} %shard_map.144), calls=%async_computation.2 | async-start | bytes 524288 | tf_op jit(solution)/shard_map/all_to_all | solution.py:536
  151.2 5.4 %collective-permute-start.11 = (bf16[192,128]{1,0:T(8,128)(2,1)S(1)}, bf16[192,128]{1,0:T(8,128)(2,1)S(1)}, u32[]{:S(2)}, u32[]{:S(2)}) collective-permute-start(bf16[192,128]{1,0:T(8,128)(2,1)S(1)} %get-tuple-element.69), channel_id=1, source_target_pairs={{0,264},{4,268},{8,272},{12,276},{16,280},{20,284},{24,288},{28,29... | collective-permute-start | bytes 147464 | tf_op jit(solution)/shard_map/ppermute | solution.py:443
  156.6 5.9 %collective-permute-start.12 = (bf16[96,128]{1,0:T(8,128)(2,1)S(1)}, bf16[96,128]{1,0:T(8,128)(2,1)S(1)}, u32[]{:S(2)}, u32[]{:S(2)}) collective-permute-start(bf16[96,128]{1,0:T(8,128)(2,1)S(1)} %get-tuple-element.70), channel_id=1, source_target_pairs={{0,244},{4,272},{8,252},{12,280},{16,260},{20,288},{24,268},{28,29... | collective-permute-start | bytes 73736 | tf_op jit(solution)/shard_map/ppermute | solution.py:443
  163.4 2.9 %collective-permute-done.12.far = bf16[96,128]{1,0:T(8,128)(2,1)S(1)} collective-permute-done((bf16[96,128]{1,0:T(8,128)(2,1)S(1)}, bf16[96,128]{1,0:T(8,128)(2,1)S(1)}, u32[]{:S(2)}, u32[]{:S(2)}) %collective-permute-start.12) | collective-permute-done | bytes 24608 | tf_op jit(solution)/shard_map/ppermute | solution.py:443
  166.3 3.7 %collective-permute-start.13 = (bf16[288,128]{1,0:T(8,128)(2,1)S(1)}, bf16[288,128]{1,0:T(8,128)(2,1)S(1)}, u32[]{:S(2)}, u32[]{:S(2)}) collective-permute-start(bf16[288,128]{1,0:T(8,128)(2,1)S(1)} %pad_maximum_fusion.1), channel_id=1, source_target_pairs={{0,4},{4,0},{8,12},{12,8},{16,20},{20,16},{24,28},{28,24},{32,36},... | collective-permute-start | bytes 221192 | tf_op jit(solution)/shard_map/ppermute | solution.py:443
  170.9 1.4 shard_map.145
  172.4 3.5 %collective-permute-start.14 = (bf16[64,16,128]{2,1,0:T(8,128)(2,1)S(1)}, bf16[64,16,128]{2,1,0:T(8,128)(2,1)S(1)}, u32[]{:S(2)}, u32[]{:S(2)}) collective-permute-start(bf16[64,16,128]{2,1,0:T(8,128)(2,1)S(1)} %all-to-all-done.2.held), channel_id=1, source_target_pairs={{0,4},{4,0},{8,12},{12,8},{16,20},{20,16},{24,28},{28,24},{32,36},... | collective-permute-start | bytes 786440 | tf_op jit(solution)/shard_map/ppermute | solution.py:443
  (56 shorter events, 11.6 us)
Async XLA Ops:
  0.6 0.8 copy-start.4
  1.5 0.7 copy-start.5
  2.2 19.9 %copy-start.2 = (bf16[64,1024]{1,0:T(8,128)(2,1)S(1)}, bf16[64,1024]{1,0:T(8,128)(2,1)}, u32[]{:S(2)}) copy-start(bf16[64,1024]{1,0:T(8,128)(2,1)} %atm.3) | copy-start | bytes 393220
  2.2 19.9 %copy-start.3 = (bf16[64,1024]{1,0:T(8,128)(2,1)S(1)}, bf16[64,1024]{1,0:T(8,128)(2,1)}, u32[]{:S(2)}) copy-start(bf16[64,1024]{1,0:T(8,128)(2,1)} %grad.5) | copy-start | bytes 393220
  2.8 24.7 %collective-permute-start = (bf16[192,128]{1,0:T(8,128)(2,1)S(1)}, bf16[192,128]{1,0:T(8,128)(2,1)S(1)}, u32[]{:S(2)}, u32[]{:S(2)}) collective-permute-start(bf16[192,128]{1,0:T(8,128)(2,1)S(1)} %get-tuple-element.40), channel_id=1, source_target_pairs={{0,248},{4,252},{8,256},{12,260},{16,264},{20,268},{24,272},{28,27... | collective-permute-start | bytes 147464 | tf_op jit(solution)/shard_map/ppermute | solution.py:443
  15.7 11.8 %collective-permute-start.1 = (bf16[192,128]{1,0:T(8,128)(2,1)S(1)}, bf16[192,128]{1,0:T(8,128)(2,1)S(1)}, u32[]{:S(2)}, u32[]{:S(2)}) collective-permute-start(bf16[192,128]{1,0:T(8,128)(2,1)S(1)} %get-tuple-element.41), channel_id=1, source_target_pairs={{0,256},{4,260},{8,264},{12,268},{16,272},{20,276},{24,280},{28,28... | collective-permute-start | bytes 147464 | tf_op jit(solution)/shard_map/ppermute | solution.py:443
  20.1 7.5 %collective-permute-start.2 = (bf16[192,128]{1,0:T(8,128)(2,1)S(1)}, bf16[192,128]{1,0:T(8,128)(2,1)S(1)}, u32[]{:S(2)}, u32[]{:S(2)}) collective-permute-start(bf16[192,128]{1,0:T(8,128)(2,1)S(1)} %get-tuple-element.42), channel_id=1, source_target_pairs={{0,264},{4,268},{8,272},{12,276},{16,280},{20,284},{24,288},{28,29... | collective-permute-start | bytes 147464 | tf_op jit(solution)/shard_map/ppermute | solution.py:443
  23.1 4.4 %copy-start.7 = (s32[1,8]{1,0:T(1,128)S(1)}, s32[1,8]{1,0:T(1,128)}, u32[]{:S(2)}) copy-start(s32[1,8]{1,0:T(1,128)} %own_near.1) | copy-start | bytes 100
  23.1 10.2 %copy-start = (bf16[9,384,256]{2,1,0:T(8,128)(2,1)S(1)}, bf16[9,384,256]{2,1,0:T(8,128)(2,1)}, u32[]{:S(2)}) copy-start(bf16[9,384,256]{2,1,0:T(8,128)(2,1)} %weights_held.1) | copy-start | bytes 5308420
  23.1 32.1 %all-to-all-start = ((bf16[4,128,1024]{2,1,0:T(8,128)(2,1)}), bf16[4,128,1024]{2,1,0:T(8,128)(2,1)}, u32[]{:S(2)}, u32[]{:S(2)}) async-start(bf16[4,128,1024]{2,1,0:T(8,128)(2,1)} %shard_map.139), calls=%async_computation | async-start | bytes 2097152 | tf_op jit(solution)/shard_map/all_to_all | solution.py:474
  27.6 12.2 %collective-permute-start.3 = (bf16[304,128]{1,0:T(8,128)(2,1)S(1)}, bf16[304,128]{1,0:T(8,128)(2,1)S(1)}, u32[]{:S(2)}, u32[]{:S(2)}) collective-permute-start(bf16[304,128]{1,0:T(8,128)(2,1)S(1)} %fusion.1), channel_id=1, source_target_pairs={{0,4},{4,0},{8,12},{12,8},{16,20},{20,16},{24,28},{28,24},{32,36},... | collective-permute-start | bytes 233480 | tf_op jit(solution)/shard_map/ppermute | solution.py:443
  31.3 8.5 %collective-permute-start.4 = (bf16[96,128]{1,0:T(8,128)(2,1)S(1)}, bf16[96,128]{1,0:T(8,128)(2,1)S(1)}, u32[]{:S(2)}, u32[]{:S(2)}) collective-permute-start(bf16[96,128]{1,0:T(8,128)(2,1)S(1)} %get-tuple-element.43), channel_id=1, source_target_pairs={{0,244},{4,272},{8,252},{12,280},{16,260},{20,288},{24,268},{28,29... | collective-permute-start | bytes 73736 | tf_op jit(solution)/shard_map/ppermute | solution.py:443
  33.3 6.5 %copy-start.1 = (bf16[12,128,128]{2,1,0:T(8,128)(2,1)S(1)}, bf16[12,128,128]{2,1,0:T(8,128)(2,1)}, u32[]{:S(2)}) copy-start(bf16[12,128,128]{2,1,0:T(8,128)(2,1)} %regrid_weights.1) | copy-start | bytes 1179652
  33.3 6.5 %copy-start.9 = (s32[1,4]{1,0:T(1,128)S(1)}, s32[1,4]{1,0:T(1,128)}, u32[]{:S(2)}) copy-start(s32[1,4]{1,0:T(1,128)} %sources.3) | copy-start | bytes 52
  33.3 6.5 %copy-start.10 = (s32[1,12]{1,0:T(1,128)S(1)}, s32[1,12]{1,0:T(1,128)}, u32[]{:S(2)}) copy-start(s32[1,12]{1,0:T(1,128)} %blocks.3) | copy-start | bytes 148
  39.8 36.2 %copy-start.8 = (f32[64]{0:T(128)S(1)}, f32[64]{0:T(128)}, u32[]{:S(2)}) copy-start(f32[64]{0:T(128)} %param.13) | copy-start | bytes 772
  41.3 5.0 %collective-permute-start.5 = (bf16[64,512]{1,0:T(8,128)(2,1)S(1)}, bf16[64,512]{1,0:T(8,128)(2,1)S(1)}, u32[]{:S(2)}, u32[]{:S(2)}) collective-permute-start(bf16[64,512]{1,0:T(8,128)(2,1)S(1)} %get-tuple-element.45), channel_id=1, source_target_pairs={{0,32},{4,36},{8,40},{12,44},{16,48},{20,52},{24,56},{28,60},{32,6... | collective-permute-start | bytes 196616 | tf_op jit(solution)/shard_map/ppermute | solution.py:486
  45.0 10.2 %collective-permute-start.6 = (bf16[64,512]{1,0:T(8,128)(2,1)S(1)}, bf16[64,512]{1,0:T(8,128)(2,1)S(1)}, u32[]{:S(2)}, u32[]{:S(2)}) collective-permute-start(bf16[64,512]{1,0:T(8,128)(2,1)S(1)} %get-tuple-element.46), channel_id=1, source_target_pairs={{32,0},{36,4},{40,8},{44,12},{48,16},{52,20},{56,24},{60,28},{64,3... | collective-permute-start | bytes 196616 | tf_op jit(solution)/shard_map/ppermute | solution.py:487
  77.0 4.0 %collective-permute-start.7 = (bf16[64,1152]{1,0:T(8,128)(2,1)S(1)}, bf16[64,1152]{1,0:T(8,128)(2,1)S(1)}, u32[]{:S(2)}, u32[]{:S(2)}) collective-permute-start(bf16[64,1152]{1,0:T(8,128)(2,1)S(1)} %get-tuple-element.52), channel_id=1, source_target_pairs={{0,4},{4,0},{8,12},{12,8},{16,20},{20,16},{24,28},{28,24},{32,36},... | collective-permute-start | bytes 442376 | tf_op jit(solution)/shard_map/ppermute | solution.py:443
  103.9 5.8 %collective-permute-start.8 = (bf16[64,16,128]{2,1,0:T(8,128)(2,1)}, bf16[64,16,128]{2,1,0:T(8,128)(2,1)S(1)}, u32[]{:S(2)}, u32[]{:S(2)}) collective-permute-start(bf16[64,16,128]{2,1,0:T(8,128)(2,1)} %get-tuple-element.56), channel_id=1, source_target_pairs={{0,4},{4,0},{8,12},{12,8},{16,20},{20,16},{24,28},{28,24},{32,36},... | collective-permute-start | bytes 786440 | tf_op jit(solution)/shard_map/ppermute | solution.py:443
  109.7 1.0 copy-start.11
  110.8 11.1 %copy-start.12 = (bf16[256,1408]{1,0:T(8,128)(2,1)S(1)}, bf16[256,1408]{1,0:T(8,128)(2,1)}, u32[]{:S(2)}) copy-start(bf16[256,1408]{1,0:T(8,128)(2,1)} %get-tuple-element.58.z_all) | copy-start | bytes 2162692
  111.5 30.1 %all-to-all-start.1 = ((bf16[64,16,128]{2,1,0:T(8,128)(2,1)}), bf16[64,16,128]{2,1,0:T(8,128)(2,1)S(1)}, u32[]{:S(2)}, u32[]{:S(2)}) async-start(bf16[64,16,128]{2,1,0:T(8,128)(2,1)} %shard_map.142), calls=%async_computation.1 | async-start | bytes 524288 | tf_op jit(solution)/shard_map/all_to_all | solution.py:516
  125.7 10.5 %collective-permute-start.9 = (bf16[192,128]{1,0:T(8,128)(2,1)S(1)}, bf16[192,128]{1,0:T(8,128)(2,1)S(1)}, u32[]{:S(2)}, u32[]{:S(2)}) collective-permute-start(bf16[192,128]{1,0:T(8,128)(2,1)S(1)} %get-tuple-element.61), channel_id=1, source_target_pairs={{0,248},{4,252},{8,256},{12,260},{16,264},{20,268},{24,272},{28,27... | collective-permute-start | bytes 147464 | tf_op jit(solution)/shard_map/ppermute | solution.py:443
  130.8 7.6 %collective-permute-start.10 = (bf16[192,128]{1,0:T(8,128)(2,1)S(1)}, bf16[192,128]{1,0:T(8,128)(2,1)S(1)}, u32[]{:S(2)}, u32[]{:S(2)}) collective-permute-start(bf16[192,128]{1,0:T(8,128)(2,1)S(1)} %get-tuple-element.62), channel_id=1, source_target_pairs={{0,256},{4,260},{8,264},{12,268},{16,272},{20,276},{24,280},{28,28... | collective-permute-start | bytes 147464 | tf_op jit(solution)/shard_map/ppermute | solution.py:443
  141.6 29.3 %copy-start.6 = (s32[1,128,3]{1,0,2:T(1,128)S(1)}, s32[1,128,3]{1,0,2:T(1,128)}, u32[]{:S(2)}) copy-start(s32[1,128,3]{1,0,2:T(1,128)} %param.19) | copy-start | bytes 4612
  142.4 30.0 %all-to-all-start.2 = ((bf16[64,16,128]{2,1,0:T(8,128)(2,1)}), bf16[64,16,128]{2,1,0:T(8,128)(2,1)S(1)}, u32[]{:S(2)}, u32[]{:S(2)}) async-start(bf16[64,16,128]{2,1,0:T(8,128)(2,1)} %shard_map.144), calls=%async_computation.2 | async-start | bytes 524288 | tf_op jit(solution)/shard_map/all_to_all | solution.py:536
  151.2 12.2 %collective-permute-start.11 = (bf16[192,128]{1,0:T(8,128)(2,1)S(1)}, bf16[192,128]{1,0:T(8,128)(2,1)S(1)}, u32[]{:S(2)}, u32[]{:S(2)}) collective-permute-start(bf16[192,128]{1,0:T(8,128)(2,1)S(1)} %get-tuple-element.69), channel_id=1, source_target_pairs={{0,264},{4,268},{8,272},{12,276},{16,280},{20,284},{24,288},{28,29... | collective-permute-start | bytes 147464 | tf_op jit(solution)/shard_map/ppermute | solution.py:443
  156.6 9.7 %collective-permute-start.12 = (bf16[96,128]{1,0:T(8,128)(2,1)S(1)}, bf16[96,128]{1,0:T(8,128)(2,1)S(1)}, u32[]{:S(2)}, u32[]{:S(2)}) collective-permute-start(bf16[96,128]{1,0:T(8,128)(2,1)S(1)} %get-tuple-element.70), channel_id=1, source_target_pairs={{0,244},{4,272},{8,252},{12,280},{16,260},{20,288},{24,268},{28,29... | collective-permute-start | bytes 73736 | tf_op jit(solution)/shard_map/ppermute | solution.py:443
  166.3 4.6 %collective-permute-start.13 = (bf16[288,128]{1,0:T(8,128)(2,1)S(1)}, bf16[288,128]{1,0:T(8,128)(2,1)S(1)}, u32[]{:S(2)}, u32[]{:S(2)}) collective-permute-start(bf16[288,128]{1,0:T(8,128)(2,1)S(1)} %pad_maximum_fusion.1), channel_id=1, source_target_pairs={{0,4},{4,0},{8,12},{12,8},{16,20},{20,16},{24,28},{28,24},{32,36},... | collective-permute-start | bytes 221192 | tf_op jit(solution)/shard_map/ppermute | solution.py:443
  172.4 4.6 %collective-permute-start.14 = (bf16[64,16,128]{2,1,0:T(8,128)(2,1)S(1)}, bf16[64,16,128]{2,1,0:T(8,128)(2,1)S(1)}, u32[]{:S(2)}, u32[]{:S(2)}) collective-permute-start(bf16[64,16,128]{2,1,0:T(8,128)(2,1)S(1)} %all-to-all-done.2.held), channel_id=1, source_target_pairs={{0,4},{4,0},{8,12},{12,8},{16,20},{20,16},{24,28},{28,24},{32,36},... | collective-permute-start | bytes 786440 | tf_op jit(solution)/shard_map/ppermute | solution.py:443

commit v4 on v3

--- a/solution.py
+++ b/solution.py
@@ -150,7 +150,7 @@
         copies[chan, 64:128] = grad[...]
 
 
-def regrid_kernel(sources, blocks, a0, a1, a2, crossed, far, weights, atm, grad, regridded, north, south, sides, held, acc):
+def regrid_kernel(sources, blocks, a0, a1, a2, crossed, far, weights, atm, grad, regridded, keep, give, sides, held, acc):
     tile = lax.axis_index("tile")
     facing = 1 - 2 * (tile & 1)
     for i, ref in enumerate((a0, a1, a2)):
@@ -175,14 +175,29 @@
 
     for a in range(8):
         regridded[:, LANES * a : LANES * (a + 1)] = acc[32 * a : 32 * (a + 1), :].astype(BF)
-    north[:, 0:256] = atm[:, 0:256]
-    north[:, 256:384] = grad[:, 0:128]
-    north[0:32, 384:512] = regridded[:, 0:128]
-    north[32:64, 384:512] = regridded[:, 128:256]
-    south[:, 0:256] = atm[:, 768:1024]
-    south[:, 256:384] = grad[:, 896:1024]
-    south[0:32, 384:512] = regridded[:, 768:896]
-    south[32:64, 384:512] = regridded[:, 896:1024]
+
+    def north(out):
+        out[:, 0:256] = atm[:, 0:256]
+        out[:, 256:384] = grad[:, 0:128]
+        out[0:32, 384:512] = regridded[:, 0:128]
+        out[32:64, 384:512] = regridded[:, 128:256]
+
+    def south(out):
+        out[:, 0:256] = atm[:, 768:1024]
+        out[:, 256:384] = grad[:, 896:1024]
+        out[0:32, 384:512] = regridded[:, 768:896]
+        out[32:64, 384:512] = regridded[:, 896:1024]
+
+    @pl.when(facing == 1)
+    def _():
+        south(keep)
+        north(give)
+
+    @pl.when(facing != 1)
+    def _():
+        north(keep)
+        south(give)
+
     edges = dot(atm[...], edge_table(0)) + dot(grad[...], grad_edge_table())
     sides[0:32, :] = (edges[0:32] + dot(regridded[...], edge_table(64))).astype(BF)
     sides[32:64, :] = edges[32:64].astype(BF)
@@ -192,23 +207,26 @@
     core = lax.axis_index("tile") & 1
     for near, out in ((own_near, own), (mate_near, mate)):
 
-        def pick(direction):
+        def strip(direction):
+            device = near[0, direction]
+            side = 1 if direction in (1, 6, 7) else 0
+            here = (device >= 0) & (core == side)
+            first = pl.multiple_of(jnp.where(here, (device & 1) ^ side, 0) * 512, 512)
+            data = gathered[jnp.where(here, (device & 7) >> 1, 0), :, pl.ds(first, 512)]
+            return jnp.where(here, data, jnp.zeros_like(data))
+
+        def beside(direction):
             device = near[0, direction]
             here = (device >= 0) & ((device & 1) == core)
-            chip = (device & 7) >> 1
-            return jnp.where(here, chip, 0), here
-
-        def strip(direction, lanes):
-            chip, here = pick(direction)
-            data = gathered[chip, :, lanes[0] : lanes[1]]
+            data = gathered[jnp.where(here, (device & 7) >> 1, 0), :, 1024:1152]
             return jnp.where(here, data, jnp.zeros_like(data))
 
-        out[:, 0:512] = strip(0, (0, 512))
-        out[:, 512:1024] = strip(1, (512, 1024))
+        out[:, 0:512] = strip(0)
+        out[:, 512:1024] = strip(1)
         total = jnp.zeros((64, 128), F32)
         halves = [jnp.zeros((32, 128), F32), jnp.zeros((32, 128), F32)]
         for east in (0, 1):
-            data = strip(2 + east, (1024, 1152))
+            data = beside(2 + east)
             given = 0 if east else 16
             picks = beside_table(given, 8 + 2 * east, 4) + beside_grad_table(32 if east else 40, OG0 + 2 + east)
             total = total + dot(data, picks)
@@ -216,7 +234,7 @@
             col = 0 if east else 126
             for at_south in (0, 1):
                 first, beyond = (10, 9) if at_south else (0, 0)
-                data = strip(4 + 2 * at_south + east, (512, 1024) if at_south else (0, 512))
+                data = strip(4 + 2 * at_south + east)
                 for q in (0, 1):
                     total = total + dot(data[:, 128 * q : 128 * q + 128], pair_table(col, 4 * (first + q) + 2 * east))
                     halves[east] = halves[east] + dot(data[32 * q : 32 * q + 32, 384:512], pair_table(col, OC0 + 2 * (first + q)))
@@ -343,11 +361,13 @@
 
 
 def backward_kernel(
-    sources, blocks, z_all, weights_held, regrid_weights, grad,
-    input_grad, r0, r1, r2, far, taps, delta, terms, weights, sem,
+    sources, blocks, z_all, weights_held, regrid_held, grad_held,
+    input_grad, r0, r1, r2, far, taps, delta, terms, weights, regrid_weights, grad, sems,
 ):
-    fetch = pltpu.make_async_copy(weights_held, weights, sem)
-    fetch.start()
+    pairs = ((weights_held, weights), (grad_held, grad), (regrid_held, regrid_weights))
+    fetches = [pltpu.make_async_copy(held, ref, sems.at[i]) for i, (held, ref) in enumerate(pairs)]
+    for fetch in fetches:
+        fetch.start()
     tile, chan = lax.axis_index("tile"), lax.axis_index("chan")
     facing = 1 - 2 * (tile & 1)
     side = z_all[:, 1280:1408]
@@ -361,7 +381,8 @@
     taps[256:512, :] = z_all[:, 0:1280]
     atm_rows = pl.ds(pl.multiple_of(chan * 64, 64), 64)
     sea_rows = pl.ds(pl.multiple_of(256 + chan * 32, 32), 32)
-    fetch.wait()
+    for fetch in fetches:
+        fetch.wait()
     for q in range(4):
         atm_total = jnp.zeros((64, 256), F32)
         sea_total = jnp.zeros((32, 256), F32)
@@ -468,30 +489,33 @@
     coupling_sends,
 ):
     sends = jnp.transpose(coupling_sends, (2, 0, 1))
-    flipped = jnp.swapaxes(conv_weight.reshape(3, 1152, 256), 1, 2)
     b0, b1, b2, far = call(parcels_kernel, [((192, 128), BF)] * 3 + [((96, 128), BF)], [SMEM, VMEM])(sends, ocean_state)
-    (copies,) = call(copies_kernel, [((4, 128, 1024), BF)], [VMEM, VMEM])(atm_state, out_grad)
-    inner = lax.all_to_all(copies, "chan", 0, 0)
     a0, a1, a2, far = chip_send(b0, 0), chip_send(b1, 1), chip_send(b2, 2), far_send(far)
-    far, flipped = lax.optimization_barrier((far, flipped))
+    a0, a1, a2, far = lax.optimization_barrier((a0, a1, a2, far))
     table = jnp.pad(atm_neighbours.astype(BF), ((0, 15), (0, 120)))
     crossed = to_mate(jnp.concatenate([a0[96:], a1[96:], a2[96:], table], axis=0))
     mate_near = crossed[288:289, 0:8].astype(jnp.int32)
-    regridded, north, south, sides = call(
+    regridded, keep, give, sides = call(
         regrid_kernel,
         [((32, 1024), BF), ((64, 512), BF), ((64, 512), BF), ((64, 128), BF)],
         [SMEM] * 2 + [VMEM] * 8,
         [pltpu.VMEM((672, 128), BF), pltpu.VMEM((256, 128), F32)],
     )(coupling_sources, coupling_blocks, a0, a1, a2, crossed, far, regrid_weight, atm_state, out_grad)
-    from_north = lax.ppermute(south, "tile", [(i, i + 8) for i in range(TILES - 8)])
-    from_south = lax.ppermute(north, "tile", [(i + 8, i) for i in range(TILES - 8)])
-    strips = jnp.concatenate([from_north, from_south, sides], axis=1)
-    strips, inner = lax.optimization_barrier((strips, inner))
+    got, weights_now, atm_now, grad_now = lax.optimization_barrier((to_mate(give), conv_weight, atm_state, out_grad))
+    (copies,) = call(copies_kernel, [((4, 128, 1024), BF)], [VMEM, VMEM])(atm_now, grad_now)
+    inner = lax.all_to_all(copies, "chan", 0, 0)
+    flipped = jnp.swapaxes(weights_now.reshape(3, 1152, 256), 1, 2)
+    pair = jnp.concatenate([keep, got], axis=1)
+    pairs = [(i, i + 8 - 16 * (i % 2)) for i in range(TILES)]
+    arrived = lax.ppermute(pair, "tile", [(i, j) for i, j in pairs if 0 <= j < TILES])
+    strips = jnp.concatenate([arrived, sides], axis=1)
+    strips, flipped = lax.optimization_barrier((strips, flipped))
     strips = lax.all_gather(strips, "tile", axis_index_groups=ROW_CHIPS)
     own, mate = call(select_kernel, [((64, 1664), BF), ((64, 1152), BF)], [SMEM] * 2 + [VMEM] * 3)(
         atm_neighbours, mate_near, strips, regridded, conv_bias.reshape(1, 64)
     )
     shard = own + jnp.pad(to_mate(mate), ((0, 0), (0, 512)))
+    shard, inner = lax.optimization_barrier((shard, inner))
     outer = lax.all_gather(shard, "chan")
     atm_output, z_all, mine, theirs = call(
         forward_kernel,
@@ -517,13 +541,15 @@
     input_grad, b0, b1, b2, far = call(
         backward_kernel,
         [((64, 1024), BF)] + [((192, 128), BF)] * 3 + [((96, 128), BF)],
-        [SMEM] * 2 + [VMEM, HELD, VMEM, VMEM],
+        [SMEM] * 2 + [VMEM] + [HELD] * 3,
         [
             pltpu.VMEM((768, 1280), BF),
             pltpu.VMEM((32, 1024), BF),
             pltpu.VMEM((480, 128), BF),
             pltpu.VMEM((9, 384, 256), BF),
-            pltpu.SemaphoreType.DMA,
+            pltpu.VMEM((12, 128, 128), BF),
+            pltpu.VMEM((64, 1024), BF),
+            pltpu.SemaphoreType.DMA((3,)),
         ],
         limit=48,
         cost=4,

time: 179 us -> 175 us (0.978)
  blocking collectives: 33.9 us -> 26.2 us
  starting transfers between devices: 88.9 us -> 92.6 us
    all_gather x1, blocking collectives: 20.7 us -> 12.9 us  [on_device(): strips = lax.all_gather(strips, 'tile', axis_index_groups=ROW_CHIPS)]
    ppermute x2 -> x1, waiting for transfers between devices: 8.88 us -> 3.43 us  [on_device(): lax.ppermute(pair, 'tile', [(i, j) for i, j in pairs if 0 <= j < TILES])]
    ppermute x13 -> x14, starting transfers between devices: 60.5 us -> 65.9 us  [send(): return lax.ppermute(array, 'tile', [(i, target(i)) for i in range(TILES)])]
    ppermute x13 -> x14, waiting for transfers between devices: 14.9 us -> 19 us  [send(): return lax.ppermute(array, 'tile', [(i, target(i)) for i in range(TILES)])]
    ppermute x2 -> x1, starting transfers between devices: 4.94 us -> 1.29 us  [on_device(): lax.ppermute(pair, 'tile', [(i, j) for i, j in pairs if 0 <= j < TILES])]
    all_to_all x1, starting transfers between devices: 10.3 us -> 12.2 us  [on_device(): shares = lax.all_to_all(total, 'tile', 0, 0, axis_index_groups=SAME_CORE)]
  transfers between devices with their start and end apart: 18 -> 18, of which waited for: 11 -> 13; matrix products, arithmetic and copies ran while one was open for 2% -> 2% of each run, Pallas kernels for 4% -> 4%
where the time goes in v4:
time: 175 us; the launch traced here: 174 us
  starting transfers between devices  92.6 us (53%)
  blocking collectives  26.2 us (15%)
  waiting for transfers between devices  25.5 us (15%)
  Pallas kernels  23.1 us (13%)
  local copies, waits for them, and re-layouts  4.84 us (3%)
    ppermute x14, starting transfers between devices, send(): return lax.ppermute(array, 'tile', [(i, target(i)) for i in range(TILES)])  65.9 us
    ppermute x14, waiting for transfers between devices, send(): return lax.ppermute(array, 'tile', [(i, target(i)) for i in range(TILES)])  19 us
    all_gather x1, blocking collectives, on_device(): outer = lax.all_gather(shard, 'chan')  13.2 us
    all_gather x1, blocking collectives, on_device(): strips = lax.all_gather(strips, 'tile', axis_index_groups=ROW_CHIPS)  12.9 us
    all_to_all x1, starting transfers between devices, on_device(): shares = lax.all_to_all(total, 'tile', 0, 0, axis_index_groups=SAME_CORE)  12.2 us
    pallas_call x1, Pallas kernels, on_device(): call(forward_kernel, [((64, 1024), BF), ((256, 1408), BF), ((64, 16, 128)...  9.67 us
    all_to_all x1, starting transfers between devices, on_device(): held = lax.all_to_all(summed, 'tile', 0, 0, axis_index_groups=SAME_CORE)  8.94 us
    all_to_all x1, starting transfers between devices, on_device(): inner = lax.all_to_all(copies, 'chan', 0, 0)  4.38 us
  transfers between devices with their start and end apart: 18, of which 13 were waited for; matrix products, arithmetic and copies ran while one was open for 2% of the time, Pallas kernels for 4%

profile of v4, /device:TPU:1, one launch (start us, length us, event | category | flops | bytes accessed | tf_op | source)
XLA Modules:
  0.0 173.8 jit_solution(8797721086678265478)
XLA Ops:
  2.9 12.9 %collective-permute-start = (bf16[192,128]{1,0:T(8,128)(2,1)S(1)}, bf16[192,128]{1,0:T(8,128)(2,1)S(1)}, u32[]{:S(2)}, u32[]{:S(2)}) collective-permute-start(bf16[192,128]{1,0:T(8,128)(2,1)S(1)} %get-tuple-element.48), channel_id=1, source_target_pairs={{0,248},{4,252},{8,256},{12,260},{16,264},{20,268},{24,272},{28,27... | collective-permute-start | bytes 147464 | tf_op jit(solution)/shard_map/ppermute | solution.py:464
  15.7 4.4 %collective-permute-start.1 = (bf16[192,128]{1,0:T(8,128)(2,1)S(1)}, bf16[192,128]{1,0:T(8,128)(2,1)S(1)}, u32[]{:S(2)}, u32[]{:S(2)}) collective-permute-start(bf16[192,128]{1,0:T(8,128)(2,1)S(1)} %get-tuple-element.49), channel_id=1, source_target_pairs={{0,256},{4,260},{8,264},{12,268},{16,272},{20,276},{24,280},{28,28... | collective-permute-start | bytes 147464 | tf_op jit(solution)/shard_map/ppermute | solution.py:464
  20.1 1.9 %collective-permute-start.2 = (bf16[192,128]{1,0:T(8,128)(2,1)S(1)}, bf16[192,128]{1,0:T(8,128)(2,1)S(1)}, u32[]{:S(2)}, u32[]{:S(2)}) collective-permute-start(bf16[192,128]{1,0:T(8,128)(2,1)S(1)} %get-tuple-element.50), channel_id=1, source_target_pairs={{0,264},{4,268},{8,272},{12,276},{16,280},{20,284},{24,288},{28,29... | collective-permute-start | bytes 147464 | tf_op jit(solution)/shard_map/ppermute | solution.py:464
  22.0 1.9 %collective-permute-start.3 = (bf16[96,128]{1,0:T(8,128)(2,1)S(1)}, bf16[96,128]{1,0:T(8,128)(2,1)S(1)}, u32[]{:S(2)}, u32[]{:S(2)}) collective-permute-start(bf16[96,128]{1,0:T(8,128)(2,1)S(1)} %get-tuple-element.51), channel_id=1, source_target_pairs={{0,244},{4,272},{8,252},{12,280},{16,260},{20,288},{24,268},{28,29... | collective-permute-start | bytes 73736 | tf_op jit(solution)/shard_map/ppermute | solution.py:464
  24.0 6.5 %collective-permute-done.3.far = bf16[96,128]{1,0:T(8,128)(2,1)S(1)} collective-permute-done((bf16[96,128]{1,0:T(8,128)(2,1)S(1)}, bf16[96,128]{1,0:T(8,128)(2,1)S(1)}, u32[]{:S(2)}, u32[]{:S(2)}) %collective-permute-start.3) | collective-permute-done | bytes 24608 | tf_op jit(solution)/shard_map/ppermute | solution.py:464
  30.5 2.9 %collective-permute-start.4 = (bf16[304,128]{1,0:T(8,128)(2,1)S(1)}, bf16[304,128]{1,0:T(8,128)(2,1)S(1)}, u32[]{:S(2)}, u32[]{:S(2)}) collective-permute-start(bf16[304,128]{1,0:T(8,128)(2,1)S(1)} %fusion.1), channel_id=1, source_target_pairs={{0,4},{4,0},{8,12},{12,8},{16,20},{20,16},{24,28},{28,24},{32,36},... | collective-permute-start | bytes 233480 | tf_op jit(solution)/shard_map/ppermute | solution.py:464
  34.3 2.5 %shard_map.138 = (bf16[32,1024]{1,0:T(8,128)(2,1)S(1)}, bf16[64,512]{1,0:T(8,128)(2,1)S(1)}, bf16[64,512]{1,0:T(8,128)(2,1)S(1)}, bf16[64,128]{1,0:T(8,128)(2,1)S(1)}) custom-call(s32[1,4]{1,0:T(1,128)S(1)} %copy-done.9, s32[1,12]{1,0:T(1,128)S(1)} %copy-done.10, bf16[192,128]{1,0:T(8,128)(2,1)S(1)} %collective-permute-done.a0, ...), custom_call_target="tpu_custom_call" | custom-call | flops 1000000000 | bytes 3000000 | tf_op jit(solution)/shard_map/pallas_call | solution.py:498
  36.8 1.9 %collective-permute-start.5 = (bf16[64,512]{1,0:T(8,128)(2,1)S(1)}, bf16[64,512]{1,0:T(8,128)(2,1)S(1)}, u32[]{:S(2)}, u32[]{:S(2)}) collective-permute-start(bf16[64,512]{1,0:T(8,128)(2,1)S(1)} %get-tuple-element.57), channel_id=1, source_target_pairs={{0,4},{4,0},{8,12},{12,8},{16,20},{20,16},{24,28},{28,24},{32,36},... | collective-permute-start | bytes 196616 | tf_op jit(solution)/shard_map/ppermute | solution.py:464
  38.7 1.2 collective-permute-done.5
  39.9 1.3 collective-permute-start.6
  42.3 4.4 %all-to-all-start = ((bf16[4,128,1024]{2,1,0:T(8,128)(2,1)}), bf16[4,128,1024]{2,1,0:T(8,128)(2,1)}, u32[]{:S(2)}, u32[]{:S(2)}) async-start(bf16[4,128,1024]{2,1,0:T(8,128)(2,1)} %shard_map.140), calls=%async_computation | async-start | bytes 2097152 | tf_op jit(solution)/shard_map/all_to_all | solution.py:506
  46.7 2.2 %copy.15 = bf16[3,1152,256]{1,2,0:T(8,128)(2,1)} copy(bf16[3,1152,256]{2,1,0:T(8,128)(2,1)S(1)} %bitcast.10) | data formatting | bytes 3538944 | tf_op jit(solution)/shard_map/reshape | solution.py:507
  49.0 3.4 %collective-permute-done.6 = bf16[64,1024]{1,0:T(8,128)(2,1)S(1)} collective-permute-done((bf16[64,1024]{1,0:T(8,128)(2,1)S(1)}, bf16[64,1024]{1,0:T(8,128)(2,1)S(1)}, u32[]{:S(2)}, u32[]{:S(2)}) %collective-permute-start.6) | collective-permute-done | bytes 131104 | tf_op jit(solution)/shard_map/ppermute | solution.py:510
  52.4 12.9 %all-gather = bf16[256,1152]{1,0:T(8,128)(2,1)S(1)} all-gather(bf16[64,1152]{1,0:T(8,128)(2,1)S(1)} %pad_maximum_fusion), channel_id=2, replica_groups={{0,8,16,24},{4,12,20,28},{32,40,48,56},{36,44,52,60},{64,72,80,88},{68,..., dimensions={0}, use_global_device_ids=true | all-gather | bytes 737280 | tf_op jit(solution)/shard_map/all_gather | solution.py:513
  66.4 7.4 %collective-permute-start.7 = (bf16[64,1152]{1,0:T(8,128)(2,1)S(1)}, bf16[64,1152]{1,0:T(8,128)(2,1)S(1)}, u32[]{:S(2)}, u32[]{:S(2)}) collective-permute-start(bf16[64,1152]{1,0:T(8,128)(2,1)S(1)} %get-tuple-element.64), channel_id=1, source_target_pairs={{0,4},{4,0},{8,12},{12,8},{16,20},{20,16},{24,28},{28,24},{32,36},... | collective-permute-start | bytes 442376 | tf_op jit(solution)/shard_map/ppermute | solution.py:464
  74.8 13.2 %all-gather.1 = bf16[256,1664]{1,0:T(8,128)(2,1)} all-gather(bf16[64,1664]{1,0:T(8,128)(2,1)S(1)} %pad_add_fusion), channel_id=3, replica_groups=mesh['tile'=128,'chan'=4] {'chan'}, dimensions={0}, use_global_device_ids=true | all-gather | bytes 1064960 | tf_op jit(solution)/shard_map/all_gather | solution.py:519
  88.0 9.7 %shard_map.141 = (bf16[64,1024]{1,0:T(8,128)(2,1)}, bf16[256,1408]{1,0:T(8,128)(2,1)}, f32[64,16,128]{2,1,0:T(8,128)}, bf16[64,16,128]{2,1,0:T(8,128)(2,1)}) custom-call(bf16[4,128,1024]{2,1,0:T(8,128)(2,1)} %all-to-all-done.inner, bf16[4,64,1664]{2,1,0:T(8,128)(2,1)} %bitcast.16, bf16[3,256,1152]{2,1,0:T(8,128)(2,1)} %bitcast.15), custom_call_target="tpu_custom_call" | custom-call | flops 10000000000 | bytes 30000000 | tf_op jit(solution)/shard_map/pallas_call | solution.py:520
  97.7 4.1 %collective-permute-start.8 = (bf16[64,16,128]{2,1,0:T(8,128)(2,1)}, bf16[64,16,128]{2,1,0:T(8,128)(2,1)S(1)}, u32[]{:S(2)}, u32[]{:S(2)}) collective-permute-start(bf16[64,16,128]{2,1,0:T(8,128)(2,1)} %get-tuple-element.72), channel_id=1, source_target_pairs={{0,4},{4,0},{8,12},{12,8},{16,20},{20,16},{24,28},{28,24},{32,36},... | collective-permute-start | bytes 786440 | tf_op jit(solution)/shard_map/ppermute | solution.py:464
  101.8 1.4 collective-permute-done.8.crossed
  104.9 12.2 %all-to-all-start.1 = ((bf16[64,16,128]{2,1,0:T(8,128)(2,1)}), bf16[64,16,128]{2,1,0:T(8,128)(2,1)S(1)}, u32[]{:S(2)}, u32[]{:S(2)}) async-start(bf16[64,16,128]{2,1,0:T(8,128)(2,1)} %shard_map.142), calls=%async_computation.1 | async-start | bytes 524288 | tf_op jit(solution)/shard_map/all_to_all | solution.py:540
  117.1 4.2 %shard_map.143 = (bf16[64,1024]{1,0:T(8,128)(2,1)}, bf16[192,128]{1,0:T(8,128)(2,1)S(1)}, bf16[192,128]{1,0:T(8,128)(2,1)S(1)}, bf16[192,128]{1,0:T(8,128)(2,1)S(1)}, bf16[96,128]{1,0:T(8,128)(2,1)S(1)}) custom-call(s32[1,4]{1,0:T(1,128)S(1)} %copy-done.9, s32[1,12]{1,0:T(1,128)S(1)} %copy-done.10, bf16[256,1408]{1,0:T(8,128)(2,1)S(1)} %copy-done.12, ...), custom_call_target="tpu_custom_call" | custom-call | flops 4000000000 | bytes 12000000 | tf_op jit(solution)/shard_map/pallas_call | solution.py:541
  121.4 5.1 %collective-permute-start.9 = (bf16[192,128]{1,0:T(8,128)(2,1)S(1)}, bf16[192,128]{1,0:T(8,128)(2,1)S(1)}, u32[]{:S(2)}, u32[]{:S(2)}) collective-permute-start(bf16[192,128]{1,0:T(8,128)(2,1)S(1)} %get-tuple-element.77), channel_id=1, source_target_pairs={{0,248},{4,252},{8,256},{12,260},{16,264},{20,268},{24,272},{28,27... | collective-permute-start | bytes 147464 | tf_op jit(solution)/shard_map/ppermute | solution.py:464
  126.5 4.5 %collective-permute-start.10 = (bf16[192,128]{1,0:T(8,128)(2,1)S(1)}, bf16[192,128]{1,0:T(8,128)(2,1)S(1)}, u32[]{:S(2)}, u32[]{:S(2)}) collective-permute-start(bf16[192,128]{1,0:T(8,128)(2,1)S(1)} %get-tuple-element.78), channel_id=1, source_target_pairs={{0,256},{4,260},{8,264},{12,268},{16,272},{20,276},{24,280},{28,28... | collective-permute-start | bytes 147464 | tf_op jit(solution)/shard_map/ppermute | solution.py:464
  131.7 2.1 %collective-permute-done.10.a1 = bf16[192,128]{1,0:T(8,128)(2,1)S(1)} collective-permute-done((bf16[192,128]{1,0:T(8,128)(2,1)S(1)}, bf16[192,128]{1,0:T(8,128)(2,1)S(1)}, u32[]{:S(2)}, u32[]{:S(2)}) %collective-permute-start.10) | collective-permute-done | bytes 49184 | tf_op jit(solution)/shard_map/ppermute | solution.py:464
  133.8 3.1 %all-to-all-done.1.arrived = bf16[64,16,128]{2,1,0:T(8,128)(2,1)S(1)} async-done(((bf16[64,16,128]{2,1,0:T(8,128)(2,1)}), bf16[64,16,128]{2,1,0:T(8,128)(2,1)S(1)}, u32[]{:S(2)}, u32[]{:S(2)}) %all-to-all-start.1) | async-done | bytes 262176 | tf_op jit(solution)/shard_map/all_to_all | solution.py:540
  137.7 8.9 %all-to-all-start.2 = ((bf16[64,16,128]{2,1,0:T(8,128)(2,1)}), bf16[64,16,128]{2,1,0:T(8,128)(2,1)S(1)}, u32[]{:S(2)}, u32[]{:S(2)}) async-start(bf16[64,16,128]{2,1,0:T(8,128)(2,1)} %shard_map.144), calls=%async_computation.2 | async-start | bytes 524288 | tf_op jit(solution)/shard_map/all_to_all | solution.py:562
  146.6 5.4 %collective-permute-start.11 = (bf16[192,128]{1,0:T(8,128)(2,1)S(1)}, bf16[192,128]{1,0:T(8,128)(2,1)S(1)}, u32[]{:S(2)}, u32[]{:S(2)}) collective-permute-start(bf16[192,128]{1,0:T(8,128)(2,1)S(1)} %get-tuple-element.85), channel_id=1, source_target_pairs={{0,264},{4,268},{8,272},{12,276},{16,280},{20,284},{24,288},{28,29... | collective-permute-start | bytes 147464 | tf_op jit(solution)/shard_map/ppermute | solution.py:464
  152.1 6.1 %collective-permute-start.12 = (bf16[96,128]{1,0:T(8,128)(2,1)S(1)}, bf16[96,128]{1,0:T(8,128)(2,1)S(1)}, u32[]{:S(2)}, u32[]{:S(2)}) collective-permute-start(bf16[96,128]{1,0:T(8,128)(2,1)S(1)} %get-tuple-element.86), channel_id=1, source_target_pairs={{0,244},{4,272},{8,252},{12,280},{16,260},{20,288},{24,268},{28,29... | collective-permute-start | bytes 73736 | tf_op jit(solution)/shard_map/ppermute | solution.py:464
  158.7 3.2 %collective-permute-done.12.far = bf16[96,128]{1,0:T(8,128)(2,1)S(1)} collective-permute-done((bf16[96,128]{1,0:T(8,128)(2,1)S(1)}, bf16[96,128]{1,0:T(8,128)(2,1)S(1)}, u32[]{:S(2)}, u32[]{:S(2)}) %collective-permute-start.12) | collective-permute-done | bytes 24608 | tf_op jit(solution)/shard_map/ppermute | solution.py:464
  161.9 3.9 %collective-permute-start.13 = (bf16[288,128]{1,0:T(8,128)(2,1)S(1)}, bf16[288,128]{1,0:T(8,128)(2,1)S(1)}, u32[]{:S(2)}, u32[]{:S(2)}) collective-permute-start(bf16[288,128]{1,0:T(8,128)(2,1)S(1)} %pad_maximum_fusion.2), channel_id=1, source_target_pairs={{0,4},{4,0},{8,12},{12,8},{16,20},{20,16},{24,28},{28,24},{32,36},... | collective-permute-start | bytes 221192 | tf_op jit(solution)/shard_map/ppermute | solution.py:464
  166.7 1.4 shard_map.145
  168.2 3.5 %collective-permute-start.14 = (bf16[64,16,128]{2,1,0:T(8,128)(2,1)S(1)}, bf16[64,16,128]{2,1,0:T(8,128)(2,1)S(1)}, u32[]{:S(2)}, u32[]{:S(2)}) collective-permute-start(bf16[64,16,128]{2,1,0:T(8,128)(2,1)S(1)} %all-to-all-done.2.held), channel_id=1, source_target_pairs={{0,4},{4,0},{8,12},{12,8},{16,20},{20,16},{24,28},{28,24},{32,36},... | collective-permute-start | bytes 786440 | tf_op jit(solution)/shard_map/ppermute | solution.py:464
  (57 shorter events, 13.1 us)
Async XLA Ops:
  0.6 0.8 copy-start.4
  1.5 0.7 copy-start.5
  2.2 21.8 %copy-start.7 = (s32[1,8]{1,0:T(1,128)S(1)}, s32[1,8]{1,0:T(1,128)}, u32[]{:S(2)}) copy-start(s32[1,8]{1,0:T(1,128)} %own_near.1) | copy-start | bytes 100
  2.2 32.1 %copy-start.1 = (bf16[12,128,128]{2,1,0:T(8,128)(2,1)S(1)}, bf16[12,128,128]{2,1,0:T(8,128)(2,1)}, u32[]{:S(2)}) copy-start(bf16[12,128,128]{2,1,0:T(8,128)(2,1)} %regrid_held.1) | copy-start | bytes 1179652
  2.2 32.1 %copy-start.2 = (bf16[64,1024]{1,0:T(8,128)(2,1)S(1)}, bf16[64,1024]{1,0:T(8,128)(2,1)}, u32[]{:S(2)}) copy-start(bf16[64,1024]{1,0:T(8,128)(2,1)} %atm.2) | copy-start | bytes 393220
  2.2 32.1 %copy-start.3 = (bf16[64,1024]{1,0:T(8,128)(2,1)S(1)}, bf16[64,1024]{1,0:T(8,128)(2,1)}, u32[]{:S(2)}) copy-start(bf16[64,1024]{1,0:T(8,128)(2,1)} %grad_held.1) | copy-start | bytes 393220
  2.2 32.1 %copy-start.9 = (s32[1,4]{1,0:T(1,128)S(1)}, s32[1,4]{1,0:T(1,128)}, u32[]{:S(2)}) copy-start(s32[1,4]{1,0:T(1,128)} %sources.3) | copy-start | bytes 52
  2.2 32.1 %copy-start.10 = (s32[1,12]{1,0:T(1,128)S(1)}, s32[1,12]{1,0:T(1,128)}, u32[]{:S(2)}) copy-start(s32[1,12]{1,0:T(1,128)} %blocks.3) | copy-start | bytes 148
  2.9 27.6 %collective-permute-start = (bf16[192,128]{1,0:T(8,128)(2,1)S(1)}, bf16[192,128]{1,0:T(8,128)(2,1)S(1)}, u32[]{:S(2)}, u32[]{:S(2)}) collective-permute-start(bf16[192,128]{1,0:T(8,128)(2,1)S(1)} %get-tuple-element.48), channel_id=1, source_target_pairs={{0,248},{4,252},{8,256},{12,260},{16,264},{20,268},{24,272},{28,27... | collective-permute-start | bytes 147464 | tf_op jit(solution)/shard_map/ppermute | solution.py:464
  15.7 14.7 %collective-permute-start.1 = (bf16[192,128]{1,0:T(8,128)(2,1)S(1)}, bf16[192,128]{1,0:T(8,128)(2,1)S(1)}, u32[]{:S(2)}, u32[]{:S(2)}) collective-permute-start(bf16[192,128]{1,0:T(8,128)(2,1)S(1)} %get-tuple-element.49), channel_id=1, source_target_pairs={{0,256},{4,260},{8,264},{12,268},{16,272},{20,276},{24,280},{28,28... | collective-permute-start | bytes 147464 | tf_op jit(solution)/shard_map/ppermute | solution.py:464
  20.1 10.4 %collective-permute-start.2 = (bf16[192,128]{1,0:T(8,128)(2,1)S(1)}, bf16[192,128]{1,0:T(8,128)(2,1)S(1)}, u32[]{:S(2)}, u32[]{:S(2)}) collective-permute-start(bf16[192,128]{1,0:T(8,128)(2,1)S(1)} %get-tuple-element.50), channel_id=1, source_target_pairs={{0,264},{4,268},{8,272},{12,276},{16,280},{20,284},{24,288},{28,29... | collective-permute-start | bytes 147464 | tf_op jit(solution)/shard_map/ppermute | solution.py:464
  22.0 8.4 %collective-permute-start.3 = (bf16[96,128]{1,0:T(8,128)(2,1)S(1)}, bf16[96,128]{1,0:T(8,128)(2,1)S(1)}, u32[]{:S(2)}, u32[]{:S(2)}) collective-permute-start(bf16[96,128]{1,0:T(8,128)(2,1)S(1)} %get-tuple-element.51), channel_id=1, source_target_pairs={{0,244},{4,272},{8,252},{12,280},{16,260},{20,288},{24,268},{28,29... | collective-permute-start | bytes 73736 | tf_op jit(solution)/shard_map/ppermute | solution.py:464
  30.5 3.8 %collective-permute-start.4 = (bf16[304,128]{1,0:T(8,128)(2,1)S(1)}, bf16[304,128]{1,0:T(8,128)(2,1)S(1)}, u32[]{:S(2)}, u32[]{:S(2)}) collective-permute-start(bf16[304,128]{1,0:T(8,128)(2,1)S(1)} %fusion.1), channel_id=1, source_target_pairs={{0,4},{4,0},{8,12},{12,8},{16,20},{20,16},{24,28},{28,24},{32,36},... | collective-permute-start | bytes 233480 | tf_op jit(solution)/shard_map/ppermute | solution.py:464
  36.8 3.1 %collective-permute-start.5 = (bf16[64,512]{1,0:T(8,128)(2,1)S(1)}, bf16[64,512]{1,0:T(8,128)(2,1)S(1)}, u32[]{:S(2)}, u32[]{:S(2)}) collective-permute-start(bf16[64,512]{1,0:T(8,128)(2,1)S(1)} %get-tuple-element.57), channel_id=1, source_target_pairs={{0,4},{4,0},{8,12},{12,8},{16,20},{20,16},{24,28},{28,24},{32,36},... | collective-permute-start | bytes 196616 | tf_op jit(solution)/shard_map/ppermute | solution.py:464
  39.9 12.4 %collective-permute-start.6 = (bf16[64,1024]{1,0:T(8,128)(2,1)S(1)}, bf16[64,1024]{1,0:T(8,128)(2,1)S(1)}, u32[]{:S(2)}, u32[]{:S(2)}) collective-permute-start(bf16[64,1024]{1,0:T(8,128)(2,1)S(1)} %pad_maximum_fusion.1), channel_id=1, source_target_pairs={{0,32},{8,40},{16,48},{24,56},{32,64},{36,4},{40,72},{44,12},{48,8... | collective-permute-start | bytes 393224 | tf_op jit(solution)/shard_map/ppermute | solution.py:510
  42.3 4.4 %copy-start = (bf16[9,384,256]{2,1,0:T(8,128)(2,1)S(1)}, bf16[9,384,256]{2,1,0:T(8,128)(2,1)}, u32[]{:S(2)}) copy-start(bf16[9,384,256]{2,1,0:T(8,128)(2,1)} %weights_held.1) | copy-start | bytes 5308420
  42.3 32.5 %all-to-all-start = ((bf16[4,128,1024]{2,1,0:T(8,128)(2,1)}), bf16[4,128,1024]{2,1,0:T(8,128)(2,1)}, u32[]{:S(2)}, u32[]{:S(2)}) async-start(bf16[4,128,1024]{2,1,0:T(8,128)(2,1)} %shard_map.140), calls=%async_computation | async-start | bytes 2097152 | tf_op jit(solution)/shard_map/all_to_all | solution.py:506
  46.7 18.6 %copy-start.8 = (f32[64]{0:T(128)S(1)}, f32[64]{0:T(128)}, u32[]{:S(2)}) copy-start(f32[64]{0:T(128)} %param.13) | copy-start | bytes 772
  66.4 8.4 %collective-permute-start.7 = (bf16[64,1152]{1,0:T(8,128)(2,1)S(1)}, bf16[64,1152]{1,0:T(8,128)(2,1)S(1)}, u32[]{:S(2)}, u32[]{:S(2)}) collective-permute-start(bf16[64,1152]{1,0:T(8,128)(2,1)S(1)} %get-tuple-element.64), channel_id=1, source_target_pairs={{0,4},{4,0},{8,12},{12,8},{16,20},{20,16},{24,28},{28,24},{32,36},... | collective-permute-start | bytes 442376 | tf_op jit(solution)/shard_map/ppermute | solution.py:464
  97.7 5.4 %collective-permute-start.8 = (bf16[64,16,128]{2,1,0:T(8,128)(2,1)}, bf16[64,16,128]{2,1,0:T(8,128)(2,1)S(1)}, u32[]{:S(2)}, u32[]{:S(2)}) collective-permute-start(bf16[64,16,128]{2,1,0:T(8,128)(2,1)} %get-tuple-element.72), channel_id=1, source_target_pairs={{0,4},{4,0},{8,12},{12,8},{16,20},{20,16},{24,28},{28,24},{32,36},... | collective-permute-start | bytes 786440 | tf_op jit(solution)/shard_map/ppermute | solution.py:464
  103.1 1.0 copy-start.11
  104.2 12.9 %copy-start.12 = (bf16[256,1408]{1,0:T(8,128)(2,1)S(1)}, bf16[256,1408]{1,0:T(8,128)(2,1)}, u32[]{:S(2)}) copy-start(bf16[256,1408]{1,0:T(8,128)(2,1)} %get-tuple-element.74.z_all) | copy-start | bytes 2162692
  104.9 32.0 %all-to-all-start.1 = ((bf16[64,16,128]{2,1,0:T(8,128)(2,1)}), bf16[64,16,128]{2,1,0:T(8,128)(2,1)S(1)}, u32[]{:S(2)}, u32[]{:S(2)}) async-start(bf16[64,16,128]{2,1,0:T(8,128)(2,1)} %shard_map.142), calls=%async_computation.1 | async-start | bytes 524288 | tf_op jit(solution)/shard_map/all_to_all | solution.py:540
  121.4 10.3 %collective-permute-start.9 = (bf16[192,128]{1,0:T(8,128)(2,1)S(1)}, bf16[192,128]{1,0:T(8,128)(2,1)S(1)}, u32[]{:S(2)}, u32[]{:S(2)}) collective-permute-start(bf16[192,128]{1,0:T(8,128)(2,1)S(1)} %get-tuple-element.77), channel_id=1, source_target_pairs={{0,248},{4,252},{8,256},{12,260},{16,264},{20,268},{24,272},{28,27... | collective-permute-start | bytes 147464 | tf_op jit(solution)/shard_map/ppermute | solution.py:464
  126.5 7.3 %collective-permute-start.10 = (bf16[192,128]{1,0:T(8,128)(2,1)S(1)}, bf16[192,128]{1,0:T(8,128)(2,1)S(1)}, u32[]{:S(2)}, u32[]{:S(2)}) collective-permute-start(bf16[192,128]{1,0:T(8,128)(2,1)S(1)} %get-tuple-element.78), channel_id=1, source_target_pairs={{0,256},{4,260},{8,264},{12,268},{16,272},{20,276},{24,280},{28,28... | collective-permute-start | bytes 147464 | tf_op jit(solution)/shard_map/ppermute | solution.py:464
  136.9 29.8 %copy-start.6 = (s32[1,128,3]{1,0,2:T(1,128)S(1)}, s32[1,128,3]{1,0,2:T(1,128)}, u32[]{:S(2)}) copy-start(s32[1,128,3]{1,0,2:T(1,128)} %param.19) | copy-start | bytes 4612
  137.7 30.5 %all-to-all-start.2 = ((bf16[64,16,128]{2,1,0:T(8,128)(2,1)}), bf16[64,16,128]{2,1,0:T(8,128)(2,1)S(1)}, u32[]{:S(2)}, u32[]{:S(2)}) async-start(bf16[64,16,128]{2,1,0:T(8,128)(2,1)} %shard_map.144), calls=%async_computation.2 | async-start | bytes 524288 | tf_op jit(solution)/shard_map/all_to_all | solution.py:562
  146.6 12.1 %collective-permute-start.11 = (bf16[192,128]{1,0:T(8,128)(2,1)S(1)}, bf16[192,128]{1,0:T(8,128)(2,1)S(1)}, u32[]{:S(2)}, u32[]{:S(2)}) collective-permute-start(bf16[192,128]{1,0:T(8,128)(2,1)S(1)} %get-tuple-element.85), channel_id=1, source_target_pairs={{0,264},{4,268},{8,272},{12,276},{16,280},{20,284},{24,288},{28,29... | collective-permute-start | bytes 147464 | tf_op jit(solution)/shard_map/ppermute | solution.py:464
  152.1 9.9 %collective-permute-start.12 = (bf16[96,128]{1,0:T(8,128)(2,1)S(1)}, bf16[96,128]{1,0:T(8,128)(2,1)S(1)}, u32[]{:S(2)}, u32[]{:S(2)}) collective-permute-start(bf16[96,128]{1,0:T(8,128)(2,1)S(1)} %get-tuple-element.86), channel_id=1, source_target_pairs={{0,244},{4,272},{8,252},{12,280},{16,260},{20,288},{24,268},{28,29... | collective-permute-start | bytes 73736 | tf_op jit(solution)/shard_map/ppermute | solution.py:464
  161.9 4.8 %collective-permute-start.13 = (bf16[288,128]{1,0:T(8,128)(2,1)S(1)}, bf16[288,128]{1,0:T(8,128)(2,1)S(1)}, u32[]{:S(2)}, u32[]{:S(2)}) collective-permute-start(bf16[288,128]{1,0:T(8,128)(2,1)S(1)} %pad_maximum_fusion.2), channel_id=1, source_target_pairs={{0,4},{4,0},{8,12},{12,8},{16,20},{20,16},{24,28},{28,24},{32,36},... | collective-permute-start | bytes 221192 | tf_op jit(solution)/shard_map/ppermute | solution.py:464
  168.2 4.7 %collective-permute-start.14 = (bf16[64,16,128]{2,1,0:T(8,128)(2,1)S(1)}, bf16[64,16,128]{2,1,0:T(8,128)(2,1)S(1)}, u32[]{:S(2)}, u32[]{:S(2)}) collective-permute-start(bf16[64,16,128]{2,1,0:T(8,128)(2,1)S(1)} %all-to-all-done.2.held), channel_id=1, source_target_pairs={{0,4},{4,0},{8,12},{12,8},{16,20},{20,16},{24,28},{28,24},{32,36},... | collective-permute-start | bytes 786440 | tf_op jit(solution)/shard_map/ppermute | solution.py:464

commit v5 on v4

--- a/solution.py
+++ b/solution.py
@@ -144,13 +144,18 @@
     parcel(outs[3], 0, -3 * facing)
 
 
-def copies_kernel(atm, grad, copies):
+def copies_kernel(atm, grad, regridded, copies):
     for chan in range(4):
         copies[chan, 0:64] = atm[...]
         copies[chan, 64:128] = grad[...]
-
-
-def regrid_kernel(sources, blocks, a0, a1, a2, crossed, far, weights, atm, grad, regridded, keep, give, sides, held, acc):
+        copies[chan, 128:160] = regridded[...]
+
+
+def edges_kernel(atm, grad, edges):
+    edges[...] = dot(atm[...], edge_table(0)) + dot(grad[...], grad_edge_table())
+
+
+def regrid_kernel(sources, blocks, a0, a1, a2, crossed, far, weights, atm, grad, edges, regridded, keep, give, sides, held, acc):
     tile = lax.axis_index("tile")
     facing = 1 - 2 * (tile & 1)
     for i, ref in enumerate((a0, a1, a2)):
@@ -198,12 +203,11 @@
         north(keep)
         south(give)
 
-    edges = dot(atm[...], edge_table(0)) + dot(grad[...], grad_edge_table())
-    sides[0:32, :] = (edges[0:32] + dot(regridded[...], edge_table(64))).astype(BF)
-    sides[32:64, :] = edges[32:64].astype(BF)
-
-
-def select_kernel(own_near, mate_near, gathered, regridded, bias, own, mate):
+    sides[0:32, :] = (edges[0:32, :] + dot(regridded[...], edge_table(64))).astype(BF)
+    sides[32:64, :] = edges[32:64, :].astype(BF)
+
+
+def select_kernel(own_near, mate_near, gathered, bias, own, mate):
     core = lax.axis_index("tile") & 1
     for near, out in ((own_near, own), (mate_near, mate)):
 
@@ -250,8 +254,6 @@
         side = jnp.where(lane == BIAS0 + i, part, side)
         rest = rest - part
     own[:, 1024:1152] = side.astype(BF)
-    own[0:32, 1152:1664] = regridded[:, 0:512]
-    own[32:64, 1152:1664] = regridded[:, 512:1024]
 
 
 def forward_kernel(
@@ -264,7 +266,9 @@
         state = taps.at[pl.ds(384 + 64 * c, 64), pl.ds(256, 1024)]
         fetches.append(pltpu.make_async_copy(inner.at[c, pl.ds(0, 64)], state, sems.at[1 + c]))
         fetches.append(pltpu.make_async_copy(inner.at[c, pl.ds(64, 64)], grads.at[own, pl.ds(128, 1024)], sems.at[5 + c]))
-    fetches.append(pltpu.make_async_copy(flipped, weights, sems.at[9]))
+        sea = taps.at[pl.ds(640 + 32 * c, 32), pl.ds(256, 1024)]
+        fetches.append(pltpu.make_async_copy(inner.at[c, pl.ds(128, 32)], sea, sems.at[9 + c]))
+    fetches.append(pltpu.make_async_copy(flipped, weights, sems.at[13]))
     for fetch in fetches:
         fetch.start()
     fetches[0].wait()
@@ -278,8 +282,6 @@
         side_atm[atm, :] = outer[c, :, 1024:1152]
         taps[sea, 0:128] = outer[c, 0:32, 384:512]
         taps[sea, 128:256] = outer[c, 32:64, 384:512]
-        taps[sea, 256:768] = outer[c, 0:32, 1152:1664]
-        taps[sea, 768:1280] = outer[c, 32:64, 1152:1664]
         taps[sea, 1280:1408] = outer[c, 0:32, 896:1024]
         taps[sea, 1408:1536] = outer[c, 32:64, 896:1024]
         side = dot(outer[c, 0:32, 1024:1152], ocean_side_table(0)) + dot(outer[c, 32:64, 1024:1152], ocean_side_table(1))
@@ -288,7 +290,7 @@
         grads[atm, 1152:1280] = outer[c, :, 768:896]
         side = outer[c, :, 1024:1152]
         grads[atm, 1280:1408] = jnp.where((lane >= OG0) & (lane < OC0), side, jnp.zeros_like(side))
-    for fetch in fetches[1:9]:
+    for fetch in fetches[1:13]:
         fetch.wait()
     side = side_atm[...]
     shifts, edges = shift_tables(), edge_rows()
@@ -310,7 +312,7 @@
         [jnp.sum(outer[c, :, 1024 + BIAS0 : 1024 + BIAS0 + 3].astype(F32), axis=1, keepdims=True) for c in range(4)], axis=0
     )
 
-    fetches[9].wait()
+    fetches[13].wait()
 
     def activate(total, lanes):
         pre = total + bias
@@ -491,30 +493,30 @@
     sends = jnp.transpose(coupling_sends, (2, 0, 1))
     b0, b1, b2, far = call(parcels_kernel, [((192, 128), BF)] * 3 + [((96, 128), BF)], [SMEM, VMEM])(sends, ocean_state)
     a0, a1, a2, far = chip_send(b0, 0), chip_send(b1, 1), chip_send(b2, 2), far_send(far)
-    a0, a1, a2, far = lax.optimization_barrier((a0, a1, a2, far))
+    flipped = jnp.swapaxes(conv_weight.reshape(3, 1152, 256), 1, 2)
+    a0, a1, a2, far, flipped = lax.optimization_barrier((a0, a1, a2, far, flipped))
     table = jnp.pad(atm_neighbours.astype(BF), ((0, 15), (0, 120)))
     crossed = to_mate(jnp.concatenate([a0[96:], a1[96:], a2[96:], table], axis=0))
     mate_near = crossed[288:289, 0:8].astype(jnp.int32)
+    (edges,) = call(edges_kernel, [((64, 128), F32)], [VMEM, VMEM])(atm_state, out_grad)
     regridded, keep, give, sides = call(
         regrid_kernel,
         [((32, 1024), BF), ((64, 512), BF), ((64, 512), BF), ((64, 128), BF)],
-        [SMEM] * 2 + [VMEM] * 8,
+        [SMEM] * 2 + [VMEM] * 9,
         [pltpu.VMEM((672, 128), BF), pltpu.VMEM((256, 128), F32)],
-    )(coupling_sources, coupling_blocks, a0, a1, a2, crossed, far, regrid_weight, atm_state, out_grad)
-    got, weights_now, atm_now, grad_now = lax.optimization_barrier((to_mate(give), conv_weight, atm_state, out_grad))
-    (copies,) = call(copies_kernel, [((4, 128, 1024), BF)], [VMEM, VMEM])(atm_now, grad_now)
+    )(coupling_sources, coupling_blocks, a0, a1, a2, crossed, far, regrid_weight, atm_state, out_grad, edges)
+    got, atm_now, grad_now = lax.optimization_barrier((to_mate(give), atm_state, out_grad))
+    (copies,) = call(copies_kernel, [((4, 160, 1024), BF)], [VMEM] * 3)(atm_now, grad_now, regridded)
     inner = lax.all_to_all(copies, "chan", 0, 0)
-    flipped = jnp.swapaxes(weights_now.reshape(3, 1152, 256), 1, 2)
     pair = jnp.concatenate([keep, got], axis=1)
     pairs = [(i, i + 8 - 16 * (i % 2)) for i in range(TILES)]
     arrived = lax.ppermute(pair, "tile", [(i, j) for i, j in pairs if 0 <= j < TILES])
     strips = jnp.concatenate([arrived, sides], axis=1)
-    strips, flipped = lax.optimization_barrier((strips, flipped))
     strips = lax.all_gather(strips, "tile", axis_index_groups=ROW_CHIPS)
-    own, mate = call(select_kernel, [((64, 1664), BF), ((64, 1152), BF)], [SMEM] * 2 + [VMEM] * 3)(
-        atm_neighbours, mate_near, strips, regridded, conv_bias.reshape(1, 64)
+    own, mate = call(select_kernel, [((64, 1152), BF)] * 2, [SMEM] * 2 + [VMEM] * 2, cost=12)(
+        atm_neighbours, mate_near, strips, conv_bias.reshape(1, 64)
     )
-    shard = own + jnp.pad(to_mate(mate), ((0, 0), (0, 512)))
+    shard = own + to_mate(mate)
     shard, inner = lax.optimization_barrier((shard, inner))
     outer = lax.all_gather(shard, "chan")
     atm_output, z_all, mine, theirs = call(
@@ -528,9 +530,9 @@
             pltpu.VMEM((256, 1408), BF),
             pltpu.VMEM((256, 1024), BF),
             pltpu.VMEM((3, 256, 1152), BF),
-            pltpu.VMEM((4, 64, 1664), BF),
+            pltpu.VMEM((4, 64, 1152), BF),
             pltpu.VMEM((192, 1536), BF),
-            pltpu.SemaphoreType.DMA((10,)),
+            pltpu.SemaphoreType.DMA((14,)),
         ],
         limit=56,
         cost=10,

time: 175 us -> 174 us (level)
    ppermute x14, starting transfers between devices: 65.9 us -> 61.4 us  [send(): return lax.ppermute(array, 'tile', [(i, target(i)) for i in range(TILES)])]
    all_to_all x1, starting transfers between devices: 12.2 us -> 14.9 us  [on_device(): shares = lax.all_to_all(total, 'tile', 0, 0, axis_index_groups=SAME_CORE)]
    ppermute x1, waiting for transfers between devices: 3.43 us -> 5.9 us  [on_device(): lax.ppermute(pair, 'tile', [(i, j) for i, j in pairs if 0 <= j < TILES])]
    ppermute x14, waiting for transfers between devices: 19 us -> 16.6 us  [send(): return lax.ppermute(array, 'tile', [(i, target(i)) for i in range(TILES)])]
  transfers between devices with their start and end apart: 18 -> 18, of which waited for: 13 -> 13; matrix products, arithmetic and copies ran while one was open for 2% -> 2% of each run, Pallas kernels for 4% -> 5%
where the time goes in v5:
time: 174 us; the launch traced here: 173 us
  starting transfers between devices  90.9 us (52%)
  blocking collectives  26.7 us (15%)
  waiting for transfers between devices  25.6 us (15%)
  Pallas kernels  23.3 us (13%)
  local copies, waits for them, and re-layouts  4.85 us (3%)
    ppermute x14, starting transfers between devices, send(): return lax.ppermute(array, 'tile', [(i, target(i)) for i in range(TILES)])  61.4 us
    ppermute x14, waiting for transfers between devices, send(): return lax.ppermute(array, 'tile', [(i, target(i)) for i in range(TILES)])  16.6 us
    all_to_all x1, starting transfers between devices, on_device(): shares = lax.all_to_all(total, 'tile', 0, 0, axis_index_groups=SAME_CORE)  14.9 us
    all_gather x1, blocking collectives, on_device(): strips = lax.all_gather(strips, 'tile', axis_index_groups=ROW_CHIPS)  14.4 us
    all_gather x1, blocking collectives, on_device(): outer = lax.all_gather(shard, 'chan')  12.3 us
    pallas_call x1, Pallas kernels, on_device(): call(forward_kernel, [((64, 1024), BF), ((256, 1408), BF), ((64, 16, 128)...  9.69 us
    all_to_all x1, starting transfers between devices, on_device(): held = lax.all_to_all(summed, 'tile', 0, 0, axis_index_groups=SAME_CORE)  8.94 us
    ppermute x1, waiting for transfers between devices, on_device(): lax.ppermute(pair, 'tile', [(i, j) for i, j in pairs if 0 <= j < TILES])  5.9 us
  transfers between devices with their start and end apart: 18, of which 13 were waited for; matrix products, arithmetic and copies ran while one was open for 2% of the time, Pallas kernels for 5%

profile of v5, /device:TPU:1, one launch (start us, length us, event | category | flops | bytes accessed | tf_op | source)
XLA Modules:
  0.0 173.0 jit_solution(13152818066235872524)
XLA Ops:
  2.8 12.9 %collective-permute-start = (bf16[192,128]{1,0:T(8,128)(2,1)S(1)}, bf16[192,128]{1,0:T(8,128)(2,1)S(1)}, u32[]{:S(2)}, u32[]{:S(2)}) collective-permute-start(bf16[192,128]{1,0:T(8,128)(2,1)S(1)} %get-tuple-element.46), channel_id=1, source_target_pairs={{0,248},{4,252},{8,256},{12,260},{16,264},{20,268},{24,272},{28,27... | collective-permute-start | bytes 147464 | tf_op jit(solution)/shard_map/ppermute | solution.py:466
  15.7 4.4 %collective-permute-start.1 = (bf16[192,128]{1,0:T(8,128)(2,1)S(1)}, bf16[192,128]{1,0:T(8,128)(2,1)S(1)}, u32[]{:S(2)}, u32[]{:S(2)}) collective-permute-start(bf16[192,128]{1,0:T(8,128)(2,1)S(1)} %get-tuple-element.47), channel_id=1, source_target_pairs={{0,256},{4,260},{8,264},{12,268},{16,272},{20,276},{24,280},{28,28... | collective-permute-start | bytes 147464 | tf_op jit(solution)/shard_map/ppermute | solution.py:466
  20.1 1.9 %collective-permute-start.2 = (bf16[192,128]{1,0:T(8,128)(2,1)S(1)}, bf16[192,128]{1,0:T(8,128)(2,1)S(1)}, u32[]{:S(2)}, u32[]{:S(2)}) collective-permute-start(bf16[192,128]{1,0:T(8,128)(2,1)S(1)} %get-tuple-element.48), channel_id=1, source_target_pairs={{0,264},{4,268},{8,272},{12,276},{16,280},{20,284},{24,288},{28,29... | collective-permute-start | bytes 147464 | tf_op jit(solution)/shard_map/ppermute | solution.py:466
  22.0 1.9 %collective-permute-start.3 = (bf16[96,128]{1,0:T(8,128)(2,1)S(1)}, bf16[96,128]{1,0:T(8,128)(2,1)S(1)}, u32[]{:S(2)}, u32[]{:S(2)}) collective-permute-start(bf16[96,128]{1,0:T(8,128)(2,1)S(1)} %get-tuple-element.49), channel_id=1, source_target_pairs={{0,244},{4,272},{8,252},{12,280},{16,260},{20,288},{24,268},{28,29... | collective-permute-start | bytes 73736 | tf_op jit(solution)/shard_map/ppermute | solution.py:466
  24.0 2.2 %copy.15 = bf16[3,1152,256]{1,2,0:T(8,128)(2,1)} copy(bf16[3,1152,256]{2,1,0:T(8,128)(2,1)S(1)} %bitcast.10) | data formatting | bytes 3538944 | tf_op jit(solution)/shard_map/reshape | solution.py:496
  26.2 4.2 %collective-permute-done.3.far = bf16[96,128]{1,0:T(8,128)(2,1)S(1)} collective-permute-done((bf16[96,128]{1,0:T(8,128)(2,1)S(1)}, bf16[96,128]{1,0:T(8,128)(2,1)S(1)}, u32[]{:S(2)}, u32[]{:S(2)}) %collective-permute-start.3) | collective-permute-done | bytes 24608 | tf_op jit(solution)/shard_map/ppermute | solution.py:466
  30.6 3.0 %collective-permute-start.4 = (bf16[304,128]{1,0:T(8,128)(2,1)S(1)}, bf16[304,128]{1,0:T(8,128)(2,1)S(1)}, u32[]{:S(2)}, u32[]{:S(2)}) collective-permute-start(bf16[304,128]{1,0:T(8,128)(2,1)S(1)} %fusion.1), channel_id=1, source_target_pairs={{0,4},{4,0},{8,12},{12,8},{16,20},{20,16},{24,28},{28,24},{32,36},... | collective-permute-start | bytes 233480 | tf_op jit(solution)/shard_map/ppermute | solution.py:466
  34.4 2.3 %shard_map.139 = (bf16[32,1024]{1,0:T(8,128)(2,1)S(1)}, bf16[64,512]{1,0:T(8,128)(2,1)S(1)}, bf16[64,512]{1,0:T(8,128)(2,1)S(1)}, bf16[64,128]{1,0:T(8,128)(2,1)S(1)}) custom-call(s32[1,4]{1,0:T(1,128)S(1)} %copy-done.9, s32[1,12]{1,0:T(1,128)S(1)} %copy-done.10, bf16[192,128]{1,0:T(8,128)(2,1)S(1)} %collective-permute-done.a0, ...), custom_call_target="tpu_custom_call" | custom-call | flops 1000000000 | bytes 3000000 | tf_op jit(solution)/shard_map/pallas_call | solution.py:502
  36.8 1.9 %collective-permute-start.5 = (bf16[64,512]{1,0:T(8,128)(2,1)S(1)}, bf16[64,512]{1,0:T(8,128)(2,1)S(1)}, u32[]{:S(2)}, u32[]{:S(2)}) collective-permute-start(bf16[64,512]{1,0:T(8,128)(2,1)S(1)} %get-tuple-element.55), channel_id=1, source_target_pairs={{0,4},{4,0},{8,12},{12,8},{16,20},{20,16},{24,28},{28,24},{32,36},... | collective-permute-start | bytes 196616 | tf_op jit(solution)/shard_map/ppermute | solution.py:466
  38.7 1.2 collective-permute-done.5
  40.0 1.3 collective-permute-start.6
  42.4 4.4 %all-to-all-start = ((bf16[4,160,1024]{2,1,0:T(8,128)(2,1)}), bf16[4,160,1024]{2,1,0:T(8,128)(2,1)}, u32[]{:S(2)}, u32[]{:S(2)}) async-start(bf16[4,160,1024]{2,1,0:T(8,128)(2,1)} %shard_map.141), calls=%async_computation | async-start | bytes 2621440 | tf_op jit(solution)/shard_map/all_to_all | solution.py:510
  46.9 5.9 %collective-permute-done.6 = bf16[64,1024]{1,0:T(8,128)(2,1)S(1)} collective-permute-done((bf16[64,1024]{1,0:T(8,128)(2,1)S(1)}, bf16[64,1024]{1,0:T(8,128)(2,1)S(1)}, u32[]{:S(2)}, u32[]{:S(2)}) %collective-permute-start.6) | collective-permute-done | bytes 131104 | tf_op jit(solution)/shard_map/ppermute | solution.py:513
  52.8 14.4 %all-gather = bf16[256,1152]{1,0:T(8,128)(2,1)S(1)} all-gather(bf16[64,1152]{1,0:T(8,128)(2,1)S(1)} %pad_maximum_fusion), channel_id=2, replica_groups={{0,8,16,24},{4,12,20,28},{32,40,48,56},{36,44,52,60},{64,72,80,88},{68,..., dimensions={0}, use_global_device_ids=true | all-gather | bytes 737280 | tf_op jit(solution)/shard_map/all_gather | solution.py:515
  68.2 2.1 %collective-permute-start.7 = (bf16[64,1152]{1,0:T(8,128)(2,1)S(1)}, bf16[64,1152]{1,0:T(8,128)(2,1)S(1)}, u32[]{:S(2)}, u32[]{:S(2)}) collective-permute-start(bf16[64,1152]{1,0:T(8,128)(2,1)S(1)} %get-tuple-element.59), channel_id=1, source_target_pairs={{0,4},{4,0},{8,12},{12,8},{16,20},{20,16},{24,28},{28,24},{32,36},... | collective-permute-start | bytes 442376 | tf_op jit(solution)/shard_map/ppermute | solution.py:466
  71.5 12.3 %all-gather.1 = bf16[256,1152]{1,0:T(8,128)(2,1)} all-gather(bf16[64,1152]{1,0:T(8,128)(2,1)S(1)} %add.5), channel_id=3, replica_groups=mesh['tile'=128,'chan'=4] {'chan'}, dimensions={0}, use_global_device_ids=true | all-gather | bytes 737280 | tf_op jit(solution)/shard_map/all_gather | solution.py:521
  83.8 9.7 %shard_map.142 = (bf16[64,1024]{1,0:T(8,128)(2,1)}, bf16[256,1408]{1,0:T(8,128)(2,1)}, f32[64,16,128]{2,1,0:T(8,128)}, bf16[64,16,128]{2,1,0:T(8,128)(2,1)}) custom-call(bf16[4,160,1024]{2,1,0:T(8,128)(2,1)} %all-to-all-done.inner, bf16[4,64,1152]{2,1,0:T(8,128)(2,1)} %bitcast.16, bf16[3,256,1152]{2,1,0:T(8,128)(2,1)} %bitcast.15), custom_call_target="tpu_custom_call" | custom-call | flops 10000000000 | bytes 30000000 | tf_op jit(solution)/shard_map/pallas_call | solution.py:522
  93.5 4.7 %collective-permute-start.8 = (bf16[64,16,128]{2,1,0:T(8,128)(2,1)}, bf16[64,16,128]{2,1,0:T(8,128)(2,1)S(1)}, u32[]{:S(2)}, u32[]{:S(2)}) collective-permute-start(bf16[64,16,128]{2,1,0:T(8,128)(2,1)} %get-tuple-element.68), channel_id=1, source_target_pairs={{0,4},{4,0},{8,12},{12,8},{16,20},{20,16},{24,28},{28,24},{32,36},... | collective-permute-start | bytes 786440 | tf_op jit(solution)/shard_map/ppermute | solution.py:466
  98.2 1.4 collective-permute-done.8.crossed
  101.3 14.9 %all-to-all-start.1 = ((bf16[64,16,128]{2,1,0:T(8,128)(2,1)}), bf16[64,16,128]{2,1,0:T(8,128)(2,1)S(1)}, u32[]{:S(2)}, u32[]{:S(2)}) async-start(bf16[64,16,128]{2,1,0:T(8,128)(2,1)} %shard_map.143), calls=%async_computation.1 | async-start | bytes 524288 | tf_op jit(solution)/shard_map/all_to_all | solution.py:542
  116.2 4.2 %shard_map.144 = (bf16[64,1024]{1,0:T(8,128)(2,1)}, bf16[192,128]{1,0:T(8,128)(2,1)S(1)}, bf16[192,128]{1,0:T(8,128)(2,1)S(1)}, bf16[192,128]{1,0:T(8,128)(2,1)S(1)}, bf16[96,128]{1,0:T(8,128)(2,1)S(1)}) custom-call(s32[1,4]{1,0:T(1,128)S(1)} %copy-done.9, s32[1,12]{1,0:T(1,128)S(1)} %copy-done.10, bf16[256,1408]{1,0:T(8,128)(2,1)S(1)} %copy-done.12, ...), custom_call_target="tpu_custom_call" | custom-call | flops 4000000000 | bytes 12000000 | tf_op jit(solution)/shard_map/pallas_call | solution.py:543
  120.5 5.1 %collective-permute-start.9 = (bf16[192,128]{1,0:T(8,128)(2,1)S(1)}, bf16[192,128]{1,0:T(8,128)(2,1)S(1)}, u32[]{:S(2)}, u32[]{:S(2)}) collective-permute-start(bf16[192,128]{1,0:T(8,128)(2,1)S(1)} %get-tuple-element.73), channel_id=1, source_target_pairs={{0,248},{4,252},{8,256},{12,260},{16,264},{20,268},{24,272},{28,27... | collective-permute-start | bytes 147464 | tf_op jit(solution)/shard_map/ppermute | solution.py:466
  125.6 4.5 %collective-permute-start.10 = (bf16[192,128]{1,0:T(8,128)(2,1)S(1)}, bf16[192,128]{1,0:T(8,128)(2,1)S(1)}, u32[]{:S(2)}, u32[]{:S(2)}) collective-permute-start(bf16[192,128]{1,0:T(8,128)(2,1)S(1)} %get-tuple-element.74), channel_id=1, source_target_pairs={{0,256},{4,260},{8,264},{12,268},{16,272},{20,276},{24,280},{28,28... | collective-permute-start | bytes 147464 | tf_op jit(solution)/shard_map/ppermute | solution.py:466
  130.8 2.1 %collective-permute-done.10.a1 = bf16[192,128]{1,0:T(8,128)(2,1)S(1)} collective-permute-done((bf16[192,128]{1,0:T(8,128)(2,1)S(1)}, bf16[192,128]{1,0:T(8,128)(2,1)S(1)}, u32[]{:S(2)}, u32[]{:S(2)}) %collective-permute-start.10) | collective-permute-done | bytes 49184 | tf_op jit(solution)/shard_map/ppermute | solution.py:466
  132.9 3.1 %all-to-all-done.1.arrived = bf16[64,16,128]{2,1,0:T(8,128)(2,1)S(1)} async-done(((bf16[64,16,128]{2,1,0:T(8,128)(2,1)}), bf16[64,16,128]{2,1,0:T(8,128)(2,1)S(1)}, u32[]{:S(2)}, u32[]{:S(2)}) %all-to-all-start.1) | async-done | bytes 262176 | tf_op jit(solution)/shard_map/all_to_all | solution.py:542
  136.8 8.9 %all-to-all-start.2 = ((bf16[64,16,128]{2,1,0:T(8,128)(2,1)}), bf16[64,16,128]{2,1,0:T(8,128)(2,1)S(1)}, u32[]{:S(2)}, u32[]{:S(2)}) async-start(bf16[64,16,128]{2,1,0:T(8,128)(2,1)} %shard_map.145), calls=%async_computation.2 | async-start | bytes 524288 | tf_op jit(solution)/shard_map/all_to_all | solution.py:564
  145.8 5.4 %collective-permute-start.11 = (bf16[192,128]{1,0:T(8,128)(2,1)S(1)}, bf16[192,128]{1,0:T(8,128)(2,1)S(1)}, u32[]{:S(2)}, u32[]{:S(2)}) collective-permute-start(bf16[192,128]{1,0:T(8,128)(2,1)S(1)} %get-tuple-element.81), channel_id=1, source_target_pairs={{0,264},{4,268},{8,272},{12,276},{16,280},{20,284},{24,288},{28,29... | collective-permute-start | bytes 147464 | tf_op jit(solution)/shard_map/ppermute | solution.py:466
  151.2 6.1 %collective-permute-start.12 = (bf16[96,128]{1,0:T(8,128)(2,1)S(1)}, bf16[96,128]{1,0:T(8,128)(2,1)S(1)}, u32[]{:S(2)}, u32[]{:S(2)}) collective-permute-start(bf16[96,128]{1,0:T(8,128)(2,1)S(1)} %get-tuple-element.82), channel_id=1, source_target_pairs={{0,244},{4,272},{8,252},{12,280},{16,260},{20,288},{24,268},{28,29... | collective-permute-start | bytes 73736 | tf_op jit(solution)/shard_map/ppermute | solution.py:466
  157.8 3.2 %collective-permute-done.12.far = bf16[96,128]{1,0:T(8,128)(2,1)S(1)} collective-permute-done((bf16[96,128]{1,0:T(8,128)(2,1)S(1)}, bf16[96,128]{1,0:T(8,128)(2,1)S(1)}, u32[]{:S(2)}, u32[]{:S(2)}) %collective-permute-start.12) | collective-permute-done | bytes 24608 | tf_op jit(solution)/shard_map/ppermute | solution.py:466
  161.1 3.9 %collective-permute-start.13 = (bf16[288,128]{1,0:T(8,128)(2,1)S(1)}, bf16[288,128]{1,0:T(8,128)(2,1)S(1)}, u32[]{:S(2)}, u32[]{:S(2)}) collective-permute-start(bf16[288,128]{1,0:T(8,128)(2,1)S(1)} %pad_maximum_fusion.2), channel_id=1, source_target_pairs={{0,4},{4,0},{8,12},{12,8},{16,20},{20,16},{24,28},{28,24},{32,36},... | collective-permute-start | bytes 221192 | tf_op jit(solution)/shard_map/ppermute | solution.py:466
  165.8 1.4 shard_map.146
  167.3 3.5 %collective-permute-start.14 = (bf16[64,16,128]{2,1,0:T(8,128)(2,1)S(1)}, bf16[64,16,128]{2,1,0:T(8,128)(2,1)S(1)}, u32[]{:S(2)}, u32[]{:S(2)}) collective-permute-start(bf16[64,16,128]{2,1,0:T(8,128)(2,1)S(1)} %all-to-all-done.2.held), channel_id=1, source_target_pairs={{0,4},{4,0},{8,12},{12,8},{16,20},{20,16},{24,28},{28,24},{32,36},... | collective-permute-start | bytes 786440 | tf_op jit(solution)/shard_map/ppermute | solution.py:466
  (58 shorter events, 13.3 us)
Async XLA Ops:
  0.6 0.8 copy-start.4
  1.5 0.7 copy-start.5
  2.2 21.8 %copy-start.7 = (s32[1,8]{1,0:T(1,128)S(1)}, s32[1,8]{1,0:T(1,128)}, u32[]{:S(2)}) copy-start(s32[1,8]{1,0:T(1,128)} %own_near.1) | copy-start | bytes 100
  2.2 21.8 %copy-start = (bf16[9,384,256]{2,1,0:T(8,128)(2,1)S(1)}, bf16[9,384,256]{2,1,0:T(8,128)(2,1)}, u32[]{:S(2)}) copy-start(bf16[9,384,256]{2,1,0:T(8,128)(2,1)} %weights_held.1) | copy-start | bytes 5308420
  2.8 27.6 %collective-permute-start = (bf16[192,128]{1,0:T(8,128)(2,1)S(1)}, bf16[192,128]{1,0:T(8,128)(2,1)S(1)}, u32[]{:S(2)}, u32[]{:S(2)}) collective-permute-start(bf16[192,128]{1,0:T(8,128)(2,1)S(1)} %get-tuple-element.46), channel_id=1, source_target_pairs={{0,248},{4,252},{8,256},{12,260},{16,264},{20,268},{24,272},{28,27... | collective-permute-start | bytes 147464 | tf_op jit(solution)/shard_map/ppermute | solution.py:466
  15.7 14.7 %collective-permute-start.1 = (bf16[192,128]{1,0:T(8,128)(2,1)S(1)}, bf16[192,128]{1,0:T(8,128)(2,1)S(1)}, u32[]{:S(2)}, u32[]{:S(2)}) collective-permute-start(bf16[192,128]{1,0:T(8,128)(2,1)S(1)} %get-tuple-element.47), channel_id=1, source_target_pairs={{0,256},{4,260},{8,264},{12,268},{16,272},{20,276},{24,280},{28,28... | collective-permute-start | bytes 147464 | tf_op jit(solution)/shard_map/ppermute | solution.py:466
  20.1 10.4 %collective-permute-start.2 = (bf16[192,128]{1,0:T(8,128)(2,1)S(1)}, bf16[192,128]{1,0:T(8,128)(2,1)S(1)}, u32[]{:S(2)}, u32[]{:S(2)}) collective-permute-start(bf16[192,128]{1,0:T(8,128)(2,1)S(1)} %get-tuple-element.48), channel_id=1, source_target_pairs={{0,264},{4,268},{8,272},{12,276},{16,280},{20,284},{24,288},{28,29... | collective-permute-start | bytes 147464 | tf_op jit(solution)/shard_map/ppermute | solution.py:466
  22.0 8.4 %collective-permute-start.3 = (bf16[96,128]{1,0:T(8,128)(2,1)S(1)}, bf16[96,128]{1,0:T(8,128)(2,1)S(1)}, u32[]{:S(2)}, u32[]{:S(2)}) collective-permute-start(bf16[96,128]{1,0:T(8,128)(2,1)S(1)} %get-tuple-element.49), channel_id=1, source_target_pairs={{0,244},{4,272},{8,252},{12,280},{16,260},{20,288},{24,268},{28,29... | collective-permute-start | bytes 73736 | tf_op jit(solution)/shard_map/ppermute | solution.py:466
  24.0 9.6 %copy-start.2 = (bf16[64,1024]{1,0:T(8,128)(2,1)S(1)}, bf16[64,1024]{1,0:T(8,128)(2,1)}, u32[]{:S(2)}) copy-start(bf16[64,1024]{1,0:T(8,128)(2,1)} %atm.4) | copy-start | bytes 393220
  24.0 9.6 %copy-start.3 = (bf16[64,1024]{1,0:T(8,128)(2,1)S(1)}, bf16[64,1024]{1,0:T(8,128)(2,1)}, u32[]{:S(2)}) copy-start(bf16[64,1024]{1,0:T(8,128)(2,1)} %grad_held.1) | copy-start | bytes 393220
  30.5 3.9 %copy-start.1 = (bf16[12,128,128]{2,1,0:T(8,128)(2,1)S(1)}, bf16[12,128,128]{2,1,0:T(8,128)(2,1)}, u32[]{:S(2)}) copy-start(bf16[12,128,128]{2,1,0:T(8,128)(2,1)} %regrid_held.1) | copy-start | bytes 1179652
  30.5 3.9 %copy-start.9 = (s32[1,4]{1,0:T(1,128)S(1)}, s32[1,4]{1,0:T(1,128)}, u32[]{:S(2)}) copy-start(s32[1,4]{1,0:T(1,128)} %sources.3) | copy-start | bytes 52
  30.5 3.9 %copy-start.10 = (s32[1,12]{1,0:T(1,128)S(1)}, s32[1,12]{1,0:T(1,128)}, u32[]{:S(2)}) copy-start(s32[1,12]{1,0:T(1,128)} %blocks.3) | copy-start | bytes 148
  30.6 3.9 %collective-permute-start.4 = (bf16[304,128]{1,0:T(8,128)(2,1)S(1)}, bf16[304,128]{1,0:T(8,128)(2,1)S(1)}, u32[]{:S(2)}, u32[]{:S(2)}) collective-permute-start(bf16[304,128]{1,0:T(8,128)(2,1)S(1)} %fusion.1), channel_id=1, source_target_pairs={{0,4},{4,0},{8,12},{12,8},{16,20},{20,16},{24,28},{28,24},{32,36},... | collective-permute-start | bytes 233480 | tf_op jit(solution)/shard_map/ppermute | solution.py:466
  36.8 3.1 %collective-permute-start.5 = (bf16[64,512]{1,0:T(8,128)(2,1)S(1)}, bf16[64,512]{1,0:T(8,128)(2,1)S(1)}, u32[]{:S(2)}, u32[]{:S(2)}) collective-permute-start(bf16[64,512]{1,0:T(8,128)(2,1)S(1)} %get-tuple-element.55), channel_id=1, source_target_pairs={{0,4},{4,0},{8,12},{12,8},{16,20},{20,16},{24,28},{28,24},{32,36},... | collective-permute-start | bytes 196616 | tf_op jit(solution)/shard_map/ppermute | solution.py:466
  40.0 12.8 %collective-permute-start.6 = (bf16[64,1024]{1,0:T(8,128)(2,1)S(1)}, bf16[64,1024]{1,0:T(8,128)(2,1)S(1)}, u32[]{:S(2)}, u32[]{:S(2)}) collective-permute-start(bf16[64,1024]{1,0:T(8,128)(2,1)S(1)} %pad_maximum_fusion.1), channel_id=1, source_target_pairs={{0,32},{8,40},{16,48},{24,56},{32,64},{36,4},{40,72},{44,12},{48,8... | collective-permute-start | bytes 393224 | tf_op jit(solution)/shard_map/ppermute | solution.py:513
  42.4 24.8 %copy-start.8 = (f32[64]{0:T(128)S(1)}, f32[64]{0:T(128)}, u32[]{:S(2)}) copy-start(f32[64]{0:T(128)} %param.13) | copy-start | bytes 772
  42.4 29.1 %all-to-all-start = ((bf16[4,160,1024]{2,1,0:T(8,128)(2,1)}), bf16[4,160,1024]{2,1,0:T(8,128)(2,1)}, u32[]{:S(2)}, u32[]{:S(2)}) async-start(bf16[4,160,1024]{2,1,0:T(8,128)(2,1)} %shard_map.141), calls=%async_computation | async-start | bytes 2621440 | tf_op jit(solution)/shard_map/all_to_all | solution.py:510
  68.2 3.3 %collective-permute-start.7 = (bf16[64,1152]{1,0:T(8,128)(2,1)S(1)}, bf16[64,1152]{1,0:T(8,128)(2,1)S(1)}, u32[]{:S(2)}, u32[]{:S(2)}) collective-permute-start(bf16[64,1152]{1,0:T(8,128)(2,1)S(1)} %get-tuple-element.59), channel_id=1, source_target_pairs={{0,4},{4,0},{8,12},{12,8},{16,20},{20,16},{24,28},{28,24},{32,36},... | collective-permute-start | bytes 442376 | tf_op jit(solution)/shard_map/ppermute | solution.py:466
  93.5 6.0 %collective-permute-start.8 = (bf16[64,16,128]{2,1,0:T(8,128)(2,1)}, bf16[64,16,128]{2,1,0:T(8,128)(2,1)S(1)}, u32[]{:S(2)}, u32[]{:S(2)}) collective-permute-start(bf16[64,16,128]{2,1,0:T(8,128)(2,1)} %get-tuple-element.68), channel_id=1, source_target_pairs={{0,4},{4,0},{8,12},{12,8},{16,20},{20,16},{24,28},{28,24},{32,36},... | collective-permute-start | bytes 786440 | tf_op jit(solution)/shard_map/ppermute | solution.py:466
  99.5 1.0 copy-start.11
  100.6 15.6 %copy-start.12 = (bf16[256,1408]{1,0:T(8,128)(2,1)S(1)}, bf16[256,1408]{1,0:T(8,128)(2,1)}, u32[]{:S(2)}) copy-start(bf16[256,1408]{1,0:T(8,128)(2,1)} %get-tuple-element.70.z_all) | copy-start | bytes 2162692
  101.3 34.7 %all-to-all-start.1 = ((bf16[64,16,128]{2,1,0:T(8,128)(2,1)}), bf16[64,16,128]{2,1,0:T(8,128)(2,1)S(1)}, u32[]{:S(2)}, u32[]{:S(2)}) async-start(bf16[64,16,128]{2,1,0:T(8,128)(2,1)} %shard_map.143), calls=%async_computation.1 | async-start | bytes 524288 | tf_op jit(solution)/shard_map/all_to_all | solution.py:542
  120.5 10.3 %collective-permute-start.9 = (bf16[192,128]{1,0:T(8,128)(2,1)S(1)}, bf16[192,128]{1,0:T(8,128)(2,1)S(1)}, u32[]{:S(2)}, u32[]{:S(2)}) collective-permute-start(bf16[192,128]{1,0:T(8,128)(2,1)S(1)} %get-tuple-element.73), channel_id=1, source_target_pairs={{0,248},{4,252},{8,256},{12,260},{16,264},{20,268},{24,272},{28,27... | collective-permute-start | bytes 147464 | tf_op jit(solution)/shard_map/ppermute | solution.py:466
  125.6 7.3 %collective-permute-start.10 = (bf16[192,128]{1,0:T(8,128)(2,1)S(1)}, bf16[192,128]{1,0:T(8,128)(2,1)S(1)}, u32[]{:S(2)}, u32[]{:S(2)}) collective-permute-start(bf16[192,128]{1,0:T(8,128)(2,1)S(1)} %get-tuple-element.74), channel_id=1, source_target_pairs={{0,256},{4,260},{8,264},{12,268},{16,272},{20,276},{24,280},{28,28... | collective-permute-start | bytes 147464 | tf_op jit(solution)/shard_map/ppermute | solution.py:466
  136.0 29.8 %copy-start.6 = (s32[1,128,3]{1,0,2:T(1,128)S(1)}, s32[1,128,3]{1,0,2:T(1,128)}, u32[]{:S(2)}) copy-start(s32[1,128,3]{1,0,2:T(1,128)} %param.19) | copy-start | bytes 4612
  136.8 30.5 %all-to-all-start.2 = ((bf16[64,16,128]{2,1,0:T(8,128)(2,1)}), bf16[64,16,128]{2,1,0:T(8,128)(2,1)S(1)}, u32[]{:S(2)}, u32[]{:S(2)}) async-start(bf16[64,16,128]{2,1,0:T(8,128)(2,1)} %shard_map.145), calls=%async_computation.2 | async-start | bytes 524288 | tf_op jit(solution)/shard_map/all_to_all | solution.py:564
  145.8 12.1 %collective-permute-start.11 = (bf16[192,128]{1,0:T(8,128)(2,1)S(1)}, bf16[192,128]{1,0:T(8,128)(2,1)S(1)}, u32[]{:S(2)}, u32[]{:S(2)}) collective-permute-start(bf16[192,128]{1,0:T(8,128)(2,1)S(1)} %get-tuple-element.81), channel_id=1, source_target_pairs={{0,264},{4,268},{8,272},{12,276},{16,280},{20,284},{24,288},{28,29... | collective-permute-start | bytes 147464 | tf_op jit(solution)/shard_map/ppermute | solution.py:466
  151.2 9.9 %collective-permute-start.12 = (bf16[96,128]{1,0:T(8,128)(2,1)S(1)}, bf16[96,128]{1,0:T(8,128)(2,1)S(1)}, u32[]{:S(2)}, u32[]{:S(2)}) collective-permute-start(bf16[96,128]{1,0:T(8,128)(2,1)S(1)} %get-tuple-element.82), channel_id=1, source_target_pairs={{0,244},{4,272},{8,252},{12,280},{16,260},{20,288},{24,268},{28,29... | collective-permute-start | bytes 73736 | tf_op jit(solution)/shard_map/ppermute | solution.py:466
  161.1 4.8 %collective-permute-start.13 = (bf16[288,128]{1,0:T(8,128)(2,1)S(1)}, bf16[288,128]{1,0:T(8,128)(2,1)S(1)}, u32[]{:S(2)}, u32[]{:S(2)}) collective-permute-start(bf16[288,128]{1,0:T(8,128)(2,1)S(1)} %pad_maximum_fusion.2), channel_id=1, source_target_pairs={{0,4},{4,0},{8,12},{12,8},{16,20},{20,16},{24,28},{28,24},{32,36},... | collective-permute-start | bytes 221192 | tf_op jit(solution)/shard_map/ppermute | solution.py:466
  167.3 4.7 %collective-permute-start.14 = (bf16[64,16,128]{2,1,0:T(8,128)(2,1)S(1)}, bf16[64,16,128]{2,1,0:T(8,128)(2,1)S(1)}, u32[]{:S(2)}, u32[]{:S(2)}) collective-permute-start(bf16[64,16,128]{2,1,0:T(8,128)(2,1)S(1)} %all-to-all-done.2.held), channel_id=1, source_target_pairs={{0,4},{4,0},{8,12},{12,8},{16,20},{20,16},{24,28},{28,24},{32,36},... | collective-permute-start | bytes 786440 | tf_op jit(solution)/shard_map/ppermute | solution.py:466

commit v6 on v5

--- a/solution.py
+++ b/solution.py
@@ -355,7 +355,7 @@
 
                     @pl.when(core == half)
                     def _():
-                        mine[at] = piece
+                        mine[at] = piece.astype(BF)
 
                     @pl.when(core != half)
                     def _():
@@ -441,7 +441,7 @@
 
 
 def add_kernel(mine, crossed, total):
-    total[...] = (mine[...] + crossed[...].astype(F32)).astype(BF)
+    total[...] = (mine[...].astype(F32) + crossed[...].astype(F32)).astype(BF)
 
 
 def sum_kernel(scale, arrived, out):
@@ -509,8 +509,7 @@
     (copies,) = call(copies_kernel, [((4, 160, 1024), BF)], [VMEM] * 3)(atm_now, grad_now, regridded)
     inner = lax.all_to_all(copies, "chan", 0, 0)
     pair = jnp.concatenate([keep, got], axis=1)
-    pairs = [(i, i + 8 - 16 * (i % 2)) for i in range(TILES)]
-    arrived = lax.ppermute(pair, "tile", [(i, j) for i, j in pairs if 0 <= j < TILES])
+    arrived = send(pair, lambda i: (i + 8 - 16 * (i % 2)) % TILES)
     strips = jnp.concatenate([arrived, sides], axis=1)
     strips = lax.all_gather(strips, "tile", axis_index_groups=ROW_CHIPS)
     own, mate = call(select_kernel, [((64, 1152), BF)] * 2, [SMEM] * 2 + [VMEM] * 2, cost=12)(
@@ -521,7 +520,7 @@
     outer = lax.all_gather(shard, "chan")
     atm_output, z_all, mine, theirs = call(
         forward_kernel,
-        [((64, 1024), BF), ((256, 1408), BF), ((64, 16, 128), F32), ((64, 16, 128), BF)],
+        [((64, 1024), BF), ((256, 1408), BF), ((64, 16, 128), BF), ((64, 16, 128), BF)],
         [HELD] * 3,
         [
             pltpu.VMEM((384, 128), BF),

time: 174 us -> 174 us (level)
  starting transfers between devices: 90.9 us -> 98.1 us
  waiting for transfers between devices: 25.6 us -> 19.6 us
    ppermute x14 -> x15, starting transfers between devices: 61.4 us -> 74 us  [send(): return lax.ppermute(array, 'tile', [(i, target(i)) for i in range(TILES)])]
    ppermute x1 -> x0, waiting for transfers between devices: 5.9 us -> none  [on_device(): lax.ppermute(pair, 'tile', [(i, j) for i, j in pairs if 0 <= j < TILES])]
    all_to_all x1, starting transfers between devices: 14.9 us -> 10.7 us  [on_device(): shares = lax.all_to_all(total, 'tile', 0, 0, axis_index_groups=SAME_CORE)]
    ppermute x14 -> x15, waiting for transfers between devices: 16.6 us -> 16.5 us  [send(): return lax.ppermute(array, 'tile', [(i, target(i)) for i in range(TILES)])]
  transfers between devices with their start and end apart: 18 -> 18, of which waited for: 13 -> 12; matrix products, arithmetic and copies ran while one was open for 2% -> 2% of each run, Pallas kernels for 5% -> 5%
where the time goes in v6:
time: 174 us; the launch traced here: 173 us
  starting transfers between devices  98.1 us (56%)
  blocking collectives  25.6 us (15%)
  Pallas kernels  23.3 us (13%)
  waiting for transfers between devices  19.6 us (11%)
  local copies, waits for them, and re-layouts  4.76 us (3%)
    ppermute x15, starting transfers between devices, send(): return lax.ppermute(array, 'tile', [(i, target(i)) for i in range(TILES)])  74 us
    ppermute x15, waiting for transfers between devices, send(): return lax.ppermute(array, 'tile', [(i, target(i)) for i in range(TILES)])  16.5 us
    all_gather x1, blocking collectives, on_device(): strips = lax.all_gather(strips, 'tile', axis_index_groups=ROW_CHIPS)  13.6 us
    all_gather x1, blocking collectives, on_device(): outer = lax.all_gather(shard, 'chan')  12 us
    all_to_all x1, starting transfers between devices, on_device(): shares = lax.all_to_all(total, 'tile', 0, 0, axis_index_groups=SAME_CORE)  10.7 us
    pallas_call x1, Pallas kernels, on_device(): call(forward_kernel, [((64, 1024), BF), ((256, 1408), BF), ((64, 16, 128)...  9.66 us
    all_to_all x1, starting transfers between devices, on_device(): held = lax.all_to_all(summed, 'tile', 0, 0, axis_index_groups=SAME_CORE)  8.94 us
    all_to_all x1, starting transfers between devices, on_device(): inner = lax.all_to_all(copies, 'chan', 0, 0)  4.43 us
  transfers between devices with their start and end apart: 18, of which 12 were waited for; matrix products, arithmetic and copies ran while one was open for 2% of the time, Pallas kernels for 5%

profile of v6, /device:TPU:1, one launch (start us, length us, event | category | flops | bytes accessed | tf_op | source)
XLA Modules:
  0.0 172.9 jit_solution(7799634595560266201)
XLA Ops:
  2.8 12.9 %collective-permute-start = (bf16[192,128]{1,0:T(8,128)(2,1)S(1)}, bf16[192,128]{1,0:T(8,128)(2,1)S(1)}, u32[]{:S(2)}, u32[]{:S(2)}) collective-permute-start(bf16[192,128]{1,0:T(8,128)(2,1)S(1)} %get-tuple-element.46), channel_id=1, source_target_pairs={{0,248},{4,252},{8,256},{12,260},{16,264},{20,268},{24,272},{28,27... | collective-permute-start | bytes 147464 | tf_op jit(solution)/shard_map/ppermute | solution.py:466
  15.7 4.4 %collective-permute-start.1 = (bf16[192,128]{1,0:T(8,128)(2,1)S(1)}, bf16[192,128]{1,0:T(8,128)(2,1)S(1)}, u32[]{:S(2)}, u32[]{:S(2)}) collective-permute-start(bf16[192,128]{1,0:T(8,128)(2,1)S(1)} %get-tuple-element.47), channel_id=1, source_target_pairs={{0,256},{4,260},{8,264},{12,268},{16,272},{20,276},{24,280},{28,28... | collective-permute-start | bytes 147464 | tf_op jit(solution)/shard_map/ppermute | solution.py:466
  20.1 1.9 %collective-permute-start.2 = (bf16[192,128]{1,0:T(8,128)(2,1)S(1)}, bf16[192,128]{1,0:T(8,128)(2,1)S(1)}, u32[]{:S(2)}, u32[]{:S(2)}) collective-permute-start(bf16[192,128]{1,0:T(8,128)(2,1)S(1)} %get-tuple-element.48), channel_id=1, source_target_pairs={{0,264},{4,268},{8,272},{12,276},{16,280},{20,284},{24,288},{28,29... | collective-permute-start | bytes 147464 | tf_op jit(solution)/shard_map/ppermute | solution.py:466
  22.0 1.9 %collective-permute-start.3 = (bf16[96,128]{1,0:T(8,128)(2,1)S(1)}, bf16[96,128]{1,0:T(8,128)(2,1)S(1)}, u32[]{:S(2)}, u32[]{:S(2)}) collective-permute-start(bf16[96,128]{1,0:T(8,128)(2,1)S(1)} %get-tuple-element.49), channel_id=1, source_target_pairs={{0,244},{4,272},{8,252},{12,280},{16,260},{20,288},{24,268},{28,29... | collective-permute-start | bytes 73736 | tf_op jit(solution)/shard_map/ppermute | solution.py:466
  24.0 2.2 %copy.15 = bf16[3,1152,256]{1,2,0:T(8,128)(2,1)} copy(bf16[3,1152,256]{2,1,0:T(8,128)(2,1)S(1)} %bitcast.10) | data formatting | bytes 3538944 | tf_op jit(solution)/shard_map/reshape | solution.py:496
  26.2 4.2 %collective-permute-done.3.far = bf16[96,128]{1,0:T(8,128)(2,1)S(1)} collective-permute-done((bf16[96,128]{1,0:T(8,128)(2,1)S(1)}, bf16[96,128]{1,0:T(8,128)(2,1)S(1)}, u32[]{:S(2)}, u32[]{:S(2)}) %collective-permute-start.3) | collective-permute-done | bytes 24608 | tf_op jit(solution)/shard_map/ppermute | solution.py:466
  30.6 3.0 %collective-permute-start.4 = (bf16[304,128]{1,0:T(8,128)(2,1)S(1)}, bf16[304,128]{1,0:T(8,128)(2,1)S(1)}, u32[]{:S(2)}, u32[]{:S(2)}) collective-permute-start(bf16[304,128]{1,0:T(8,128)(2,1)S(1)} %fusion.1), channel_id=1, source_target_pairs={{0,4},{4,0},{8,12},{12,8},{16,20},{20,16},{24,28},{28,24},{32,36},... | collective-permute-start | bytes 233480 | tf_op jit(solution)/shard_map/ppermute | solution.py:466
  34.4 2.3 %shard_map.139 = (bf16[32,1024]{1,0:T(8,128)(2,1)S(1)}, bf16[64,512]{1,0:T(8,128)(2,1)S(1)}, bf16[64,512]{1,0:T(8,128)(2,1)S(1)}, bf16[64,128]{1,0:T(8,128)(2,1)S(1)}) custom-call(s32[1,4]{1,0:T(1,128)S(1)} %copy-done.9, s32[1,12]{1,0:T(1,128)S(1)} %copy-done.10, bf16[192,128]{1,0:T(8,128)(2,1)S(1)} %collective-permute-done.a0, ...), custom_call_target="tpu_custom_call" | custom-call | flops 1000000000 | bytes 3000000 | tf_op jit(solution)/shard_map/pallas_call | solution.py:502
  36.8 1.9 %collective-permute-start.5 = (bf16[64,512]{1,0:T(8,128)(2,1)S(1)}, bf16[64,512]{1,0:T(8,128)(2,1)S(1)}, u32[]{:S(2)}, u32[]{:S(2)}) collective-permute-start(bf16[64,512]{1,0:T(8,128)(2,1)S(1)} %get-tuple-element.55), channel_id=1, source_target_pairs={{0,4},{4,0},{8,12},{12,8},{16,20},{20,16},{24,28},{28,24},{32,36},... | collective-permute-start | bytes 196616 | tf_op jit(solution)/shard_map/ppermute | solution.py:466
  38.7 1.2 collective-permute-done.5
  40.0 8.4 %collective-permute-start.6 = (bf16[64,1024]{1,0:T(8,128)(2,1)S(1)}, bf16[64,1024]{1,0:T(8,128)(2,1)S(1)}, u32[]{:S(2)}, u32[]{:S(2)}) collective-permute-start(bf16[64,1024]{1,0:T(8,128)(2,1)S(1)} %pad_maximum_fusion.1), channel_id=1, source_target_pairs={{0,32},{4,484},{8,40},{12,492},{16,48},{20,500},{24,56},{28,508},{... | collective-permute-start | bytes 393224 | tf_op jit(solution)/shard_map/ppermute | solution.py:466
  48.4 1.2 shard_map.141
  49.6 4.4 %all-to-all-start = ((bf16[4,160,1024]{2,1,0:T(8,128)(2,1)}), bf16[4,160,1024]{2,1,0:T(8,128)(2,1)}, u32[]{:S(2)}, u32[]{:S(2)}) async-start(bf16[4,160,1024]{2,1,0:T(8,128)(2,1)} %shard_map.141), calls=%async_computation | async-start | bytes 2621440 | tf_op jit(solution)/shard_map/all_to_all | solution.py:510
  54.1 13.6 %all-gather = bf16[256,1152]{1,0:T(8,128)(2,1)S(1)} all-gather(bf16[64,1152]{1,0:T(8,128)(2,1)S(1)} %pad_maximum_fusion), channel_id=2, replica_groups={{0,8,16,24},{4,12,20,28},{32,40,48,56},{36,44,52,60},{64,72,80,88},{68,..., dimensions={0}, use_global_device_ids=true | all-gather | bytes 737280 | tf_op jit(solution)/shard_map/all_gather | solution.py:514
  68.7 6.7 %collective-permute-start.7 = (bf16[64,1152]{1,0:T(8,128)(2,1)S(1)}, bf16[64,1152]{1,0:T(8,128)(2,1)S(1)}, u32[]{:S(2)}, u32[]{:S(2)}) collective-permute-start(bf16[64,1152]{1,0:T(8,128)(2,1)S(1)} %get-tuple-element.59), channel_id=1, source_target_pairs={{0,4},{4,0},{8,12},{12,8},{16,20},{20,16},{24,28},{28,24},{32,36},... | collective-permute-start | bytes 442376 | tf_op jit(solution)/shard_map/ppermute | solution.py:466
  76.4 12.0 %all-gather.1 = bf16[256,1152]{1,0:T(8,128)(2,1)} all-gather(bf16[64,1152]{1,0:T(8,128)(2,1)S(1)} %add.5), channel_id=3, replica_groups=mesh['tile'=128,'chan'=4] {'chan'}, dimensions={0}, use_global_device_ids=true | all-gather | bytes 737280 | tf_op jit(solution)/shard_map/all_gather | solution.py:520
  88.4 9.7 %shard_map.142 = (bf16[64,1024]{1,0:T(8,128)(2,1)}, bf16[256,1408]{1,0:T(8,128)(2,1)}, bf16[64,16,128]{2,1,0:T(8,128)(2,1)}, bf16[64,16,128]{2,1,0:T(8,128)(2,1)}) custom-call(bf16[4,160,1024]{2,1,0:T(8,128)(2,1)} %all-to-all-done.inner, bf16[4,64,1152]{2,1,0:T(8,128)(2,1)} %bitcast.16, bf16[3,256,1152]{2,1,0:T(8,128)(2,1)} %bitcast.15), custom_call_target="tpu_custom_call" | custom-call | flops 10000000000 | bytes 30000000 | tf_op jit(solution)/shard_map/pallas_call | solution.py:521
  98.1 4.3 %collective-permute-start.8 = (bf16[64,16,128]{2,1,0:T(8,128)(2,1)}, bf16[64,16,128]{2,1,0:T(8,128)(2,1)S(1)}, u32[]{:S(2)}, u32[]{:S(2)}) collective-permute-start(bf16[64,16,128]{2,1,0:T(8,128)(2,1)} %get-tuple-element.68), channel_id=1, source_target_pairs={{0,4},{4,0},{8,12},{12,8},{16,20},{20,16},{24,28},{28,24},{32,36},... | collective-permute-start | bytes 786440 | tf_op jit(solution)/shard_map/ppermute | solution.py:466
  102.4 1.4 collective-permute-done.8.crossed
  105.5 10.7 %all-to-all-start.1 = ((bf16[64,16,128]{2,1,0:T(8,128)(2,1)}), bf16[64,16,128]{2,1,0:T(8,128)(2,1)S(1)}, u32[]{:S(2)}, u32[]{:S(2)}) async-start(bf16[64,16,128]{2,1,0:T(8,128)(2,1)} %shard_map.143), calls=%async_computation.1 | async-start | bytes 524288 | tf_op jit(solution)/shard_map/all_to_all | solution.py:541
  116.2 4.2 %shard_map.144 = (bf16[64,1024]{1,0:T(8,128)(2,1)}, bf16[192,128]{1,0:T(8,128)(2,1)S(1)}, bf16[192,128]{1,0:T(8,128)(2,1)S(1)}, bf16[192,128]{1,0:T(8,128)(2,1)S(1)}, bf16[96,128]{1,0:T(8,128)(2,1)S(1)}) custom-call(s32[1,4]{1,0:T(1,128)S(1)} %copy-done.9, s32[1,12]{1,0:T(1,128)S(1)} %copy-done.10, bf16[256,1408]{1,0:T(8,128)(2,1)S(1)} %copy-done.12, ...), custom_call_target="tpu_custom_call" | custom-call | flops 4000000000 | bytes 12000000 | tf_op jit(solution)/shard_map/pallas_call | solution.py:542
  120.4 5.1 %collective-permute-start.9 = (bf16[192,128]{1,0:T(8,128)(2,1)S(1)}, bf16[192,128]{1,0:T(8,128)(2,1)S(1)}, u32[]{:S(2)}, u32[]{:S(2)}) collective-permute-start(bf16[192,128]{1,0:T(8,128)(2,1)S(1)} %get-tuple-element.73), channel_id=1, source_target_pairs={{0,248},{4,252},{8,256},{12,260},{16,264},{20,268},{24,272},{28,27... | collective-permute-start | bytes 147464 | tf_op jit(solution)/shard_map/ppermute | solution.py:466
  125.6 4.5 %collective-permute-start.10 = (bf16[192,128]{1,0:T(8,128)(2,1)S(1)}, bf16[192,128]{1,0:T(8,128)(2,1)S(1)}, u32[]{:S(2)}, u32[]{:S(2)}) collective-permute-start(bf16[192,128]{1,0:T(8,128)(2,1)S(1)} %get-tuple-element.74), channel_id=1, source_target_pairs={{0,256},{4,260},{8,264},{12,268},{16,272},{20,276},{24,280},{28,28... | collective-permute-start | bytes 147464 | tf_op jit(solution)/shard_map/ppermute | solution.py:466
  130.8 2.1 %collective-permute-done.10.a1 = bf16[192,128]{1,0:T(8,128)(2,1)S(1)} collective-permute-done((bf16[192,128]{1,0:T(8,128)(2,1)S(1)}, bf16[192,128]{1,0:T(8,128)(2,1)S(1)}, u32[]{:S(2)}, u32[]{:S(2)}) %collective-permute-start.10) | collective-permute-done | bytes 49184 | tf_op jit(solution)/shard_map/ppermute | solution.py:466
  132.9 3.1 %all-to-all-done.1.arrived = bf16[64,16,128]{2,1,0:T(8,128)(2,1)S(1)} async-done(((bf16[64,16,128]{2,1,0:T(8,128)(2,1)}), bf16[64,16,128]{2,1,0:T(8,128)(2,1)S(1)}, u32[]{:S(2)}, u32[]{:S(2)}) %all-to-all-start.1) | async-done | bytes 262176 | tf_op jit(solution)/shard_map/all_to_all | solution.py:541
  136.8 8.9 %all-to-all-start.2 = ((bf16[64,16,128]{2,1,0:T(8,128)(2,1)}), bf16[64,16,128]{2,1,0:T(8,128)(2,1)S(1)}, u32[]{:S(2)}, u32[]{:S(2)}) async-start(bf16[64,16,128]{2,1,0:T(8,128)(2,1)} %shard_map.145), calls=%async_computation.2 | async-start | bytes 524288 | tf_op jit(solution)/shard_map/all_to_all | solution.py:563
  145.7 5.4 %collective-permute-start.11 = (bf16[192,128]{1,0:T(8,128)(2,1)S(1)}, bf16[192,128]{1,0:T(8,128)(2,1)S(1)}, u32[]{:S(2)}, u32[]{:S(2)}) collective-permute-start(bf16[192,128]{1,0:T(8,128)(2,1)S(1)} %get-tuple-element.81), channel_id=1, source_target_pairs={{0,264},{4,268},{8,272},{12,276},{16,280},{20,284},{24,288},{28,29... | collective-permute-start | bytes 147464 | tf_op jit(solution)/shard_map/ppermute | solution.py:466
  151.1 6.1 %collective-permute-start.12 = (bf16[96,128]{1,0:T(8,128)(2,1)S(1)}, bf16[96,128]{1,0:T(8,128)(2,1)S(1)}, u32[]{:S(2)}, u32[]{:S(2)}) collective-permute-start(bf16[96,128]{1,0:T(8,128)(2,1)S(1)} %get-tuple-element.82), channel_id=1, source_target_pairs={{0,244},{4,272},{8,252},{12,280},{16,260},{20,288},{24,268},{28,29... | collective-permute-start | bytes 73736 | tf_op jit(solution)/shard_map/ppermute | solution.py:466
  157.8 3.2 %collective-permute-done.12.far = bf16[96,128]{1,0:T(8,128)(2,1)S(1)} collective-permute-done((bf16[96,128]{1,0:T(8,128)(2,1)S(1)}, bf16[96,128]{1,0:T(8,128)(2,1)S(1)}, u32[]{:S(2)}, u32[]{:S(2)}) %collective-permute-start.12) | collective-permute-done | bytes 24608 | tf_op jit(solution)/shard_map/ppermute | solution.py:466
  161.0 3.9 %collective-permute-start.13 = (bf16[288,128]{1,0:T(8,128)(2,1)S(1)}, bf16[288,128]{1,0:T(8,128)(2,1)S(1)}, u32[]{:S(2)}, u32[]{:S(2)}) collective-permute-start(bf16[288,128]{1,0:T(8,128)(2,1)S(1)} %pad_maximum_fusion.2), channel_id=1, source_target_pairs={{0,4},{4,0},{8,12},{12,8},{16,20},{20,16},{24,28},{28,24},{32,36},... | collective-permute-start | bytes 221192 | tf_op jit(solution)/shard_map/ppermute | solution.py:466
  165.8 1.4 shard_map.146
  167.2 3.5 %collective-permute-start.14 = (bf16[64,16,128]{2,1,0:T(8,128)(2,1)S(1)}, bf16[64,16,128]{2,1,0:T(8,128)(2,1)S(1)}, u32[]{:S(2)}, u32[]{:S(2)}) collective-permute-start(bf16[64,16,128]{2,1,0:T(8,128)(2,1)S(1)} %all-to-all-done.2.held), channel_id=1, source_target_pairs={{0,4},{4,0},{8,12},{12,8},{16,20},{20,16},{24,28},{28,24},{32,36},... | collective-permute-start | bytes 786440 | tf_op jit(solution)/shard_map/ppermute | solution.py:466
  (58 shorter events, 11.9 us)
Async XLA Ops:
  0.6 0.8 copy-start.4
  1.5 0.7 copy-start.5
  2.2 21.8 %copy-start.7 = (s32[1,8]{1,0:T(1,128)S(1)}, s32[1,8]{1,0:T(1,128)}, u32[]{:S(2)}) copy-start(s32[1,8]{1,0:T(1,128)} %own_near.1) | copy-start | bytes 100
  2.2 21.8 %copy-start = (bf16[9,384,256]{2,1,0:T(8,128)(2,1)S(1)}, bf16[9,384,256]{2,1,0:T(8,128)(2,1)}, u32[]{:S(2)}) copy-start(bf16[9,384,256]{2,1,0:T(8,128)(2,1)} %weights_held.1) | copy-start | bytes 5308420
  2.8 27.6 %collective-permute-start = (bf16[192,128]{1,0:T(8,128)(2,1)S(1)}, bf16[192,128]{1,0:T(8,128)(2,1)S(1)}, u32[]{:S(2)}, u32[]{:S(2)}) collective-permute-start(bf16[192,128]{1,0:T(8,128)(2,1)S(1)} %get-tuple-element.46), channel_id=1, source_target_pairs={{0,248},{4,252},{8,256},{12,260},{16,264},{20,268},{24,272},{28,27... | collective-permute-start | bytes 147464 | tf_op jit(solution)/shard_map/ppermute | solution.py:466
  15.7 14.7 %collective-permute-start.1 = (bf16[192,128]{1,0:T(8,128)(2,1)S(1)}, bf16[192,128]{1,0:T(8,128)(2,1)S(1)}, u32[]{:S(2)}, u32[]{:S(2)}) collective-permute-start(bf16[192,128]{1,0:T(8,128)(2,1)S(1)} %get-tuple-element.47), channel_id=1, source_target_pairs={{0,256},{4,260},{8,264},{12,268},{16,272},{20,276},{24,280},{28,28... | collective-permute-start | bytes 147464 | tf_op jit(solution)/shard_map/ppermute | solution.py:466
  20.1 10.4 %collective-permute-start.2 = (bf16[192,128]{1,0:T(8,128)(2,1)S(1)}, bf16[192,128]{1,0:T(8,128)(2,1)S(1)}, u32[]{:S(2)}, u32[]{:S(2)}) collective-permute-start(bf16[192,128]{1,0:T(8,128)(2,1)S(1)} %get-tuple-element.48), channel_id=1, source_target_pairs={{0,264},{4,268},{8,272},{12,276},{16,280},{20,284},{24,288},{28,29... | collective-permute-start | bytes 147464 | tf_op jit(solution)/shard_map/ppermute | solution.py:466
  22.0 8.4 %collective-permute-start.3 = (bf16[96,128]{1,0:T(8,128)(2,1)S(1)}, bf16[96,128]{1,0:T(8,128)(2,1)S(1)}, u32[]{:S(2)}, u32[]{:S(2)}) collective-permute-start(bf16[96,128]{1,0:T(8,128)(2,1)S(1)} %get-tuple-element.49), channel_id=1, source_target_pairs={{0,244},{4,272},{8,252},{12,280},{16,260},{20,288},{24,268},{28,29... | collective-permute-start | bytes 73736 | tf_op jit(solution)/shard_map/ppermute | solution.py:466
  24.0 9.6 %copy-start.2 = (bf16[64,1024]{1,0:T(8,128)(2,1)S(1)}, bf16[64,1024]{1,0:T(8,128)(2,1)}, u32[]{:S(2)}) copy-start(bf16[64,1024]{1,0:T(8,128)(2,1)} %atm.4) | copy-start | bytes 393220
  24.0 9.6 %copy-start.3 = (bf16[64,1024]{1,0:T(8,128)(2,1)S(1)}, bf16[64,1024]{1,0:T(8,128)(2,1)}, u32[]{:S(2)}) copy-start(bf16[64,1024]{1,0:T(8,128)(2,1)} %grad_held.1) | copy-start | bytes 393220
  30.5 3.9 %copy-start.1 = (bf16[12,128,128]{2,1,0:T(8,128)(2,1)S(1)}, bf16[12,128,128]{2,1,0:T(8,128)(2,1)}, u32[]{:S(2)}) copy-start(bf16[12,128,128]{2,1,0:T(8,128)(2,1)} %regrid_held.1) | copy-start | bytes 1179652
  30.5 3.9 %copy-start.9 = (s32[1,4]{1,0:T(1,128)S(1)}, s32[1,4]{1,0:T(1,128)}, u32[]{:S(2)}) copy-start(s32[1,4]{1,0:T(1,128)} %sources.3) | copy-start | bytes 52
  30.5 3.9 %copy-start.10 = (s32[1,12]{1,0:T(1,128)S(1)}, s32[1,12]{1,0:T(1,128)}, u32[]{:S(2)}) copy-start(s32[1,12]{1,0:T(1,128)} %blocks.3) | copy-start | bytes 148
  30.6 3.9 %collective-permute-start.4 = (bf16[304,128]{1,0:T(8,128)(2,1)S(1)}, bf16[304,128]{1,0:T(8,128)(2,1)S(1)}, u32[]{:S(2)}, u32[]{:S(2)}) collective-permute-start(bf16[304,128]{1,0:T(8,128)(2,1)S(1)} %fusion.1), channel_id=1, source_target_pairs={{0,4},{4,0},{8,12},{12,8},{16,20},{20,16},{24,28},{28,24},{32,36},... | collective-permute-start | bytes 233480 | tf_op jit(solution)/shard_map/ppermute | solution.py:466
  36.8 3.1 %collective-permute-start.5 = (bf16[64,512]{1,0:T(8,128)(2,1)S(1)}, bf16[64,512]{1,0:T(8,128)(2,1)S(1)}, u32[]{:S(2)}, u32[]{:S(2)}) collective-permute-start(bf16[64,512]{1,0:T(8,128)(2,1)S(1)} %get-tuple-element.55), channel_id=1, source_target_pairs={{0,4},{4,0},{8,12},{12,8},{16,20},{20,16},{24,28},{28,24},{32,36},... | collective-permute-start | bytes 196616 | tf_op jit(solution)/shard_map/ppermute | solution.py:466
  40.0 14.1 %collective-permute-start.6 = (bf16[64,1024]{1,0:T(8,128)(2,1)S(1)}, bf16[64,1024]{1,0:T(8,128)(2,1)S(1)}, u32[]{:S(2)}, u32[]{:S(2)}) collective-permute-start(bf16[64,1024]{1,0:T(8,128)(2,1)S(1)} %pad_maximum_fusion.1), channel_id=1, source_target_pairs={{0,32},{4,484},{8,40},{12,492},{16,48},{20,500},{24,56},{28,508},{... | collective-permute-start | bytes 393224 | tf_op jit(solution)/shard_map/ppermute | solution.py:466
  49.6 18.1 %copy-start.8 = (f32[64]{0:T(128)S(1)}, f32[64]{0:T(128)}, u32[]{:S(2)}) copy-start(f32[64]{0:T(128)} %param.13) | copy-start | bytes 772
  49.6 26.8 %all-to-all-start = ((bf16[4,160,1024]{2,1,0:T(8,128)(2,1)}), bf16[4,160,1024]{2,1,0:T(8,128)(2,1)}, u32[]{:S(2)}, u32[]{:S(2)}) async-start(bf16[4,160,1024]{2,1,0:T(8,128)(2,1)} %shard_map.141), calls=%async_computation | async-start | bytes 2621440 | tf_op jit(solution)/shard_map/all_to_all | solution.py:510
  68.7 7.7 %collective-permute-start.7 = (bf16[64,1152]{1,0:T(8,128)(2,1)S(1)}, bf16[64,1152]{1,0:T(8,128)(2,1)S(1)}, u32[]{:S(2)}, u32[]{:S(2)}) collective-permute-start(bf16[64,1152]{1,0:T(8,128)(2,1)S(1)} %get-tuple-element.59), channel_id=1, source_target_pairs={{0,4},{4,0},{8,12},{12,8},{16,20},{20,16},{24,28},{28,24},{32,36},... | collective-permute-start | bytes 442376 | tf_op jit(solution)/shard_map/ppermute | solution.py:466
  98.1 5.7 %collective-permute-start.8 = (bf16[64,16,128]{2,1,0:T(8,128)(2,1)}, bf16[64,16,128]{2,1,0:T(8,128)(2,1)S(1)}, u32[]{:S(2)}, u32[]{:S(2)}) collective-permute-start(bf16[64,16,128]{2,1,0:T(8,128)(2,1)} %get-tuple-element.68), channel_id=1, source_target_pairs={{0,4},{4,0},{8,12},{12,8},{16,20},{20,16},{24,28},{28,24},{32,36},... | collective-permute-start | bytes 786440 | tf_op jit(solution)/shard_map/ppermute | solution.py:466
  103.8 0.9 copy-start.11
  104.7 11.5 %copy-start.12 = (bf16[256,1408]{1,0:T(8,128)(2,1)S(1)}, bf16[256,1408]{1,0:T(8,128)(2,1)}, u32[]{:S(2)}) copy-start(bf16[256,1408]{1,0:T(8,128)(2,1)} %get-tuple-element.70.z_all) | copy-start | bytes 2162692
  105.5 30.5 %all-to-all-start.1 = ((bf16[64,16,128]{2,1,0:T(8,128)(2,1)}), bf16[64,16,128]{2,1,0:T(8,128)(2,1)S(1)}, u32[]{:S(2)}, u32[]{:S(2)}) async-start(bf16[64,16,128]{2,1,0:T(8,128)(2,1)} %shard_map.143), calls=%async_computation.1 | async-start | bytes 524288 | tf_op jit(solution)/shard_map/all_to_all | solution.py:541
  120.4 10.3 %collective-permute-start.9 = (bf16[192,128]{1,0:T(8,128)(2,1)S(1)}, bf16[192,128]{1,0:T(8,128)(2,1)S(1)}, u32[]{:S(2)}, u32[]{:S(2)}) collective-permute-start(bf16[192,128]{1,0:T(8,128)(2,1)S(1)} %get-tuple-element.73), channel_id=1, source_target_pairs={{0,248},{4,252},{8,256},{12,260},{16,264},{20,268},{24,272},{28,27... | collective-permute-start | bytes 147464 | tf_op jit(solution)/shard_map/ppermute | solution.py:466
  125.6 7.3 %collective-permute-start.10 = (bf16[192,128]{1,0:T(8,128)(2,1)S(1)}, bf16[192,128]{1,0:T(8,128)(2,1)S(1)}, u32[]{:S(2)}, u32[]{:S(2)}) collective-permute-start(bf16[192,128]{1,0:T(8,128)(2,1)S(1)} %get-tuple-element.74), channel_id=1, source_target_pairs={{0,256},{4,260},{8,264},{12,268},{16,272},{20,276},{24,280},{28,28... | collective-permute-start | bytes 147464 | tf_op jit(solution)/shard_map/ppermute | solution.py:466
  136.0 29.8 %copy-start.6 = (s32[1,128,3]{1,0,2:T(1,128)S(1)}, s32[1,128,3]{1,0,2:T(1,128)}, u32[]{:S(2)}) copy-start(s32[1,128,3]{1,0,2:T(1,128)} %param.19) | copy-start | bytes 4612
  136.8 30.5 %all-to-all-start.2 = ((bf16[64,16,128]{2,1,0:T(8,128)(2,1)}), bf16[64,16,128]{2,1,0:T(8,128)(2,1)S(1)}, u32[]{:S(2)}, u32[]{:S(2)}) async-start(bf16[64,16,128]{2,1,0:T(8,128)(2,1)} %shard_map.145), calls=%async_computation.2 | async-start | bytes 524288 | tf_op jit(solution)/shard_map/all_to_all | solution.py:563
  145.7 12.1 %collective-permute-start.11 = (bf16[192,128]{1,0:T(8,128)(2,1)S(1)}, bf16[192,128]{1,0:T(8,128)(2,1)S(1)}, u32[]{:S(2)}, u32[]{:S(2)}) collective-permute-start(bf16[192,128]{1,0:T(8,128)(2,1)S(1)} %get-tuple-element.81), channel_id=1, source_target_pairs={{0,264},{4,268},{8,272},{12,276},{16,280},{20,284},{24,288},{28,29... | collective-permute-start | bytes 147464 | tf_op jit(solution)/shard_map/ppermute | solution.py:466
  151.1 9.9 %collective-permute-start.12 = (bf16[96,128]{1,0:T(8,128)(2,1)S(1)}, bf16[96,128]{1,0:T(8,128)(2,1)S(1)}, u32[]{:S(2)}, u32[]{:S(2)}) collective-permute-start(bf16[96,128]{1,0:T(8,128)(2,1)S(1)} %get-tuple-element.82), channel_id=1, source_target_pairs={{0,244},{4,272},{8,252},{12,280},{16,260},{20,288},{24,268},{28,29... | collective-permute-start | bytes 73736 | tf_op jit(solution)/shard_map/ppermute | solution.py:466
  161.0 4.8 %collective-permute-start.13 = (bf16[288,128]{1,0:T(8,128)(2,1)S(1)}, bf16[288,128]{1,0:T(8,128)(2,1)S(1)}, u32[]{:S(2)}, u32[]{:S(2)}) collective-permute-start(bf16[288,128]{1,0:T(8,128)(2,1)S(1)} %pad_maximum_fusion.2), channel_id=1, source_target_pairs={{0,4},{4,0},{8,12},{12,8},{16,20},{20,16},{24,28},{28,24},{32,36},... | collective-permute-start | bytes 221192 | tf_op jit(solution)/shard_map/ppermute | solution.py:466
  167.2 4.7 %collective-permute-start.14 = (bf16[64,16,128]{2,1,0:T(8,128)(2,1)S(1)}, bf16[64,16,128]{2,1,0:T(8,128)(2,1)S(1)}, u32[]{:S(2)}, u32[]{:S(2)}) collective-permute-start(bf16[64,16,128]{2,1,0:T(8,128)(2,1)S(1)} %all-to-all-done.2.held), channel_id=1, source_target_pairs={{0,4},{4,0},{8,12},{12,8},{16,20},{20,16},{24,28},{28,24},{32,36},... | collective-permute-start | bytes 786440 | tf_op jit(solution)/shard_map/ppermute | solution.py:466
